TPU v7x, 32 devices: a whole 2x2x4 slice. The times are simulated.
32 devices in a mesh: grp: 2 (over y), probe: 4 (over z), prof: 2 (over x), sub: 2 (over core).
Axes of the slice: x: 2, y: 2, z: 4, core: 2. Of those that a mesh axis runs over, the one named last changes fastest.
Arguments:
- signal: float32 [8192, 4096], P(('grp', 'probe', 'sub'), 'prof'), parts along dimension 0, may hold values from -32 to 32, as said below
- jump_sizes: float32 [8192, 4096], P(('grp', 'probe', 'sub'), 'prof'), parts along dimension 0, may hold values from -95 to 95
- thresholds: float32 [8192], P(('grp', 'probe', 'sub')), parts along dimension 0, may hold values from 2 to 40
Outputs:
- new_jumps: float32 [8192, 4096], P(('grp', 'probe', 'sub'), 'prof'), parts along dimension 0
There are 2 independent parts, one for each index of `grp`. A program takes and returns all parts, laid end to end along the dimension named above; each array names one. Nothing has to cross between parts.
Inputs may be any that keep to these rules, and one draw needn't show every extreme that they name: `signal`: measurements of one profile share a scale.
All inputs are finite; a program needn't handle non-finite values.
Results may differ from a plain program's by a relative error of at most 0.0001.
Values sent between devices are 32-bit elements; how exact they have to be, the bound alone decides.
No kernel may reach another device: no remote copies, remote signals or barrier semaphores. Data moves between devices by JAX's collectives and lax.ppermute only.
A program may use at most 64 MiB of HBM per device.

v0:
```python
import functools

import jax
import jax.numpy as jnp
from jax import lax
from jax.experimental import pallas as pl
from jax.experimental.pallas import tpu as pltpu
from jax.sharding import PartitionSpec as P

ITERS = 8
STEP_LENGTH = 2.0
LANES = 128
SUBLANES = 8
VMEM_LIMIT = 16 * 1024 * 1024


def tiles(cols):
    return [slice(j * LANES, (j + 1) * LANES) for j in range(cols // LANES)]


def row_weights():
    return (SUBLANES - 1 - lax.broadcasted_iota(jnp.int32, (SUBLANES, LANES), 0)).astype(jnp.float32)


def finish_sums(depth, total, weighted, totals_ref, weighted_ref, message_ref, cols):
    weights = row_weights() * float(depth)
    for j, c in enumerate(tiles(cols)):
        totals_ref[:, c] = total[j]
        weighted_ref[:, c] = weighted[j]
        message_ref[0:1, c] = jnp.sum(total[j], axis=0, keepdims=True)
        message_ref[1:2, c] = jnp.sum(weights * total[j] + weighted[j], axis=0, keepdims=True)


def begin_kernel(beta, count, signal_hbm, jumps_hbm, state_ref, const_ref, minus_ref, totals_ref, weighted_ref,
                 message_ref, sems):
    depth, _, cols = state_ref.shape
    cs = tiles(cols)
    parts = depth // SUBLANES

    def copies(part):
        for a, (src, dst) in enumerate(((signal_hbm, const_ref), (jumps_hbm, state_ref))):
            for s in range(SUBLANES):
                yield pltpu.make_async_copy(
                    src.at[pl.ds(s * depth + part * SUBLANES, SUBLANES), :],
                    dst.at[pl.ds(part * SUBLANES, SUBLANES), s, :],
                    sems.at[a, part, s],
                )

    for part in reversed(range(parts)):
        for copy in copies(part):
            copy.start()
    zero = jnp.zeros((SUBLANES, LANES), jnp.float32)
    carry = ([zero] * len(cs), [zero] * len(cs), [zero] * len(cs))
    for part in reversed(range(parts)):
        for copy in copies(part):
            copy.wait()

        def step(i, carry, part=part):
            suffix, total, weighted = (list(x) for x in carry)
            k = part * SUBLANES + SUBLANES - 1 - i
            weight = (depth - k).astype(jnp.float32)
            for j, c in enumerate(cs):
                suffix[j] = suffix[j] + const_ref[k, :, c]
                const_ref[k, :, c] = suffix[j] * beta
                jump = state_ref[k, :, c]
                total[j] = total[j] + jump
                weighted[j] = weighted[j] + jump * weight
            return suffix, total, weighted

        carry = lax.fori_loop(0, SUBLANES, step, carry)
    suffix, total, weighted = carry
    for j, c in enumerate(cs):
        minus = suffix[j] * -count
        minus_ref[:, c] = minus
        weighted[j] = weighted[j] + minus
    finish_sums(depth, total, weighted, totals_ref, weighted_ref, message_ref, cols)


def shrink(own_ref, other_ref, limits_ref, factor_ref):
    squares = own_ref[...] + other_ref[...]
    factor = jnp.maximum(0.0, 1.0 - limits_ref[...] / jnp.sqrt(squares + 1e-06))
    rows = factor.shape[1]
    spread = jnp.broadcast_to(factor, (LANES, rows)).T
    factor_ref[...] = spread.reshape(factor_ref.shape)


def sums_kernel(own_ref, other_ref, limits_ref, state_ref, minus_ref, factor_ref, totals_ref, weighted_ref, message_ref):
    depth, _, cols = state_ref.shape
    cs = tiles(cols)
    shrink(own_ref, other_ref, limits_ref, factor_ref)

    def step(k, carry):
        total, weighted = (list(x) for x in carry)
        factor = factor_ref[k]
        for j, c in enumerate(cs):
            total[j] = total[j] + state_ref[k, :, c] * factor
            weighted[j] = weighted[j] + total[j]
        return total, weighted

    zero = jnp.zeros((SUBLANES, LANES), jnp.float32)
    total, weighted = lax.fori_loop(0, depth, step, ([zero] * len(cs), [minus_ref[:, c] for c in cs]), unroll=2)
    finish_sums(depth, total, weighted, totals_ref, weighted_ref, message_ref, cols)


def prefix_rows(x, sublane):
    for shift in (1, 2, 4):
        x = x + jnp.where(sublane >= shift, pltpu.roll(x, shift, 0), 0.0)
    return x


def suffix_rows(x, sublane):
    for shift in (1, 2, 4):
        x = x + jnp.where(sublane < SUBLANES - shift, pltpu.roll(x, SUBLANES - shift, 0), 0.0)
    return x


def inner_kernel(alpha, chips, scaled, state_ref, const_ref, factor_ref, totals_ref, weighted_ref, message_ref,
                 sibling_ref, inner_ref, slope_ref, base_ref):
    depth, _, cols = state_ref.shape
    rows = float(depth * SUBLANES)
    cs = tiles(cols)
    chip, core = lax.axis_index("probe"), lax.axis_index("sub")
    first = (core == 0).astype(jnp.float32)
    later = (chips - 1 - chip).astype(jnp.float32) * (2.0 * rows)
    sublane = lax.broadcasted_iota(jnp.int32, (SUBLANES, LANES), 0)
    weights = row_weights() * float(depth)

    def step(i, carry):
        running, double = (list(x) for x in carry)
        k = depth - 1 - i
        if scaled:
            factor = factor_ref[k]
        for j, c in enumerate(cs):
            jump = state_ref[k, :, c]
            if scaled:
                jump = jump * factor
            double[j] = double[j] + running[j]
            inner_ref[k, :, c] = jump + const_ref[k, :, c] - double[j]
            running[j] = running[j] - jump * alpha
        return running, double

    zero = jnp.zeros((SUBLANES, LANES), jnp.float32)
    lax.fori_loop(0, depth, step, ([totals_ref[:, c] * alpha for c in cs], [zero] * len(cs)), unroll=2)

    for c in cs:
        total = totals_ref[:, c]
        before = jnp.where(sublane >= 1, pltpu.roll(prefix_rows(total, sublane), 1, 0), 0.0)
        chunk = before * float(depth) + weighted_ref[:, c]
        after = jnp.where(
            sublane < SUBLANES - 1, pltpu.roll(suffix_rows(chunk, sublane), SUBLANES - 1, 0), 0.0
        )
        own, sibling = message_ref[0:1, c], sibling_ref[0:1, c]
        lower = first * own + (1.0 - first) * sibling
        shift = (1.0 - first) * lower
        base = later * (own + sibling) + first * (rows * lower + sibling_ref[1:2, c])
        slope_ref[:, c] = alpha * (before + shift)
        base_ref[:, c] = alpha * (after + base + weights * shift)


def outer_kernel(alpha, chips, offsets, inner_ref, slope_ref, base_ref, *refs):
    received, (state_ref, squares_ref, wide_ref) = refs[: len(offsets)], refs[len(offsets) :]
    depth, _, cols = inner_ref.shape
    rows = float(depth * SUBLANES)
    cs = tiles(cols)
    chip, core = lax.axis_index("probe"), lax.axis_index("sub")
    later = (chips - 1 - chip).astype(jnp.float32) * (2.0 * rows) + (core == 0).astype(jnp.float32) * rows
    weights = row_weights() * float(depth) + later
    earlier = [(jnp.bitwise_xor(chip, k) < chip).astype(jnp.float32) for k in offsets]

    slope, value = [], []
    for c in cs:
        above = sum(e * ref[:, c] for e, ref in zip(earlier, received))
        below = sum((1.0 - e) * ref[:, c] for e, ref in zip(earlier, received))
        above, below = above * alpha, below * alpha
        slope.append(slope_ref[:, c] + above)
        value.append(base_ref[:, c] + below + weights * above + slope[-1])

    def step(i, value):
        value = list(value)
        k = depth - 1 - i
        squares = []
        for j, c in enumerate(cs):
            stepped = inner_ref[k, :, c] - value[j]
            state_ref[k, :, c] = stepped
            value[j] = value[j] + slope[j]
            squares.append(stepped * stepped)
        while len(squares) > 1:
            squares = [a + b for a, b in zip(squares[::2], squares[1::2])]
        wide_ref[pl.ds(pl.multiple_of(k * SUBLANES, SUBLANES), SUBLANES), :] = squares[0]
        return value

    lax.fori_loop(0, depth, step, value, unroll=2)
    ones = jnp.ones((SUBLANES, LANES), jnp.float32)
    squares = lax.dot_general(
        ones, wide_ref[...], (((1,), (1,)), ((), ())), precision=lax.Precision.HIGHEST,
        preferred_element_type=jnp.float32,
    )
    squares_ref[...] = squares[0:1, :]


def end_kernel(own_ref, other_ref, limits_ref, state_ref, out_hbm, factor_ref, jumps_ref, sems):
    depth, _, cols = state_ref.shape
    cs = tiles(cols)
    shrink(own_ref, other_ref, limits_ref, factor_ref)
    copies = []
    for part in range(depth // SUBLANES):

        def step(i, carry, part=part):
            k = part * SUBLANES + i
            factor = factor_ref[k]
            for c in cs:
                jumps_ref[k, :, c] = state_ref[k, :, c] * factor
            return carry

        lax.fori_loop(0, SUBLANES, step, 0, unroll=2)
        for s in range(SUBLANES):
            copy = pltpu.make_async_copy(
                jumps_ref.at[pl.ds(part * SUBLANES, SUBLANES), s, :],
                out_hbm.at[pl.ds(s * depth + part * SUBLANES, SUBLANES), :],
                sems.at[part, s],
            )
            copy.start()
            copies.append(copy)
    for copy in copies:
        copy.wait()


def vmem(*shape):
    return pltpu.VMEM(shape, jnp.float32)


def call(kernel, name, operands, outs, kept=(), scratch=(), aliases=None, hbm=(), hbm_out=False):
    in_vmem = pl.BlockSpec(memory_space=pltpu.VMEM)
    in_hbm = pl.BlockSpec(memory_space=pl.ANY)
    operands = [
        pltpu.with_memory_space_constraint(x, pltpu.VMEM) if i in kept else x for i, x in enumerate(operands)
    ]
    return pl.pallas_call(
        kernel,
        out_shape=outs,
        in_specs=[in_hbm if i in hbm else in_vmem for i in range(len(operands))],
        out_specs=in_hbm if hbm_out else [in_vmem] * len(outs),
        scratch_shapes=scratch,
        input_output_aliases=aliases or {},
        compiler_params=pltpu.CompilerParams(vmem_limit_bytes=VMEM_LIMIT),
        name=name,
    )(*operands)


def local(mesh, signal, jump_sizes, thresholds):
    rows, cols = signal.shape
    chips, cores, halves = mesh.shape["probe"], mesh.shape["sub"], mesh.shape["prof"]
    depth = rows // SUBLANES
    count = float(rows * chips * cores)
    alpha, beta = STEP_LENGTH / (count * count), STEP_LENGTH / count
    chip, core = lax.axis_index("probe"), lax.axis_index("sub")
    offsets = tuple(reversed(range(1, chips)))
    swap = [(0, 1), (1, 0)]
    routes = {
        k: [(z * 2 + c, (z ^ k) * 2 + 1 - c) for z in range(chips) for c in range(2)] for k in offsets
    }
    limits = thresholds.reshape(SUBLANES, depth).T.reshape(1, rows)

    block = vmem(depth, SUBLANES, cols)
    strip, line, pair = vmem(SUBLANES, cols), vmem(1, rows), vmem(2, cols)
    spread = vmem(depth, SUBLANES, LANES)

    state, const, minus, totals, weighted, message = call(
        functools.partial(begin_kernel, beta, count), "begin", [signal, jump_sizes],
        [block, block, strip, strip, strip, pair], hbm=(0, 1),
        scratch=[pltpu.SemaphoreType.DMA((2, depth // SUBLANES, SUBLANES))],
    )
    factor = None
    for iteration in range(ITERS):
        if iteration:
            factor, totals, weighted, message = call(
                sums_kernel, "sums", [own, other, limits, state, minus], [spread, strip, strip, pair], kept=(3, 4)
            )
        sibling = lax.ppermute(message, "sub", swap)
        both = message + sibling
        lower = jnp.where(core == 0, message[0:1], sibling[0:1])
        upward = both[0:1]
        later = (chips - 1 - chip).astype(jnp.float32) * (2.0 * rows)
        downward = both[1:2] + float(rows) * lower + later * upward
        received = [
            lax.ppermute(jnp.where(jnp.bitwise_xor(chip, k) > chip, upward, downward), ("probe", "sub"), routes[k])
            for k in offsets
        ]
        scaled = factor is not None
        inner, slope, base = call(
            functools.partial(inner_kernel, alpha, chips, scaled), "inner",
            [state, const, factor if scaled else minus, totals, weighted, message, sibling],
            [block, strip, strip], kept=(0, 1, 2, 3, 4), aliases={0: 0},
        )
        state, own = call(
            functools.partial(outer_kernel, alpha, chips, offsets), "outer", [inner, slope, base, *received],
            [block, line], kept=(0, 1, 2), aliases={0: 0}, scratch=[vmem(rows, LANES)],
        )
        if halves == 2:
            other = lax.ppermute(own, "prof", swap)
        else:
            own, other = lax.psum(own, "prof"), jnp.zeros_like(own)
    return call(
        end_kernel, "finish", [own, other, limits, state], jax.ShapeDtypeStruct((rows, cols), jnp.float32), kept=(3,),
        hbm_out=True,
        scratch=[spread, block, pltpu.SemaphoreType.DMA((depth // SUBLANES, SUBLANES))],
    )


def solution(mesh):
    spec = P(("grp", "probe", "sub"), "prof")
    return jax.shard_map(
        functools.partial(local, mesh),
        mesh=mesh,
        in_specs=(spec, spec, P(("grp", "probe", "sub"))),
        out_specs=spec,
        check_vma=False,
    )
```

profile of v0, /device:TPU:0, one launch (start us, length us, event | category | flops | bytes accessed | tf_op | source)
XLA Modules:
  0.0 171.5 jit_solution(10273725490261449092)
XLA Ops:
  4.4 9.3 %begin.1 = (f32[64,8,2048]{2,1,0:T(8,128)S(1)}, f32[64,8,2048]{2,1,0:T(8,128)S(1)}, f32[8,2048]{1,0:T(8,128)S(1)}, f32[8,2048]{1,0:T(8,128)S(1)}, f32[8,2048]{1,0:T(8,128)S(1)}, /*index=5*/f32[2,2048]{1,0:T(2,128)S(1)}) custom-call(f32[512,2048]{1,0:T(8,128)S(1)} %copy-done.7, f32[512,2048]{1,0:T(8,128)S(1)} %copy-done.8), custom_call_target="tpu_custom_call" | custom-call | tf_op jit(solution)/shard_map/begin/pallas_call | solution.py:238
  19.1 3.8 %collective-permute-start.2 = (f32[1,2048]{1,0:T(1,128)S(1)}, f32[1,2048]{1,0:T(1,128)S(1)}, u32[]{:S(2)}, u32[]{:S(2)}) collective-permute-start(f32[1,2048]{1,0:T(1,128)S(1)} %get-tuple-element.183), channel_id=1, source_target_pairs={{0,9},{1,8},{4,13},{5,12},{8,1},{9,0},{12,5},{13,4},{2,11},{3,10},... | collective-permute-start | bytes 24584 | tf_op jit(solution)/shard_map/ppermute | solution.py:286
  28.8 3.6 %inner.8 = (f32[64,8,2048]{2,1,0:T(8,128)S(1)}, f32[8,2048]{1,0:T(8,128)S(1)}, f32[8,2048]{1,0:T(8,128)S(1)}) custom-call(f32[64,8,2048]{2,1,0:T(8,128)S(1)} %copy-done.1, f32[64,8,2048]{2,1,0:T(8,128)S(1)} %copy-done.5, f32[8,2048]{1,0:T(8,128)S(1)} %get-tuple-element.81.factor_ref.minus_ref, ...), custom_call_target="tpu_custom_call", output_to_operand_aliasing={{0}: (0, {})} | custom-call | tf_op jit(solution)/shard_map/inner/pallas_call | solution.py:238
  32.4 3.4 %outer.8 = (f32[64,8,2048]{2,1,0:T(8,128)S(1)}, f32[1,512]{1,0:T(1,128)S(1)}) custom-call(f32[64,8,2048]{2,1,0:T(8,128)S(1)} %get-tuple-element.85.inner_ref, f32[8,2048]{1,0:T(8,128)S(1)} %get-tuple-element.86.slope_ref, f32[8,2048]{1,0:T(8,128)S(1)} %get-tuple-element.87.base_ref, ...), custom_call_target="tpu_custom_call", output_to_operand_aliasing={{0}: (0, {})} | custom-call | tf_op jit(solution)/shard_map/outer/pallas_call | solution.py:238
  49.6 4.6 %inner.9 = (f32[64,8,2048]{2,1,0:T(8,128)S(1)}, f32[8,2048]{1,0:T(8,128)S(1)}, f32[8,2048]{1,0:T(8,128)S(1)}) custom-call(f32[64,8,2048]{2,1,0:T(8,128)S(1)} %copy-done.3, f32[64,8,2048]{2,1,0:T(8,128)S(1)} %copy-done.6, f32[64,8,128]{2,1,0:T(8,128)S(1)} %get-tuple-element.90.factor_ref, ...), custom_call_target="tpu_custom_call", output_to_operand_aliasing={{0}: (0, {})} | custom-call | tf_op jit(solution)/shard_map/inner/pallas_call | solution.py:238
  54.3 3.4 %outer.9 = (f32[64,8,2048]{2,1,0:T(8,128)S(1)}, f32[1,512]{1,0:T(1,128)S(1)}) custom-call(f32[64,8,2048]{2,1,0:T(8,128)S(1)} %get-tuple-element.94.inner_ref, f32[8,2048]{1,0:T(8,128)S(1)} %get-tuple-element.95.slope_ref, f32[8,2048]{1,0:T(8,128)S(1)} %get-tuple-element.96.base_ref, ...), custom_call_target="tpu_custom_call", output_to_operand_aliasing={{0}: (0, {})} | custom-call | tf_op jit(solution)/shard_map/outer/pallas_call | solution.py:238
  63.6 2.6 %collective-permute-start.12 = (f32[1,2048]{1,0:T(1,128)S(1)}, f32[1,2048]{1,0:T(1,128)S(1)}, u32[]{:S(2)}, u32[]{:S(2)}) collective-permute-start(f32[1,2048]{1,0:T(1,128)S(1)} %get-tuple-element.179), channel_id=1, source_target_pairs={{0,9},{1,8},{4,13},{5,12},{8,1},{9,0},{12,5},{13,4},{2,11},{3,10},... | collective-permute-start | bytes 24584 | tf_op jit(solution)/shard_map/ppermute | solution.py:286
  67.5 4.6 %inner.10 = (f32[64,8,2048]{2,1,0:T(8,128)S(1)}, f32[8,2048]{1,0:T(8,128)S(1)}, f32[8,2048]{1,0:T(8,128)S(1)}) custom-call(f32[64,8,2048]{2,1,0:T(8,128)S(1)} %get-tuple-element.97.state_ref, f32[64,8,2048]{2,1,0:T(8,128)S(1)} %copy-done.6, f32[64,8,128]{2,1,0:T(8,128)S(1)} %get-tuple-element.99.factor_ref, ...), custom_call_target="tpu_custom_call", output_to_operand_aliasing={{0}: (0, {})} | custom-call | tf_op jit(solution)/shard_map/inner/pallas_call | solution.py:238
  72.1 3.4 %outer.10 = (f32[64,8,2048]{2,1,0:T(8,128)S(1)}, f32[1,512]{1,0:T(1,128)S(1)}) custom-call(f32[64,8,2048]{2,1,0:T(8,128)S(1)} %get-tuple-element.103.inner_ref, f32[8,2048]{1,0:T(8,128)S(1)} %get-tuple-element.104.slope_ref, f32[8,2048]{1,0:T(8,128)S(1)} %get-tuple-element.105.base_ref, ...), custom_call_target="tpu_custom_call", output_to_operand_aliasing={{0}: (0, {})} | custom-call | tf_op jit(solution)/shard_map/outer/pallas_call | solution.py:238
  85.4 4.6 %inner.11 = (f32[64,8,2048]{2,1,0:T(8,128)S(1)}, f32[8,2048]{1,0:T(8,128)S(1)}, f32[8,2048]{1,0:T(8,128)S(1)}) custom-call(f32[64,8,2048]{2,1,0:T(8,128)S(1)} %get-tuple-element.106.state_ref, f32[64,8,2048]{2,1,0:T(8,128)S(1)} %copy-done.6, f32[64,8,128]{2,1,0:T(8,128)S(1)} %get-tuple-element.108.factor_ref, ...), custom_call_target="tpu_custom_call", output_to_operand_aliasing={{0}: (0, {})} | custom-call | tf_op jit(solution)/shard_map/inner/pallas_call | solution.py:238
  90.0 3.4 %outer.11 = (f32[64,8,2048]{2,1,0:T(8,128)S(1)}, f32[1,512]{1,0:T(1,128)S(1)}) custom-call(f32[64,8,2048]{2,1,0:T(8,128)S(1)} %get-tuple-element.112.inner_ref, f32[8,2048]{1,0:T(8,128)S(1)} %get-tuple-element.113.slope_ref, f32[8,2048]{1,0:T(8,128)S(1)} %get-tuple-element.114.base_ref, ...), custom_call_target="tpu_custom_call", output_to_operand_aliasing={{0}: (0, {})} | custom-call | tf_op jit(solution)/shard_map/outer/pallas_call | solution.py:238
  99.4 2.6 %collective-permute-start.22 = (f32[1,2048]{1,0:T(1,128)S(1)}, f32[1,2048]{1,0:T(1,128)S(1)}, u32[]{:S(2)}, u32[]{:S(2)}) collective-permute-start(f32[1,2048]{1,0:T(1,128)S(1)} %get-tuple-element.175), channel_id=1, source_target_pairs={{0,9},{1,8},{4,13},{5,12},{8,1},{9,0},{12,5},{13,4},{2,11},{3,10},... | collective-permute-start | bytes 24584 | tf_op jit(solution)/shard_map/ppermute | solution.py:286
  103.3 4.6 %inner.12 = (f32[64,8,2048]{2,1,0:T(8,128)S(1)}, f32[8,2048]{1,0:T(8,128)S(1)}, f32[8,2048]{1,0:T(8,128)S(1)}) custom-call(f32[64,8,2048]{2,1,0:T(8,128)S(1)} %get-tuple-element.115.state_ref, f32[64,8,2048]{2,1,0:T(8,128)S(1)} %copy-done.6, f32[64,8,128]{2,1,0:T(8,128)S(1)} %get-tuple-element.117.factor_ref, ...), custom_call_target="tpu_custom_call", output_to_operand_aliasing={{0}: (0, {})} | custom-call | tf_op jit(solution)/shard_map/inner/pallas_call | solution.py:238
  107.9 3.4 %outer.12 = (f32[64,8,2048]{2,1,0:T(8,128)S(1)}, f32[1,512]{1,0:T(1,128)S(1)}) custom-call(f32[64,8,2048]{2,1,0:T(8,128)S(1)} %get-tuple-element.121.inner_ref, f32[8,2048]{1,0:T(8,128)S(1)} %get-tuple-element.122.slope_ref, f32[8,2048]{1,0:T(8,128)S(1)} %get-tuple-element.123.base_ref, ...), custom_call_target="tpu_custom_call", output_to_operand_aliasing={{0}: (0, {})} | custom-call | tf_op jit(solution)/shard_map/outer/pallas_call | solution.py:238
  117.2 2.6 %collective-permute-start.27 = (f32[1,2048]{1,0:T(1,128)S(1)}, f32[1,2048]{1,0:T(1,128)S(1)}, u32[]{:S(2)}, u32[]{:S(2)}) collective-permute-start(f32[1,2048]{1,0:T(1,128)S(1)} %get-tuple-element.173), channel_id=1, source_target_pairs={{0,9},{1,8},{4,13},{5,12},{8,1},{9,0},{12,5},{13,4},{2,11},{3,10},... | collective-permute-start | bytes 24584 | tf_op jit(solution)/shard_map/ppermute | solution.py:286
  121.2 4.6 %inner.13 = (f32[64,8,2048]{2,1,0:T(8,128)S(1)}, f32[8,2048]{1,0:T(8,128)S(1)}, f32[8,2048]{1,0:T(8,128)S(1)}) custom-call(f32[64,8,2048]{2,1,0:T(8,128)S(1)} %get-tuple-element.124.state_ref, f32[64,8,2048]{2,1,0:T(8,128)S(1)} %copy-done.6, f32[64,8,128]{2,1,0:T(8,128)S(1)} %get-tuple-element.126.factor_ref, ...), custom_call_target="tpu_custom_call", output_to_operand_aliasing={{0}: (0, {})} | custom-call | tf_op jit(solution)/shard_map/inner/pallas_call | solution.py:238
  125.8 3.4 %outer.13 = (f32[64,8,2048]{2,1,0:T(8,128)S(1)}, f32[1,512]{1,0:T(1,128)S(1)}) custom-call(f32[64,8,2048]{2,1,0:T(8,128)S(1)} %get-tuple-element.130.inner_ref, f32[8,2048]{1,0:T(8,128)S(1)} %get-tuple-element.131.slope_ref, f32[8,2048]{1,0:T(8,128)S(1)} %get-tuple-element.132.base_ref, ...), custom_call_target="tpu_custom_call", output_to_operand_aliasing={{0}: (0, {})} | custom-call | tf_op jit(solution)/shard_map/outer/pallas_call | solution.py:238
  135.1 2.6 %collective-permute-start.32 = (f32[1,2048]{1,0:T(1,128)S(1)}, f32[1,2048]{1,0:T(1,128)S(1)}, u32[]{:S(2)}, u32[]{:S(2)}) collective-permute-start(f32[1,2048]{1,0:T(1,128)S(1)} %get-tuple-element.171), channel_id=1, source_target_pairs={{0,9},{1,8},{4,13},{5,12},{8,1},{9,0},{12,5},{13,4},{2,11},{3,10},... | collective-permute-start | bytes 24584 | tf_op jit(solution)/shard_map/ppermute | solution.py:286
  139.1 4.6 %inner.14 = (f32[64,8,2048]{2,1,0:T(8,128)S(1)}, f32[8,2048]{1,0:T(8,128)S(1)}, f32[8,2048]{1,0:T(8,128)S(1)}) custom-call(f32[64,8,2048]{2,1,0:T(8,128)S(1)} %get-tuple-element.133.state_ref, f32[64,8,2048]{2,1,0:T(8,128)S(1)} %copy-done.6, f32[64,8,128]{2,1,0:T(8,128)S(1)} %get-tuple-element.135.factor_ref, ...), custom_call_target="tpu_custom_call", output_to_operand_aliasing={{0}: (0, {})} | custom-call | tf_op jit(solution)/shard_map/inner/pallas_call | solution.py:238
  143.7 3.4 %outer.14 = (f32[64,8,2048]{2,1,0:T(8,128)S(1)}, f32[1,512]{1,0:T(1,128)S(1)}) custom-call(f32[64,8,2048]{2,1,0:T(8,128)S(1)} %get-tuple-element.139.inner_ref, f32[8,2048]{1,0:T(8,128)S(1)} %get-tuple-element.140.slope_ref, f32[8,2048]{1,0:T(8,128)S(1)} %get-tuple-element.141.base_ref, ...), custom_call_target="tpu_custom_call", output_to_operand_aliasing={{0}: (0, {})} | custom-call | tf_op jit(solution)/shard_map/outer/pallas_call | solution.py:238
  153.0 2.6 %collective-permute-start.37 = (f32[1,2048]{1,0:T(1,128)S(1)}, f32[1,2048]{1,0:T(1,128)S(1)}, u32[]{:S(2)}, u32[]{:S(2)}) collective-permute-start(f32[1,2048]{1,0:T(1,128)S(1)} %get-tuple-element.169), channel_id=1, source_target_pairs={{0,9},{1,8},{4,13},{5,12},{8,1},{9,0},{12,5},{13,4},{2,11},{3,10},... | collective-permute-start | bytes 24584 | tf_op jit(solution)/shard_map/ppermute | solution.py:286
  156.9 4.6 %inner.15 = (f32[64,8,2048]{2,1,0:T(8,128)S(1)}, f32[8,2048]{1,0:T(8,128)S(1)}, f32[8,2048]{1,0:T(8,128)S(1)}) custom-call(f32[64,8,2048]{2,1,0:T(8,128)S(1)} %get-tuple-element.142.state_ref, f32[64,8,2048]{2,1,0:T(8,128)S(1)} %copy-done.6, f32[64,8,128]{2,1,0:T(8,128)S(1)} %get-tuple-element.144.factor_ref, ...), custom_call_target="tpu_custom_call", output_to_operand_aliasing={{0}: (0, {})} | custom-call | tf_op jit(solution)/shard_map/inner/pallas_call | solution.py:238
  161.6 3.4 %outer.15 = (f32[64,8,2048]{2,1,0:T(8,128)S(1)}, f32[1,512]{1,0:T(1,128)S(1)}) custom-call(f32[64,8,2048]{2,1,0:T(8,128)S(1)} %get-tuple-element.148.inner_ref, f32[8,2048]{1,0:T(8,128)S(1)} %get-tuple-element.149.slope_ref, f32[8,2048]{1,0:T(8,128)S(1)} %get-tuple-element.150.base_ref, ...), custom_call_target="tpu_custom_call", output_to_operand_aliasing={{0}: (0, {})} | custom-call | tf_op jit(solution)/shard_map/outer/pallas_call | solution.py:238
  168.6 2.7 %finish.1 = f32[512,2048]{1,0:T(8,128)} custom-call(f32[1,512]{1,0:T(1,128)S(1)} %get-tuple-element.151.own_ref, f32[1,512]{1,0:T(1,128)S(1)} %collective-permute-done.39.other_ref, f32[1,512]{1,0:T(1,128)S(1)} %reshape.7.limits_ref, f32[64,8,2048]{2,1,0:T(8,128)S(1)} %get-tuple-element.152.state_ref), custom_call_target="tpu_custom_call" | custom-call | tf_op jit(solution)/shard_map/finish/pallas_call | solution.py:238
  (128 shorter events, 78.7 us)
Async XLA Ops:
  19.1 13.3 %collective-permute-start.2 = (f32[1,2048]{1,0:T(1,128)S(1)}, f32[1,2048]{1,0:T(1,128)S(1)}, u32[]{:S(2)}, u32[]{:S(2)}) collective-permute-start(f32[1,2048]{1,0:T(1,128)S(1)} %get-tuple-element.183), channel_id=1, source_target_pairs={{0,9},{1,8},{4,13},{5,12},{8,1},{9,0},{12,5},{13,4},{2,11},{3,10},... | collective-permute-start | bytes 24584 | tf_op jit(solution)/shard_map/ppermute | solution.py:286
  22.8 9.5 %collective-permute-start.1 = (f32[1,2048]{1,0:T(1,128)S(1)}, f32[1,2048]{1,0:T(1,128)S(1)}, u32[]{:S(2)}, u32[]{:S(2)}) collective-permute-start(f32[1,2048]{1,0:T(1,128)S(1)} %get-tuple-element.184), channel_id=1, source_target_pairs={{0,13},{1,12},{4,9},{5,8},{8,5},{9,4},{12,1},{13,0},{2,15},{3,14},... | collective-permute-start | bytes 24584 | tf_op jit(solution)/shard_map/ppermute | solution.py:286
  24.1 8.2 %collective-permute-start.3 = (f32[1,2048]{1,0:T(1,128)S(1)}, f32[1,2048]{1,0:T(1,128)S(1)}, u32[]{:S(2)}, u32[]{:S(2)}) collective-permute-start(f32[1,2048]{1,0:T(1,128)S(1)} %get-tuple-element.167), channel_id=1, source_target_pairs={{0,5},{1,4},{4,1},{5,0},{8,13},{9,12},{12,9},{13,8},{2,7},{3,6},{6... | collective-permute-start | bytes 24584 | tf_op jit(solution)/shard_map/ppermute | solution.py:286
  45.9 8.3 %collective-permute-start.7 = (f32[1,2048]{1,0:T(1,128)S(1)}, f32[1,2048]{1,0:T(1,128)S(1)}, u32[]{:S(2)}, u32[]{:S(2)}) collective-permute-start(f32[1,2048]{1,0:T(1,128)S(1)} %get-tuple-element.181), channel_id=1, source_target_pairs={{0,9},{1,8},{4,13},{5,12},{8,1},{9,0},{12,5},{13,4},{2,11},{3,10},... | collective-permute-start | bytes 24584 | tf_op jit(solution)/shard_map/ppermute | solution.py:286
  48.3 5.9 %collective-permute-start.6 = (f32[1,2048]{1,0:T(1,128)S(1)}, f32[1,2048]{1,0:T(1,128)S(1)}, u32[]{:S(2)}, u32[]{:S(2)}) collective-permute-start(f32[1,2048]{1,0:T(1,128)S(1)} %get-tuple-element.182), channel_id=1, source_target_pairs={{0,13},{1,12},{4,9},{5,8},{8,5},{9,4},{12,1},{13,0},{2,15},{3,14},... | collective-permute-start | bytes 24584 | tf_op jit(solution)/shard_map/ppermute | solution.py:286
  49.6 4.6 %collective-permute-start.8 = (f32[1,2048]{1,0:T(1,128)S(1)}, f32[1,2048]{1,0:T(1,128)S(1)}, u32[]{:S(2)}, u32[]{:S(2)}) collective-permute-start(f32[1,2048]{1,0:T(1,128)S(1)} %get-tuple-element.165), channel_id=1, source_target_pairs={{0,5},{1,4},{4,1},{5,0},{8,13},{9,12},{12,9},{13,8},{2,7},{3,6},{6... | collective-permute-start | bytes 24584 | tf_op jit(solution)/shard_map/ppermute | solution.py:286
  63.6 8.5 %collective-permute-start.12 = (f32[1,2048]{1,0:T(1,128)S(1)}, f32[1,2048]{1,0:T(1,128)S(1)}, u32[]{:S(2)}, u32[]{:S(2)}) collective-permute-start(f32[1,2048]{1,0:T(1,128)S(1)} %get-tuple-element.179), channel_id=1, source_target_pairs={{0,9},{1,8},{4,13},{5,12},{8,1},{9,0},{12,5},{13,4},{2,11},{3,10},... | collective-permute-start | bytes 24584 | tf_op jit(solution)/shard_map/ppermute | solution.py:286
  66.2 5.9 %collective-permute-start.11 = (f32[1,2048]{1,0:T(1,128)S(1)}, f32[1,2048]{1,0:T(1,128)S(1)}, u32[]{:S(2)}, u32[]{:S(2)}) collective-permute-start(f32[1,2048]{1,0:T(1,128)S(1)} %get-tuple-element.180), channel_id=1, source_target_pairs={{0,13},{1,12},{4,9},{5,8},{8,5},{9,4},{12,1},{13,0},{2,15},{3,14},... | collective-permute-start | bytes 24584 | tf_op jit(solution)/shard_map/ppermute | solution.py:286
  67.5 4.6 %collective-permute-start.13 = (f32[1,2048]{1,0:T(1,128)S(1)}, f32[1,2048]{1,0:T(1,128)S(1)}, u32[]{:S(2)}, u32[]{:S(2)}) collective-permute-start(f32[1,2048]{1,0:T(1,128)S(1)} %get-tuple-element.163), channel_id=1, source_target_pairs={{0,5},{1,4},{4,1},{5,0},{8,13},{9,12},{12,9},{13,8},{2,7},{3,6},{6... | collective-permute-start | bytes 24584 | tf_op jit(solution)/shard_map/ppermute | solution.py:286
  81.5 8.5 %collective-permute-start.17 = (f32[1,2048]{1,0:T(1,128)S(1)}, f32[1,2048]{1,0:T(1,128)S(1)}, u32[]{:S(2)}, u32[]{:S(2)}) collective-permute-start(f32[1,2048]{1,0:T(1,128)S(1)} %get-tuple-element.177), channel_id=1, source_target_pairs={{0,9},{1,8},{4,13},{5,12},{8,1},{9,0},{12,5},{13,4},{2,11},{3,10},... | collective-permute-start | bytes 24584 | tf_op jit(solution)/shard_map/ppermute | solution.py:286
  84.1 5.9 %collective-permute-start.16 = (f32[1,2048]{1,0:T(1,128)S(1)}, f32[1,2048]{1,0:T(1,128)S(1)}, u32[]{:S(2)}, u32[]{:S(2)}) collective-permute-start(f32[1,2048]{1,0:T(1,128)S(1)} %get-tuple-element.178), channel_id=1, source_target_pairs={{0,13},{1,12},{4,9},{5,8},{8,5},{9,4},{12,1},{13,0},{2,15},{3,14},... | collective-permute-start | bytes 24584 | tf_op jit(solution)/shard_map/ppermute | solution.py:286
  85.4 4.6 %collective-permute-start.18 = (f32[1,2048]{1,0:T(1,128)S(1)}, f32[1,2048]{1,0:T(1,128)S(1)}, u32[]{:S(2)}, u32[]{:S(2)}) collective-permute-start(f32[1,2048]{1,0:T(1,128)S(1)} %get-tuple-element.161), channel_id=1, source_target_pairs={{0,5},{1,4},{4,1},{5,0},{8,13},{9,12},{12,9},{13,8},{2,7},{3,6},{6... | collective-permute-start | bytes 24584 | tf_op jit(solution)/shard_map/ppermute | solution.py:286
  99.4 8.5 %collective-permute-start.22 = (f32[1,2048]{1,0:T(1,128)S(1)}, f32[1,2048]{1,0:T(1,128)S(1)}, u32[]{:S(2)}, u32[]{:S(2)}) collective-permute-start(f32[1,2048]{1,0:T(1,128)S(1)} %get-tuple-element.175), channel_id=1, source_target_pairs={{0,9},{1,8},{4,13},{5,12},{8,1},{9,0},{12,5},{13,4},{2,11},{3,10},... | collective-permute-start | bytes 24584 | tf_op jit(solution)/shard_map/ppermute | solution.py:286
  102.0 5.9 %collective-permute-start.21 = (f32[1,2048]{1,0:T(1,128)S(1)}, f32[1,2048]{1,0:T(1,128)S(1)}, u32[]{:S(2)}, u32[]{:S(2)}) collective-permute-start(f32[1,2048]{1,0:T(1,128)S(1)} %get-tuple-element.176), channel_id=1, source_target_pairs={{0,13},{1,12},{4,9},{5,8},{8,5},{9,4},{12,1},{13,0},{2,15},{3,14},... | collective-permute-start | bytes 24584 | tf_op jit(solution)/shard_map/ppermute | solution.py:286
  103.3 4.6 %collective-permute-start.23 = (f32[1,2048]{1,0:T(1,128)S(1)}, f32[1,2048]{1,0:T(1,128)S(1)}, u32[]{:S(2)}, u32[]{:S(2)}) collective-permute-start(f32[1,2048]{1,0:T(1,128)S(1)} %get-tuple-element.159), channel_id=1, source_target_pairs={{0,5},{1,4},{4,1},{5,0},{8,13},{9,12},{12,9},{13,8},{2,7},{3,6},{6... | collective-permute-start | bytes 24584 | tf_op jit(solution)/shard_map/ppermute | solution.py:286
  117.2 8.5 %collective-permute-start.27 = (f32[1,2048]{1,0:T(1,128)S(1)}, f32[1,2048]{1,0:T(1,128)S(1)}, u32[]{:S(2)}, u32[]{:S(2)}) collective-permute-start(f32[1,2048]{1,0:T(1,128)S(1)} %get-tuple-element.173), channel_id=1, source_target_pairs={{0,9},{1,8},{4,13},{5,12},{8,1},{9,0},{12,5},{13,4},{2,11},{3,10},... | collective-permute-start | bytes 24584 | tf_op jit(solution)/shard_map/ppermute | solution.py:286
  119.9 5.9 %collective-permute-start.26 = (f32[1,2048]{1,0:T(1,128)S(1)}, f32[1,2048]{1,0:T(1,128)S(1)}, u32[]{:S(2)}, u32[]{:S(2)}) collective-permute-start(f32[1,2048]{1,0:T(1,128)S(1)} %get-tuple-element.174), channel_id=1, source_target_pairs={{0,13},{1,12},{4,9},{5,8},{8,5},{9,4},{12,1},{13,0},{2,15},{3,14},... | collective-permute-start | bytes 24584 | tf_op jit(solution)/shard_map/ppermute | solution.py:286
  121.2 4.6 %collective-permute-start.28 = (f32[1,2048]{1,0:T(1,128)S(1)}, f32[1,2048]{1,0:T(1,128)S(1)}, u32[]{:S(2)}, u32[]{:S(2)}) collective-permute-start(f32[1,2048]{1,0:T(1,128)S(1)} %get-tuple-element.157), channel_id=1, source_target_pairs={{0,5},{1,4},{4,1},{5,0},{8,13},{9,12},{12,9},{13,8},{2,7},{3,6},{6... | collective-permute-start | bytes 24584 | tf_op jit(solution)/shard_map/ppermute | solution.py:286
  135.1 8.5 %collective-permute-start.32 = (f32[1,2048]{1,0:T(1,128)S(1)}, f32[1,2048]{1,0:T(1,128)S(1)}, u32[]{:S(2)}, u32[]{:S(2)}) collective-permute-start(f32[1,2048]{1,0:T(1,128)S(1)} %get-tuple-element.171), channel_id=1, source_target_pairs={{0,9},{1,8},{4,13},{5,12},{8,1},{9,0},{12,5},{13,4},{2,11},{3,10},... | collective-permute-start | bytes 24584 | tf_op jit(solution)/shard_map/ppermute | solution.py:286
  137.8 5.9 %collective-permute-start.31 = (f32[1,2048]{1,0:T(1,128)S(1)}, f32[1,2048]{1,0:T(1,128)S(1)}, u32[]{:S(2)}, u32[]{:S(2)}) collective-permute-start(f32[1,2048]{1,0:T(1,128)S(1)} %get-tuple-element.172), channel_id=1, source_target_pairs={{0,13},{1,12},{4,9},{5,8},{8,5},{9,4},{12,1},{13,0},{2,15},{3,14},... | collective-permute-start | bytes 24584 | tf_op jit(solution)/shard_map/ppermute | solution.py:286
  139.1 4.6 %collective-permute-start.33 = (f32[1,2048]{1,0:T(1,128)S(1)}, f32[1,2048]{1,0:T(1,128)S(1)}, u32[]{:S(2)}, u32[]{:S(2)}) collective-permute-start(f32[1,2048]{1,0:T(1,128)S(1)} %get-tuple-element.155), channel_id=1, source_target_pairs={{0,5},{1,4},{4,1},{5,0},{8,13},{9,12},{12,9},{13,8},{2,7},{3,6},{6... | collective-permute-start | bytes 24584 | tf_op jit(solution)/shard_map/ppermute | solution.py:286
  153.0 8.5 %collective-permute-start.37 = (f32[1,2048]{1,0:T(1,128)S(1)}, f32[1,2048]{1,0:T(1,128)S(1)}, u32[]{:S(2)}, u32[]{:S(2)}) collective-permute-start(f32[1,2048]{1,0:T(1,128)S(1)} %get-tuple-element.169), channel_id=1, source_target_pairs={{0,9},{1,8},{4,13},{5,12},{8,1},{9,0},{12,5},{13,4},{2,11},{3,10},... | collective-permute-start | bytes 24584 | tf_op jit(solution)/shard_map/ppermute | solution.py:286
  155.6 5.9 %collective-permute-start.36 = (f32[1,2048]{1,0:T(1,128)S(1)}, f32[1,2048]{1,0:T(1,128)S(1)}, u32[]{:S(2)}, u32[]{:S(2)}) collective-permute-start(f32[1,2048]{1,0:T(1,128)S(1)} %get-tuple-element.170), channel_id=1, source_target_pairs={{0,13},{1,12},{4,9},{5,8},{8,5},{9,4},{12,1},{13,0},{2,15},{3,14},... | collective-permute-start | bytes 24584 | tf_op jit(solution)/shard_map/ppermute | solution.py:286
  156.9 4.6 %collective-permute-start.38 = (f32[1,2048]{1,0:T(1,128)S(1)}, f32[1,2048]{1,0:T(1,128)S(1)}, u32[]{:S(2)}, u32[]{:S(2)}) collective-permute-start(f32[1,2048]{1,0:T(1,128)S(1)} %get-tuple-element.153), channel_id=1, source_target_pairs={{0,5},{1,4},{4,1},{5,0},{8,13},{9,12},{12,9},{13,8},{2,7},{3,6},{6... | collective-permute-start | bytes 24584 | tf_op jit(solution)/shard_map/ppermute | solution.py:286
  (26 other events, 68.9 us)
where the time goes:
time: 172 us; the launch traced here: 171 us
  Pallas kernels  81.9 us (48%)
  starting transfers between devices  45.6 us (27%)
  waiting for transfers between devices  25.6 us (15%)
  local copies, waits for them, and re-layouts  17.3 us (10%)
    pallas_call x25, Pallas kernels, call(): pl.pallas_call(kernel, out_shape=outs, in_specs=[in_hbm if i in hbm else...  81.9 us
    ppermute x24, starting transfers between devices, local(): lax.ppermute(jnp.where(jnp.bitwise_xor(chip, k) > chip, upward, downward)...  32.6 us
    unnamed x20, local copies, waits for them, and re-layouts  17 us
    ppermute x8, waiting for transfers between devices, local(): other = lax.ppermute(own, 'prof', swap)  16.5 us
    ppermute x8, starting transfers between devices, local(): other = lax.ppermute(own, 'prof', swap)  12 us
    ppermute x8, waiting for transfers between devices, local(): sibling = lax.ppermute(message, 'sub', swap)  9.03 us
  transfers between devices with their start and end apart: 40, of which 16 were waited for; matrix products, arithmetic and copies ran while one was open for 0% of the time, Pallas kernels for 21%

commit v1 on v0

--- a/solution.py
+++ b/solution.py
@@ -12,10 +12,17 @@
 LANES = 128
 SUBLANES = 8
 VMEM_LIMIT = 16 * 1024 * 1024
+WIDTH, BATCH = 8, 4
+OUTER_WIDTH, OUTER_BATCH = 8, 4
 
 
 def tiles(cols):
     return [slice(j * LANES, (j + 1) * LANES) for j in range(cols // LANES)]
+
+
+def groups(cols, width):
+    cs = tiles(cols)
+    return [cs[g : g + width] for g in range(0, len(cs), width)]
 
 
 def row_weights():
@@ -31,8 +38,8 @@
         message_ref[1:2, c] = jnp.sum(weights * total[j] + weighted[j], axis=0, keepdims=True)
 
 
-def begin_kernel(beta, count, signal_hbm, jumps_hbm, state_ref, const_ref, minus_ref, totals_ref, weighted_ref,
-                 message_ref, sems):
+def begin_kernel(chips, beta, count, signal_hbm, jumps_hbm, thresholds_ref, state_ref, const_ref, minus_ref, totals_ref,
+                 weighted_ref, message_ref, limits_ref, marks_ref, sems):
     depth, _, cols = state_ref.shape
     cs = tiles(cols)
     parts = depth // SUBLANES
@@ -49,6 +56,22 @@
     for part in reversed(range(parts)):
         for copy in copies(part):
             copy.start()
+
+    rows = depth * SUBLANES
+    source = lax.broadcasted_iota(jnp.int32, (rows, rows), 0)
+    target = lax.broadcasted_iota(jnp.int32, (rows, rows), 1)
+    chosen = jnp.where(source == (target % SUBLANES) * depth + target // SUBLANES, 1.0, 0.0)
+    limits_ref[...] = lax.dot_general(
+        jnp.broadcast_to(thresholds_ref[...], (SUBLANES, rows)), chosen, (((1,), (0,)), ((), ())),
+        precision=lax.Precision.HIGHEST, preferred_element_type=jnp.float32,
+    )[0:1, :]
+    chip, core = lax.axis_index("probe"), lax.axis_index("sub")
+    later = (chips - 1 - chip).astype(jnp.float32) * (2.0 * rows)
+    marks = [(core == 0).astype(jnp.float32), later]
+    marks += [(jnp.bitwise_xor(chip, k) > chip).astype(jnp.float32) for k in range(1, chips)]
+    for i, mark in enumerate(marks):
+        marks_ref[i : i + 1, :] = jnp.full((1, cols), mark, jnp.float32)
+
     zero = jnp.zeros((SUBLANES, LANES), jnp.float32)
     carry = ([zero] * len(cs), [zero] * len(cs), [zero] * len(cs))
     for part in reversed(range(parts)):
@@ -60,11 +83,12 @@
             k = part * SUBLANES + SUBLANES - 1 - i
             weight = (depth - k).astype(jnp.float32)
             for j, c in enumerate(cs):
-                suffix[j] = suffix[j] + const_ref[k, :, c]
-                const_ref[k, :, c] = suffix[j] * beta
                 jump = state_ref[k, :, c]
                 total[j] = total[j] + jump
                 weighted[j] = weighted[j] + jump * weight
+                suffix[j] = suffix[j] + const_ref[k, :, c]
+            for j, c in enumerate(cs):
+                const_ref[k, :, c] = suffix[j] * beta
             return suffix, total, weighted
 
         carry = lax.fori_loop(0, SUBLANES, step, carry)
@@ -125,22 +149,29 @@
     sublane = lax.broadcasted_iota(jnp.int32, (SUBLANES, LANES), 0)
     weights = row_weights() * float(depth)
 
-    def step(i, carry):
-        running, double = (list(x) for x in carry)
-        k = depth - 1 - i
-        if scaled:
-            factor = factor_ref[k]
-        for j, c in enumerate(cs):
-            jump = state_ref[k, :, c]
-            if scaled:
-                jump = jump * factor
-            double[j] = double[j] + running[j]
-            inner_ref[k, :, c] = jump + const_ref[k, :, c] - double[j]
-            running[j] = running[j] - jump * alpha
-        return running, double
-
     zero = jnp.zeros((SUBLANES, LANES), jnp.float32)
-    lax.fori_loop(0, depth, step, ([totals_ref[:, c] * alpha for c in cs], [zero] * len(cs)), unroll=2)
+    for group in groups(cols, WIDTH):
+
+        def step(i, carry, group=group):
+            running, double = (list(x) for x in carry)
+            start = depth - (i + 1) * BATCH
+            results = []
+            for k in reversed([start + q for q in range(BATCH)]):
+                factor = factor_ref[k] if scaled else None
+                for j, c in enumerate(group):
+                    jump = state_ref[k, :, c]
+                    if scaled:
+                        jump = jump * factor
+                    double[j] = double[j] + running[j]
+                    results.append((k, c, jump + const_ref[k, :, c] - double[j]))
+                    running[j] = running[j] - jump * alpha
+            for k, c, value in results:
+                inner_ref[k, :, c] = value
+            return running, double
+
+        lax.fori_loop(
+            0, depth // BATCH, step, ([totals_ref[:, c] * alpha for c in group], [zero] * len(group))
+        )
 
     for c in cs:
         total = totals_ref[:, c]
@@ -161,36 +192,43 @@
     received, (state_ref, squares_ref, wide_ref) = refs[: len(offsets)], refs[len(offsets) :]
     depth, _, cols = inner_ref.shape
     rows = float(depth * SUBLANES)
-    cs = tiles(cols)
     chip, core = lax.axis_index("probe"), lax.axis_index("sub")
     later = (chips - 1 - chip).astype(jnp.float32) * (2.0 * rows) + (core == 0).astype(jnp.float32) * rows
     weights = row_weights() * float(depth) + later
     earlier = [(jnp.bitwise_xor(chip, k) < chip).astype(jnp.float32) for k in offsets]
 
-    slope, value = [], []
-    for c in cs:
-        above = sum(e * ref[:, c] for e, ref in zip(earlier, received))
-        below = sum((1.0 - e) * ref[:, c] for e, ref in zip(earlier, received))
-        above, below = above * alpha, below * alpha
-        slope.append(slope_ref[:, c] + above)
-        value.append(base_ref[:, c] + below + weights * above + slope[-1])
-
-    def step(i, value):
-        value = list(value)
-        k = depth - 1 - i
-        squares = []
-        for j, c in enumerate(cs):
-            stepped = inner_ref[k, :, c] - value[j]
-            state_ref[k, :, c] = stepped
-            value[j] = value[j] + slope[j]
-            squares.append(stepped * stepped)
-        while len(squares) > 1:
-            squares = [a + b for a, b in zip(squares[::2], squares[1::2])]
-        wide_ref[pl.ds(pl.multiple_of(k * SUBLANES, SUBLANES), SUBLANES), :] = squares[0]
-        return value
-
-    lax.fori_loop(0, depth, step, value, unroll=2)
-    ones = jnp.ones((SUBLANES, LANES), jnp.float32)
+    for g, group in enumerate(groups(cols, OUTER_WIDTH)):
+        slope, value = [], []
+        for c in group:
+            above = sum(e * ref[:, c] for e, ref in zip(earlier, received))
+            below = sum((1.0 - e) * ref[:, c] for e, ref in zip(earlier, received))
+            above, below = above * alpha, below * alpha
+            slope.append(slope_ref[:, c] + above)
+            value.append(base_ref[:, c] + below + weights * above + slope[-1])
+
+        def step(i, value, g=g, group=group, slope=slope):
+            value = list(value)
+            start = depth - (i + 1) * OUTER_BATCH
+            results, sums = [], []
+            for k in reversed([start + q for q in range(OUTER_BATCH)]):
+                squares = []
+                for j, c in enumerate(group):
+                    stepped = inner_ref[k, :, c] - value[j]
+                    value[j] = value[j] + slope[j]
+                    results.append((k, c, stepped))
+                    squares.append(stepped * stepped)
+                while len(squares) > 1:
+                    squares = [a + b for a, b in zip(squares[::2], squares[1::2])]
+                sums.append((k, squares[0]))
+            for k, c, stepped in results:
+                state_ref[k, :, c] = stepped
+            for k, total in sums:
+                wide_ref[pl.ds(pl.multiple_of(k * SUBLANES, SUBLANES), SUBLANES), g * LANES : (g + 1) * LANES] = total
+            return value
+
+        lax.fori_loop(0, depth // OUTER_BATCH, step, value)
+
+    ones = jnp.ones((SUBLANES, wide_ref.shape[1]), jnp.float32)
     squares = lax.dot_general(
         ones, wide_ref[...], (((1,), (1,)), ((), ())), precision=lax.Precision.HIGHEST,
         preferred_element_type=jnp.float32,
@@ -208,8 +246,9 @@
         def step(i, carry, part=part):
             k = part * SUBLANES + i
             factor = factor_ref[k]
-            for c in cs:
-                jumps_ref[k, :, c] = state_ref[k, :, c] * factor
+            values = [state_ref[k, :, c] * factor for c in cs]
+            for c, value in zip(cs, values):
+                jumps_ref[k, :, c] = value
             return carry
 
         lax.fori_loop(0, SUBLANES, step, 0, unroll=2)
@@ -231,9 +270,10 @@
 
 def call(kernel, name, operands, outs, kept=(), scratch=(), aliases=None, hbm=(), hbm_out=False):
     in_vmem = pl.BlockSpec(memory_space=pltpu.VMEM)
-    in_hbm = pl.BlockSpec(memory_space=pl.ANY)
+    in_hbm = pl.BlockSpec(memory_space=pltpu.HBM)
     operands = [
-        pltpu.with_memory_space_constraint(x, pltpu.VMEM) if i in kept else x for i, x in enumerate(operands)
+        pltpu.with_memory_space_constraint(x, pltpu.VMEM if i in kept else pltpu.HBM) if i in kept or i in hbm else x
+        for i, x in enumerate(operands)
     ]
     return pl.pallas_call(
         kernel,
@@ -253,21 +293,19 @@
     depth = rows // SUBLANES
     count = float(rows * chips * cores)
     alpha, beta = STEP_LENGTH / (count * count), STEP_LENGTH / count
-    chip, core = lax.axis_index("probe"), lax.axis_index("sub")
     offsets = tuple(reversed(range(1, chips)))
     swap = [(0, 1), (1, 0)]
     routes = {
         k: [(z * 2 + c, (z ^ k) * 2 + 1 - c) for z in range(chips) for c in range(2)] for k in offsets
     }
-    limits = thresholds.reshape(SUBLANES, depth).T.reshape(1, rows)
 
     block = vmem(depth, SUBLANES, cols)
     strip, line, pair = vmem(SUBLANES, cols), vmem(1, rows), vmem(2, cols)
     spread = vmem(depth, SUBLANES, LANES)
 
-    state, const, minus, totals, weighted, message = call(
-        functools.partial(begin_kernel, beta, count), "begin", [signal, jump_sizes],
-        [block, block, strip, strip, strip, pair], hbm=(0, 1),
+    state, const, minus, totals, weighted, message, limits, marks = call(
+        functools.partial(begin_kernel, chips, beta, count), "begin", [signal, jump_sizes, thresholds.reshape(1, rows)],
+        [block, block, strip, strip, strip, pair, line, vmem(chips + 1, cols)], hbm=(0, 1),
         scratch=[pltpu.SemaphoreType.DMA((2, depth // SUBLANES, SUBLANES))],
     )
     factor = None
@@ -278,12 +316,11 @@
             )
         sibling = lax.ppermute(message, "sub", swap)
         both = message + sibling
-        lower = jnp.where(core == 0, message[0:1], sibling[0:1])
+        lower = jnp.where(marks[0:1] > 0.0, message[0:1], sibling[0:1])
         upward = both[0:1]
-        later = (chips - 1 - chip).astype(jnp.float32) * (2.0 * rows)
-        downward = both[1:2] + float(rows) * lower + later * upward
+        downward = both[1:2] + float(rows) * lower + marks[1:2] * upward
         received = [
-            lax.ppermute(jnp.where(jnp.bitwise_xor(chip, k) > chip, upward, downward), ("probe", "sub"), routes[k])
+            lax.ppermute(jnp.where(marks[1 + k : 2 + k] > 0.0, upward, downward), ("probe", "sub"), routes[k])
             for k in offsets
         ]
         scaled = factor is not None
@@ -294,7 +331,7 @@
         )
         state, own = call(
             functools.partial(outer_kernel, alpha, chips, offsets), "outer", [inner, slope, base, *received],
-            [block, line], kept=(0, 1, 2), aliases={0: 0}, scratch=[vmem(rows, LANES)],
+            [block, line], kept=(0, 1, 2), aliases={0: 0}, scratch=[vmem(rows, LANES * len(groups(cols, OUTER_WIDTH)))],
         )
         if halves == 2:
             other = lax.ppermute(own, "prof", swap)

time: 172 us -> 115 us (0.67)
  Pallas kernels: 81.9 us -> 33.4 us
  local copies, waits for them, and re-layouts: 17.3 us -> 0.68 us
  waiting for transfers between devices: 25.6 us -> 40 us
  starting transfers between devices: 45.6 us -> 39.7 us
    pallas_call x25, Pallas kernels: 81.9 us -> 33.4 us  [call(): pl.pallas_call(kernel, out_shape=outs, in_specs=[in_hbm if i in hbm else...]
    unnamed x20 -> x2, local copies, waits for them, and re-layouts: 17 us -> 0.68 us
    ppermute x24, waiting for transfers between devices: 0.06 us -> 14.2 us  [local(): lax.ppermute(jnp.where(marks[1 + k:2 + k] > 0.0, upward, downward), ('pro...]
    ppermute x24, starting transfers between devices: 32.6 us -> 26.6 us  [local(): lax.ppermute(jnp.where(marks[1 + k:2 + k] > 0.0, upward, downward), ('pro...]
  transfers between devices with their start and end apart: 40 -> 40, of which waited for: 16 -> 28; matrix products, arithmetic and copies ran while one was open for 0% -> 0% of each run, Pallas kernels for 21% -> 7%
where the time goes in v1:
time: 115 us
  waiting for transfers between devices  40 us (35%)
  starting transfers between devices  39.7 us (35%)
  Pallas kernels  33.4 us (29%)
    pallas_call x25, Pallas kernels, call(): pl.pallas_call(kernel, out_shape=outs, in_specs=[in_hbm if i in hbm else...  33.4 us
    ppermute x24, starting transfers between devices, local(): lax.ppermute(jnp.where(marks[1 + k:2 + k] > 0.0, upward, downward), ('pro...  26.6 us
    ppermute x8, waiting for transfers between devices, local(): other = lax.ppermute(own, 'prof', swap)  16.7 us
    ppermute x24, waiting for transfers between devices, local(): lax.ppermute(jnp.where(marks[1 + k:2 + k] > 0.0, upward, downward), ('pro...  14.2 us
    ppermute x8, starting transfers between devices, local(): other = lax.ppermute(own, 'prof', swap)  12.1 us
    ppermute x8, waiting for transfers between devices, local(): sibling = lax.ppermute(message, 'sub', swap)  9.03 us
  transfers between devices with their start and end apart: 40, of which 28 were waited for; matrix products, arithmetic and copies ran while one was open for 0% of the time, Pallas kernels for 7%

profile of v1, /device:TPU:0, one launch (start us, length us, event | category | flops | bytes accessed | tf_op | source)
XLA Modules:
  0.0 114.7 jit_solution(6828162790218937914)
XLA Ops:
  0.7 4.9 %begin.1 = (f32[64,8,2048]{2,1,0:T(8,128)S(1)}, f32[64,8,2048]{2,1,0:T(8,128)S(1)}, f32[8,2048]{1,0:T(8,128)S(1)}, f32[8,2048]{1,0:T(8,128)S(1)}, f32[8,2048]{1,...) custom-call(f32[512,2048]{1,0:T(8,128)} %signal_hbm.1, f32[512,2048]{1,0:T(8,128)} %jumps_hbm.1, ...), custom_call_target="tpu_custom_call" | custom-call | tf_op jit(solution)/shard_map/begin/pallas_call | solution.py:278
  7.0 3.8 %collective-permute-start.2 = (f32[1,2048]{1,0:T(1,128)S(1)}, f32[1,2048]{1,0:T(1,128)S(1)}, u32[]{:S(2)}, u32[]{:S(2)}) collective-permute-start(f32[1,2048]{1,0:T(1,128)S(1)} %get-tuple-element.187), channel_id=1, source_target_pairs={{0,9},{1,8},{4,13},{5,12},{8,1},{9,0},{12,5},{13,4},{2,11},{3,10},... | collective-permute-start | bytes 24584 | tf_op jit(solution)/shard_map/ppermute | solution.py:323
  13.3 2.4 %collective-permute-done.1.refs_0_ = f32[1,2048]{1,0:T(1,128)S(1)} collective-permute-done((f32[1,2048]{1,0:T(1,128)S(1)}, f32[1,2048]{1,0:T(1,128)S(1)}, u32[]{:S(2)}, u32[]{:S(2)}) %collective-permute-start.1) | collective-permute-done | bytes 8224 | tf_op jit(solution)/shard_map/ppermute | solution.py:323
  18.5 2.1 %collective-permute-done.4.other_ref = f32[1,512]{1,0:T(1,128)S(1)} collective-permute-done((f32[1,512]{1,0:T(1,128)S(1)}, f32[1,512]{1,0:T(1,128)S(1)}, u32[]{:S(2)}, u32[]{:S(2)}) %collective-permute-start.4) | collective-permute-done | bytes 2080 | tf_op jit(solution)/shard_map/ppermute | solution.py:337
  27.1 1.7 %collective-permute-done.6.refs_0_ = f32[1,2048]{1,0:T(1,128)S(1)} collective-permute-done((f32[1,2048]{1,0:T(1,128)S(1)}, f32[1,2048]{1,0:T(1,128)S(1)}, u32[]{:S(2)}, u32[]{:S(2)}) %collective-permute-start.6) | collective-permute-done | bytes 8224 | tf_op jit(solution)/shard_map/ppermute | solution.py:323
  31.6 2.1 %collective-permute-done.9.other_ref = f32[1,512]{1,0:T(1,128)S(1)} collective-permute-done((f32[1,512]{1,0:T(1,128)S(1)}, f32[1,512]{1,0:T(1,128)S(1)}, u32[]{:S(2)}, u32[]{:S(2)}) %collective-permute-start.9) | collective-permute-done | bytes 2080 | tf_op jit(solution)/shard_map/ppermute | solution.py:337
  36.8 1.8 %collective-permute-start.11 = (f32[1,2048]{1,0:T(1,128)S(1)}, f32[1,2048]{1,0:T(1,128)S(1)}, u32[]{:S(2)}, u32[]{:S(2)}) collective-permute-start(f32[1,2048]{1,0:T(1,128)S(1)} %get-tuple-element.184), channel_id=1, source_target_pairs={{0,13},{1,12},{4,9},{5,8},{8,5},{9,4},{12,1},{13,0},{2,15},{3,14},... | collective-permute-start | bytes 24584 | tf_op jit(solution)/shard_map/ppermute | solution.py:323
  40.2 1.5 %collective-permute-done.11.refs_0_ = f32[1,2048]{1,0:T(1,128)S(1)} collective-permute-done((f32[1,2048]{1,0:T(1,128)S(1)}, f32[1,2048]{1,0:T(1,128)S(1)}, u32[]{:S(2)}, u32[]{:S(2)}) %collective-permute-start.11) | collective-permute-done | bytes 8224 | tf_op jit(solution)/shard_map/ppermute | solution.py:323
  44.6 2.1 %collective-permute-done.14.other_ref = f32[1,512]{1,0:T(1,128)S(1)} collective-permute-done((f32[1,512]{1,0:T(1,128)S(1)}, f32[1,512]{1,0:T(1,128)S(1)}, u32[]{:S(2)}, u32[]{:S(2)}) %collective-permute-start.14) | collective-permute-done | bytes 2080 | tf_op jit(solution)/shard_map/ppermute | solution.py:337
  49.9 1.8 %collective-permute-start.16 = (f32[1,2048]{1,0:T(1,128)S(1)}, f32[1,2048]{1,0:T(1,128)S(1)}, u32[]{:S(2)}, u32[]{:S(2)}) collective-permute-start(f32[1,2048]{1,0:T(1,128)S(1)} %get-tuple-element.182), channel_id=1, source_target_pairs={{0,13},{1,12},{4,9},{5,8},{8,5},{9,4},{12,1},{13,0},{2,15},{3,14},... | collective-permute-start | bytes 24584 | tf_op jit(solution)/shard_map/ppermute | solution.py:323
  53.2 1.7 %collective-permute-done.16.refs_0_ = f32[1,2048]{1,0:T(1,128)S(1)} collective-permute-done((f32[1,2048]{1,0:T(1,128)S(1)}, f32[1,2048]{1,0:T(1,128)S(1)}, u32[]{:S(2)}, u32[]{:S(2)}) %collective-permute-start.16) | collective-permute-done | bytes 8224 | tf_op jit(solution)/shard_map/ppermute | solution.py:323
  57.7 2.1 %collective-permute-done.19.other_ref = f32[1,512]{1,0:T(1,128)S(1)} collective-permute-done((f32[1,512]{1,0:T(1,128)S(1)}, f32[1,512]{1,0:T(1,128)S(1)}, u32[]{:S(2)}, u32[]{:S(2)}) %collective-permute-start.19) | collective-permute-done | bytes 2080 | tf_op jit(solution)/shard_map/ppermute | solution.py:337
  62.8 1.9 %collective-permute-start.21 = (f32[1,2048]{1,0:T(1,128)S(1)}, f32[1,2048]{1,0:T(1,128)S(1)}, u32[]{:S(2)}, u32[]{:S(2)}) collective-permute-start(f32[1,2048]{1,0:T(1,128)S(1)} %get-tuple-element.180), channel_id=1, source_target_pairs={{0,13},{1,12},{4,9},{5,8},{8,5},{9,4},{12,1},{13,0},{2,15},{3,14},... | collective-permute-start | bytes 24584 | tf_op jit(solution)/shard_map/ppermute | solution.py:323
  70.6 2.1 %collective-permute-done.24.other_ref = f32[1,512]{1,0:T(1,128)S(1)} collective-permute-done((f32[1,512]{1,0:T(1,128)S(1)}, f32[1,512]{1,0:T(1,128)S(1)}, u32[]{:S(2)}, u32[]{:S(2)}) %collective-permute-start.24) | collective-permute-done | bytes 2080 | tf_op jit(solution)/shard_map/ppermute | solution.py:337
  76.0 1.9 %collective-permute-start.26 = (f32[1,2048]{1,0:T(1,128)S(1)}, f32[1,2048]{1,0:T(1,128)S(1)}, u32[]{:S(2)}, u32[]{:S(2)}) collective-permute-start(f32[1,2048]{1,0:T(1,128)S(1)} %get-tuple-element.178), channel_id=1, source_target_pairs={{0,13},{1,12},{4,9},{5,8},{8,5},{9,4},{12,1},{13,0},{2,15},{3,14},... | collective-permute-start | bytes 24584 | tf_op jit(solution)/shard_map/ppermute | solution.py:323
  79.2 1.6 %collective-permute-done.26.refs_0_ = f32[1,2048]{1,0:T(1,128)S(1)} collective-permute-done((f32[1,2048]{1,0:T(1,128)S(1)}, f32[1,2048]{1,0:T(1,128)S(1)}, u32[]{:S(2)}, u32[]{:S(2)}) %collective-permute-start.26) | collective-permute-done | bytes 8224 | tf_op jit(solution)/shard_map/ppermute | solution.py:323
  83.7 2.1 %collective-permute-done.29.other_ref = f32[1,512]{1,0:T(1,128)S(1)} collective-permute-done((f32[1,512]{1,0:T(1,128)S(1)}, f32[1,512]{1,0:T(1,128)S(1)}, u32[]{:S(2)}, u32[]{:S(2)}) %collective-permute-start.29) | collective-permute-done | bytes 2080 | tf_op jit(solution)/shard_map/ppermute | solution.py:337
  89.0 1.8 %collective-permute-start.31 = (f32[1,2048]{1,0:T(1,128)S(1)}, f32[1,2048]{1,0:T(1,128)S(1)}, u32[]{:S(2)}, u32[]{:S(2)}) collective-permute-start(f32[1,2048]{1,0:T(1,128)S(1)} %get-tuple-element.176), channel_id=1, source_target_pairs={{0,13},{1,12},{4,9},{5,8},{8,5},{9,4},{12,1},{13,0},{2,15},{3,14},... | collective-permute-start | bytes 24584 | tf_op jit(solution)/shard_map/ppermute | solution.py:323
  92.3 1.6 %collective-permute-done.31.refs_0_ = f32[1,2048]{1,0:T(1,128)S(1)} collective-permute-done((f32[1,2048]{1,0:T(1,128)S(1)}, f32[1,2048]{1,0:T(1,128)S(1)}, u32[]{:S(2)}, u32[]{:S(2)}) %collective-permute-start.31) | collective-permute-done | bytes 8224 | tf_op jit(solution)/shard_map/ppermute | solution.py:323
  96.8 2.1 %collective-permute-done.34.other_ref = f32[1,512]{1,0:T(1,128)S(1)} collective-permute-done((f32[1,512]{1,0:T(1,128)S(1)}, f32[1,512]{1,0:T(1,128)S(1)}, u32[]{:S(2)}, u32[]{:S(2)}) %collective-permute-start.34) | collective-permute-done | bytes 2080 | tf_op jit(solution)/shard_map/ppermute | solution.py:337
  102.1 1.8 %collective-permute-start.36 = (f32[1,2048]{1,0:T(1,128)S(1)}, f32[1,2048]{1,0:T(1,128)S(1)}, u32[]{:S(2)}, u32[]{:S(2)}) collective-permute-start(f32[1,2048]{1,0:T(1,128)S(1)} %get-tuple-element.174), channel_id=1, source_target_pairs={{0,13},{1,12},{4,9},{5,8},{8,5},{9,4},{12,1},{13,0},{2,15},{3,14},... | collective-permute-start | bytes 24584 | tf_op jit(solution)/shard_map/ppermute | solution.py:323
  105.3 1.7 %collective-permute-done.36.refs_0_ = f32[1,2048]{1,0:T(1,128)S(1)} collective-permute-done((f32[1,2048]{1,0:T(1,128)S(1)}, f32[1,2048]{1,0:T(1,128)S(1)}, u32[]{:S(2)}, u32[]{:S(2)}) %collective-permute-start.36) | collective-permute-done | bytes 8224 | tf_op jit(solution)/shard_map/ppermute | solution.py:323
  109.9 2.1 %collective-permute-done.39.other_ref = f32[1,512]{1,0:T(1,128)S(1)} collective-permute-done((f32[1,512]{1,0:T(1,128)S(1)}, f32[1,512]{1,0:T(1,128)S(1)}, u32[]{:S(2)}, u32[]{:S(2)}) %collective-permute-start.39) | collective-permute-done | bytes 2080 | tf_op jit(solution)/shard_map/ppermute | solution.py:337
  112.0 2.7 %finish.1 = f32[512,2048]{1,0:T(8,128)} custom-call(f32[1,512]{1,0:T(1,128)S(1)} %get-tuple-element.155.own_ref, f32[1,512]{1,0:T(1,128)S(1)} %collective-permute-done.39.other_ref, f32[1,512]{1,0:T(1,128)S(1)} %get-tuple-element.93.limits_ref, f32[64,8,2048]{2,1,0:T(8,128)S(1)} %get-tuple-element.156.state_ref), custom_call_target="tpu_custom_call" | custom-call | tf_op jit(solution)/shard_map/finish/pallas_call | solution.py:278
  (107 shorter events, 62.8 us)
Async XLA Ops:
  7.0 6.2 %collective-permute-start.2 = (f32[1,2048]{1,0:T(1,128)S(1)}, f32[1,2048]{1,0:T(1,128)S(1)}, u32[]{:S(2)}, u32[]{:S(2)}) collective-permute-start(f32[1,2048]{1,0:T(1,128)S(1)} %get-tuple-element.187), channel_id=1, source_target_pairs={{0,9},{1,8},{4,13},{5,12},{8,1},{9,0},{12,5},{13,4},{2,11},{3,10},... | collective-permute-start | bytes 24584 | tf_op jit(solution)/shard_map/ppermute | solution.py:323
  10.8 4.9 %collective-permute-start.1 = (f32[1,2048]{1,0:T(1,128)S(1)}, f32[1,2048]{1,0:T(1,128)S(1)}, u32[]{:S(2)}, u32[]{:S(2)}) collective-permute-start(f32[1,2048]{1,0:T(1,128)S(1)} %get-tuple-element.188), channel_id=1, source_target_pairs={{0,13},{1,12},{4,9},{5,8},{8,5},{9,4},{12,1},{13,0},{2,15},{3,14},... | collective-permute-start | bytes 24584 | tf_op jit(solution)/shard_map/ppermute | solution.py:323
  17.0 3.6 %collective-permute-start.4 = (f32[1,512]{1,0:T(1,128)S(1)}, f32[1,512]{1,0:T(1,128)S(1)}, u32[]{:S(2)}, u32[]{:S(2)}) collective-permute-start(f32[1,512]{1,0:T(1,128)S(1)} %get-tuple-element.92.own_ref), channel_id=1, source_target_pairs={{0,2},{2,0},{1,3},{3,1},{4,6},{6,4},{5,7},{7,5},{8,10},{10,8},{9,1... | collective-permute-start | bytes 6152 | tf_op jit(solution)/shard_map/ppermute | solution.py:337
  22.9 4.1 %collective-permute-start.7 = (f32[1,2048]{1,0:T(1,128)S(1)}, f32[1,2048]{1,0:T(1,128)S(1)}, u32[]{:S(2)}, u32[]{:S(2)}) collective-permute-start(f32[1,2048]{1,0:T(1,128)S(1)} %get-tuple-element.185), channel_id=1, source_target_pairs={{0,9},{1,8},{4,13},{5,12},{8,1},{9,0},{12,5},{13,4},{2,11},{3,10},... | collective-permute-start | bytes 24584 | tf_op jit(solution)/shard_map/ppermute | solution.py:323
  23.9 4.9 %collective-permute-start.6 = (f32[1,2048]{1,0:T(1,128)S(1)}, f32[1,2048]{1,0:T(1,128)S(1)}, u32[]{:S(2)}, u32[]{:S(2)}) collective-permute-start(f32[1,2048]{1,0:T(1,128)S(1)} %get-tuple-element.186), channel_id=1, source_target_pairs={{0,13},{1,12},{4,9},{5,8},{8,5},{9,4},{12,1},{13,0},{2,15},{3,14},... | collective-permute-start | bytes 24584 | tf_op jit(solution)/shard_map/ppermute | solution.py:323
  24.8 4.0 %collective-permute-start.8 = (f32[1,2048]{1,0:T(1,128)S(1)}, f32[1,2048]{1,0:T(1,128)S(1)}, u32[]{:S(2)}, u32[]{:S(2)}) collective-permute-start(f32[1,2048]{1,0:T(1,128)S(1)} %get-tuple-element.169), channel_id=1, source_target_pairs={{0,5},{1,4},{4,1},{5,0},{8,13},{9,12},{12,9},{13,8},{2,7},{3,6},{6... | collective-permute-start | bytes 24584 | tf_op jit(solution)/shard_map/ppermute | solution.py:323
  30.1 3.6 %collective-permute-start.9 = (f32[1,512]{1,0:T(1,128)S(1)}, f32[1,512]{1,0:T(1,128)S(1)}, u32[]{:S(2)}, u32[]{:S(2)}) collective-permute-start(f32[1,512]{1,0:T(1,128)S(1)} %get-tuple-element.102.own_ref), channel_id=1, source_target_pairs={{0,2},{2,0},{1,3},{3,1},{4,6},{6,4},{5,7},{7,5},{8,10},{10,8},{9,1... | collective-permute-start | bytes 6152 | tf_op jit(solution)/shard_map/ppermute | solution.py:337
  36.0 4.1 %collective-permute-start.12 = (f32[1,2048]{1,0:T(1,128)S(1)}, f32[1,2048]{1,0:T(1,128)S(1)}, u32[]{:S(2)}, u32[]{:S(2)}) collective-permute-start(f32[1,2048]{1,0:T(1,128)S(1)} %get-tuple-element.183), channel_id=1, source_target_pairs={{0,9},{1,8},{4,13},{5,12},{8,1},{9,0},{12,5},{13,4},{2,11},{3,10},... | collective-permute-start | bytes 24584 | tf_op jit(solution)/shard_map/ppermute | solution.py:323
  36.8 4.9 %collective-permute-start.11 = (f32[1,2048]{1,0:T(1,128)S(1)}, f32[1,2048]{1,0:T(1,128)S(1)}, u32[]{:S(2)}, u32[]{:S(2)}) collective-permute-start(f32[1,2048]{1,0:T(1,128)S(1)} %get-tuple-element.184), channel_id=1, source_target_pairs={{0,13},{1,12},{4,9},{5,8},{8,5},{9,4},{12,1},{13,0},{2,15},{3,14},... | collective-permute-start | bytes 24584 | tf_op jit(solution)/shard_map/ppermute | solution.py:323
  43.1 3.6 %collective-permute-start.14 = (f32[1,512]{1,0:T(1,128)S(1)}, f32[1,512]{1,0:T(1,128)S(1)}, u32[]{:S(2)}, u32[]{:S(2)}) collective-permute-start(f32[1,512]{1,0:T(1,128)S(1)} %get-tuple-element.111.own_ref), channel_id=1, source_target_pairs={{0,2},{2,0},{1,3},{3,1},{4,6},{6,4},{5,7},{7,5},{8,10},{10,8},{9,1... | collective-permute-start | bytes 6152 | tf_op jit(solution)/shard_map/ppermute | solution.py:337
  49.0 4.1 %collective-permute-start.17 = (f32[1,2048]{1,0:T(1,128)S(1)}, f32[1,2048]{1,0:T(1,128)S(1)}, u32[]{:S(2)}, u32[]{:S(2)}) collective-permute-start(f32[1,2048]{1,0:T(1,128)S(1)} %get-tuple-element.181), channel_id=1, source_target_pairs={{0,9},{1,8},{4,13},{5,12},{8,1},{9,0},{12,5},{13,4},{2,11},{3,10},... | collective-permute-start | bytes 24584 | tf_op jit(solution)/shard_map/ppermute | solution.py:323
  49.9 4.9 %collective-permute-start.16 = (f32[1,2048]{1,0:T(1,128)S(1)}, f32[1,2048]{1,0:T(1,128)S(1)}, u32[]{:S(2)}, u32[]{:S(2)}) collective-permute-start(f32[1,2048]{1,0:T(1,128)S(1)} %get-tuple-element.182), channel_id=1, source_target_pairs={{0,13},{1,12},{4,9},{5,8},{8,5},{9,4},{12,1},{13,0},{2,15},{3,14},... | collective-permute-start | bytes 24584 | tf_op jit(solution)/shard_map/ppermute | solution.py:323
  56.2 3.6 %collective-permute-start.19 = (f32[1,512]{1,0:T(1,128)S(1)}, f32[1,512]{1,0:T(1,128)S(1)}, u32[]{:S(2)}, u32[]{:S(2)}) collective-permute-start(f32[1,512]{1,0:T(1,128)S(1)} %get-tuple-element.120.own_ref), channel_id=1, source_target_pairs={{0,2},{2,0},{1,3},{3,1},{4,6},{6,4},{5,7},{7,5},{8,10},{10,8},{9,1... | collective-permute-start | bytes 6152 | tf_op jit(solution)/shard_map/ppermute | solution.py:337
  62.1 4.1 %collective-permute-start.22 = (f32[1,2048]{1,0:T(1,128)S(1)}, f32[1,2048]{1,0:T(1,128)S(1)}, u32[]{:S(2)}, u32[]{:S(2)}) collective-permute-start(f32[1,2048]{1,0:T(1,128)S(1)} %get-tuple-element.179), channel_id=1, source_target_pairs={{0,9},{1,8},{4,13},{5,12},{8,1},{9,0},{12,5},{13,4},{2,11},{3,10},... | collective-permute-start | bytes 24584 | tf_op jit(solution)/shard_map/ppermute | solution.py:323
  62.8 4.9 %collective-permute-start.21 = (f32[1,2048]{1,0:T(1,128)S(1)}, f32[1,2048]{1,0:T(1,128)S(1)}, u32[]{:S(2)}, u32[]{:S(2)}) collective-permute-start(f32[1,2048]{1,0:T(1,128)S(1)} %get-tuple-element.180), channel_id=1, source_target_pairs={{0,13},{1,12},{4,9},{5,8},{8,5},{9,4},{12,1},{13,0},{2,15},{3,14},... | collective-permute-start | bytes 24584 | tf_op jit(solution)/shard_map/ppermute | solution.py:323
  69.1 3.6 %collective-permute-start.24 = (f32[1,512]{1,0:T(1,128)S(1)}, f32[1,512]{1,0:T(1,128)S(1)}, u32[]{:S(2)}, u32[]{:S(2)}) collective-permute-start(f32[1,512]{1,0:T(1,128)S(1)} %get-tuple-element.129.own_ref), channel_id=1, source_target_pairs={{0,2},{2,0},{1,3},{3,1},{4,6},{6,4},{5,7},{7,5},{8,10},{10,8},{9,1... | collective-permute-start | bytes 6152 | tf_op jit(solution)/shard_map/ppermute | solution.py:337
  75.1 4.1 %collective-permute-start.27 = (f32[1,2048]{1,0:T(1,128)S(1)}, f32[1,2048]{1,0:T(1,128)S(1)}, u32[]{:S(2)}, u32[]{:S(2)}) collective-permute-start(f32[1,2048]{1,0:T(1,128)S(1)} %get-tuple-element.177), channel_id=1, source_target_pairs={{0,9},{1,8},{4,13},{5,12},{8,1},{9,0},{12,5},{13,4},{2,11},{3,10},... | collective-permute-start | bytes 24584 | tf_op jit(solution)/shard_map/ppermute | solution.py:323
  76.0 4.9 %collective-permute-start.26 = (f32[1,2048]{1,0:T(1,128)S(1)}, f32[1,2048]{1,0:T(1,128)S(1)}, u32[]{:S(2)}, u32[]{:S(2)}) collective-permute-start(f32[1,2048]{1,0:T(1,128)S(1)} %get-tuple-element.178), channel_id=1, source_target_pairs={{0,13},{1,12},{4,9},{5,8},{8,5},{9,4},{12,1},{13,0},{2,15},{3,14},... | collective-permute-start | bytes 24584 | tf_op jit(solution)/shard_map/ppermute | solution.py:323
  82.2 3.6 %collective-permute-start.29 = (f32[1,512]{1,0:T(1,128)S(1)}, f32[1,512]{1,0:T(1,128)S(1)}, u32[]{:S(2)}, u32[]{:S(2)}) collective-permute-start(f32[1,512]{1,0:T(1,128)S(1)} %get-tuple-element.138.own_ref), channel_id=1, source_target_pairs={{0,2},{2,0},{1,3},{3,1},{4,6},{6,4},{5,7},{7,5},{8,10},{10,8},{9,1... | collective-permute-start | bytes 6152 | tf_op jit(solution)/shard_map/ppermute | solution.py:337
  88.2 4.1 %collective-permute-start.32 = (f32[1,2048]{1,0:T(1,128)S(1)}, f32[1,2048]{1,0:T(1,128)S(1)}, u32[]{:S(2)}, u32[]{:S(2)}) collective-permute-start(f32[1,2048]{1,0:T(1,128)S(1)} %get-tuple-element.175), channel_id=1, source_target_pairs={{0,9},{1,8},{4,13},{5,12},{8,1},{9,0},{12,5},{13,4},{2,11},{3,10},... | collective-permute-start | bytes 24584 | tf_op jit(solution)/shard_map/ppermute | solution.py:323
  89.0 5.0 %collective-permute-start.31 = (f32[1,2048]{1,0:T(1,128)S(1)}, f32[1,2048]{1,0:T(1,128)S(1)}, u32[]{:S(2)}, u32[]{:S(2)}) collective-permute-start(f32[1,2048]{1,0:T(1,128)S(1)} %get-tuple-element.176), channel_id=1, source_target_pairs={{0,13},{1,12},{4,9},{5,8},{8,5},{9,4},{12,1},{13,0},{2,15},{3,14},... | collective-permute-start | bytes 24584 | tf_op jit(solution)/shard_map/ppermute | solution.py:323
  95.2 3.6 %collective-permute-start.34 = (f32[1,512]{1,0:T(1,128)S(1)}, f32[1,512]{1,0:T(1,128)S(1)}, u32[]{:S(2)}, u32[]{:S(2)}) collective-permute-start(f32[1,512]{1,0:T(1,128)S(1)} %get-tuple-element.147.own_ref), channel_id=1, source_target_pairs={{0,2},{2,0},{1,3},{3,1},{4,6},{6,4},{5,7},{7,5},{8,10},{10,8},{9,1... | collective-permute-start | bytes 6152 | tf_op jit(solution)/shard_map/ppermute | solution.py:337
  101.2 4.1 %collective-permute-start.37 = (f32[1,2048]{1,0:T(1,128)S(1)}, f32[1,2048]{1,0:T(1,128)S(1)}, u32[]{:S(2)}, u32[]{:S(2)}) collective-permute-start(f32[1,2048]{1,0:T(1,128)S(1)} %get-tuple-element.173), channel_id=1, source_target_pairs={{0,9},{1,8},{4,13},{5,12},{8,1},{9,0},{12,5},{13,4},{2,11},{3,10},... | collective-permute-start | bytes 24584 | tf_op jit(solution)/shard_map/ppermute | solution.py:323
  102.1 5.0 %collective-permute-start.36 = (f32[1,2048]{1,0:T(1,128)S(1)}, f32[1,2048]{1,0:T(1,128)S(1)}, u32[]{:S(2)}, u32[]{:S(2)}) collective-permute-start(f32[1,2048]{1,0:T(1,128)S(1)} %get-tuple-element.174), channel_id=1, source_target_pairs={{0,13},{1,12},{4,9},{5,8},{8,5},{9,4},{12,1},{13,0},{2,15},{3,14},... | collective-permute-start | bytes 24584 | tf_op jit(solution)/shard_map/ppermute | solution.py:323
  (17 other events, 36.8 us)

commit v2 on v1

--- a/solution.py
+++ b/solution.py
@@ -12,8 +12,7 @@
 LANES = 128
 SUBLANES = 8
 VMEM_LIMIT = 16 * 1024 * 1024
-WIDTH, BATCH = 8, 4
-OUTER_WIDTH, OUTER_BATCH = 8, 4
+WIDTH, BATCH, SUM_BATCH = 8, 4, 8
 
 
 def tiles(cols):
@@ -38,33 +37,26 @@
         message_ref[1:2, c] = jnp.sum(weights * total[j] + weighted[j], axis=0, keepdims=True)
 
 
-def begin_kernel(chips, beta, count, signal_hbm, jumps_hbm, thresholds_ref, state_ref, const_ref, minus_ref, totals_ref,
-                 weighted_ref, message_ref, limits_ref, marks_ref, sems):
+def begin_kernel(chips, count, cuts, signal_hbm, jumps_hbm, thresholds_hbm, state_ref, signal_ref, minus_ref, totals_ref,
+                 weighted_ref, message_ref, limits_ref, marks_ref, thresholds_ref, sems, limits_sem):
     depth, _, cols = state_ref.shape
-    cs = tiles(cols)
-    parts = depth // SUBLANES
+    rows = depth * SUBLANES
 
     def copies(part):
-        for a, (src, dst) in enumerate(((signal_hbm, const_ref), (jumps_hbm, state_ref))):
+        low, high = cuts[part], cuts[part + 1]
+        for a, (src, dst) in enumerate(((jumps_hbm, state_ref), (signal_hbm, signal_ref))):
             for s in range(SUBLANES):
                 yield pltpu.make_async_copy(
-                    src.at[pl.ds(s * depth + part * SUBLANES, SUBLANES), :],
-                    dst.at[pl.ds(part * SUBLANES, SUBLANES), s, :],
-                    sems.at[a, part, s],
+                    src.at[pl.ds(s * depth + low, high - low), :], dst.at[pl.ds(low, high - low), s, :],
+                    sems.at[part, a, s],
                 )
 
-    for part in reversed(range(parts)):
+    limits_copy = pltpu.make_async_copy(thresholds_hbm, thresholds_ref, limits_sem)
+    limits_copy.start()
+    for part in range(len(cuts) - 1):
         for copy in copies(part):
             copy.start()
 
-    rows = depth * SUBLANES
-    source = lax.broadcasted_iota(jnp.int32, (rows, rows), 0)
-    target = lax.broadcasted_iota(jnp.int32, (rows, rows), 1)
-    chosen = jnp.where(source == (target % SUBLANES) * depth + target // SUBLANES, 1.0, 0.0)
-    limits_ref[...] = lax.dot_general(
-        jnp.broadcast_to(thresholds_ref[...], (SUBLANES, rows)), chosen, (((1,), (0,)), ((), ())),
-        precision=lax.Precision.HIGHEST, preferred_element_type=jnp.float32,
-    )[0:1, :]
     chip, core = lax.axis_index("probe"), lax.axis_index("sub")
     later = (chips - 1 - chip).astype(jnp.float32) * (2.0 * rows)
     marks = [(core == 0).astype(jnp.float32), later]
@@ -72,58 +64,98 @@
     for i, mark in enumerate(marks):
         marks_ref[i : i + 1, :] = jnp.full((1, cols), mark, jnp.float32)
 
+    limits_copy.wait()
+    sublane = lax.broadcasted_iota(jnp.int32, (SUBLANES, LANES), 0)
+    lane = lax.broadcasted_iota(jnp.int32, (SUBLANES, LANES), 1)
+    limits = jnp.zeros((SUBLANES, LANES), jnp.float32)
+    for s in range(SUBLANES):
+        tile, offset = divmod(s * depth, LANES)
+        line = jnp.broadcast_to(thresholds_ref[0:1, tile * LANES : (tile + 1) * LANES], (SUBLANES, LANES))
+        for copy in range(LANES // depth):
+            shift = (copy * depth - offset) % LANES
+            moved = pltpu.roll(line, shift, 1) if shift else line
+            limits = jnp.where((sublane == s) & (lane // depth == copy), moved, limits)
+    limits_ref[...] = limits
+
     zero = jnp.zeros((SUBLANES, LANES), jnp.float32)
-    carry = ([zero] * len(cs), [zero] * len(cs), [zero] * len(cs))
-    for part in reversed(range(parts)):
+    grouped = groups(cols, WIDTH)
+    carries = [([zero] * len(group), [zero] * len(group), [zero] * len(group)) for group in grouped]
+    for part in range(len(cuts) - 1):
         for copy in copies(part):
             copy.wait()
-
-        def step(i, carry, part=part):
-            suffix, total, weighted = (list(x) for x in carry)
-            k = part * SUBLANES + SUBLANES - 1 - i
-            weight = (depth - k).astype(jnp.float32)
-            for j, c in enumerate(cs):
-                jump = state_ref[k, :, c]
-                total[j] = total[j] + jump
-                weighted[j] = weighted[j] + jump * weight
-                suffix[j] = suffix[j] + const_ref[k, :, c]
-            for j, c in enumerate(cs):
-                const_ref[k, :, c] = suffix[j] * beta
-            return suffix, total, weighted
-
-        carry = lax.fori_loop(0, SUBLANES, step, carry)
-    suffix, total, weighted = carry
-    for j, c in enumerate(cs):
-        minus = suffix[j] * -count
-        minus_ref[:, c] = minus
-        weighted[j] = weighted[j] + minus
+        for g, group in enumerate(grouped):
+
+            def step(i, carry, group=group, low=cuts[part]):
+                total, weighted, signals = (list(x) for x in carry)
+                for q in range(BATCH):
+                    k = low + i * BATCH + q
+                    for j, c in enumerate(group):
+                        total[j] = total[j] + state_ref[k, :, c]
+                        weighted[j] = weighted[j] + total[j]
+                        signals[j] = signals[j] + signal_ref[k, :, c]
+                return total, weighted, signals
+
+            carries[g] = lax.fori_loop(0, (cuts[part + 1] - cuts[part]) // BATCH, step, carries[g])
+    total, weighted = [], []
+    for group, carry in zip(grouped, carries):
+        for c, t, w, x in zip(group, *carry):
+            minus = x * -count
+            minus_ref[:, c] = minus
+            total.append(t)
+            weighted.append(w + minus)
     finish_sums(depth, total, weighted, totals_ref, weighted_ref, message_ref, cols)
+
+
+def suffix_kernel(beta, signal_ref, const_ref):
+    depth, _, cols = signal_ref.shape
+    zero = jnp.zeros((SUBLANES, LANES), jnp.float32)
+    for group in groups(cols, WIDTH):
+
+        def step(i, suffix, group=group):
+            suffix = list(suffix)
+            start = depth - (i + 1) * BATCH
+            results = []
+            for k in reversed([start + q for q in range(BATCH)]):
+                for j, c in enumerate(group):
+                    suffix[j] = suffix[j] + signal_ref[k, :, c]
+                    results.append((k, c, suffix[j] * beta))
+            for k, c, value in results:
+                const_ref[k, :, c] = value
+            return suffix
+
+        lax.fori_loop(0, depth // BATCH, step, [zero] * len(group))
 
 
 def shrink(own_ref, other_ref, limits_ref, factor_ref):
     squares = own_ref[...] + other_ref[...]
     factor = jnp.maximum(0.0, 1.0 - limits_ref[...] / jnp.sqrt(squares + 1e-06))
-    rows = factor.shape[1]
-    spread = jnp.broadcast_to(factor, (LANES, rows)).T
-    factor_ref[...] = spread.reshape(factor_ref.shape)
+    for k in range(factor_ref.shape[0]):
+        factor_ref[k] = jnp.broadcast_to(factor[:, k : k + 1], (SUBLANES, LANES))
 
 
 def sums_kernel(own_ref, other_ref, limits_ref, state_ref, minus_ref, factor_ref, totals_ref, weighted_ref, message_ref):
     depth, _, cols = state_ref.shape
-    cs = tiles(cols)
     shrink(own_ref, other_ref, limits_ref, factor_ref)
-
-    def step(k, carry):
-        total, weighted = (list(x) for x in carry)
-        factor = factor_ref[k]
-        for j, c in enumerate(cs):
-            total[j] = total[j] + state_ref[k, :, c] * factor
-            weighted[j] = weighted[j] + total[j]
-        return total, weighted
-
     zero = jnp.zeros((SUBLANES, LANES), jnp.float32)
-    total, weighted = lax.fori_loop(0, depth, step, ([zero] * len(cs), [minus_ref[:, c] for c in cs]), unroll=2)
-    finish_sums(depth, total, weighted, totals_ref, weighted_ref, message_ref, cols)
+    totals, weights = [], []
+    for group in groups(cols, WIDTH):
+
+        def step(i, carry, group=group):
+            total, weighted = (list(x) for x in carry)
+            for q in range(SUM_BATCH):
+                k = i * SUM_BATCH + q
+                factor = factor_ref[k]
+                for j, c in enumerate(group):
+                    total[j] = total[j] + state_ref[k, :, c] * factor
+                    weighted[j] = weighted[j] + total[j]
+            return total, weighted
+
+        total, weighted = lax.fori_loop(
+            0, depth // SUM_BATCH, step, ([zero] * len(group), [minus_ref[:, c] for c in group])
+        )
+        totals += total
+        weights += weighted
+    finish_sums(depth, totals, weights, totals_ref, weighted_ref, message_ref, cols)
 
 
 def prefix_rows(x, sublane):
@@ -197,7 +229,8 @@
     weights = row_weights() * float(depth) + later
     earlier = [(jnp.bitwise_xor(chip, k) < chip).astype(jnp.float32) for k in offsets]
 
-    for g, group in enumerate(groups(cols, OUTER_WIDTH)):
+    grouped = groups(cols, WIDTH)
+    for g, group in enumerate(grouped):
         slope, value = [], []
         for c in group:
             above = sum(e * ref[:, c] for e, ref in zip(earlier, received))
@@ -208,9 +241,9 @@
 
         def step(i, value, g=g, group=group, slope=slope):
             value = list(value)
-            start = depth - (i + 1) * OUTER_BATCH
+            start = depth - (i + 1) * BATCH
             results, sums = [], []
-            for k in reversed([start + q for q in range(OUTER_BATCH)]):
+            for k in reversed([start + q for q in range(BATCH)]):
                 squares = []
                 for j, c in enumerate(group):
                     stepped = inner_ref[k, :, c] - value[j]
@@ -223,39 +256,43 @@
             for k, c, stepped in results:
                 state_ref[k, :, c] = stepped
             for k, total in sums:
-                wide_ref[pl.ds(pl.multiple_of(k * SUBLANES, SUBLANES), SUBLANES), g * LANES : (g + 1) * LANES] = total
+                wide_ref[g, k] = total
             return value
 
-        lax.fori_loop(0, depth // OUTER_BATCH, step, value)
-
-    ones = jnp.ones((SUBLANES, wide_ref.shape[1]), jnp.float32)
-    squares = lax.dot_general(
-        ones, wide_ref[...], (((1,), (1,)), ((), ())), precision=lax.Precision.HIGHEST,
-        preferred_element_type=jnp.float32,
-    )
-    squares_ref[...] = squares[0:1, :]
-
-
-def end_kernel(own_ref, other_ref, limits_ref, state_ref, out_hbm, factor_ref, jumps_ref, sems):
+        lax.fori_loop(0, depth // BATCH, step, value, unroll=2)
+    lane = lax.broadcasted_iota(jnp.int32, (SUBLANES, LANES), 1)
+    parts = []
+    for low in range(0, depth, SUBLANES):
+        part = jnp.zeros((SUBLANES, LANES), jnp.float32)
+        for k in range(low, low + SUBLANES):
+            total = jnp.sum(sum(wide_ref[g, k] for g in range(len(grouped))), axis=1, keepdims=True)
+            part = jnp.where(lane % depth == k, jnp.broadcast_to(total, part.shape), part)
+        parts.append(part)
+    squares_ref[...] = sum(parts)
+
+
+def end_kernel(cuts, own_ref, other_ref, limits_ref, state_ref, out_hbm, factor_ref, jumps_ref, sems):
     depth, _, cols = state_ref.shape
-    cs = tiles(cols)
     shrink(own_ref, other_ref, limits_ref, factor_ref)
     copies = []
-    for part in range(depth // SUBLANES):
-
-        def step(i, carry, part=part):
-            k = part * SUBLANES + i
-            factor = factor_ref[k]
-            values = [state_ref[k, :, c] * factor for c in cs]
-            for c, value in zip(cs, values):
-                jumps_ref[k, :, c] = value
-            return carry
-
-        lax.fori_loop(0, SUBLANES, step, 0, unroll=2)
+    for part in range(len(cuts) - 1):
+        low, high = cuts[part], cuts[part + 1]
+        for group in groups(cols, WIDTH):
+
+            def step(i, carry, low=low, group=group):
+                results = []
+                for q in range(BATCH):
+                    k = low + i * BATCH + q
+                    factor = factor_ref[k]
+                    results += [(k, c, state_ref[k, :, c] * factor) for c in group]
+                for k, c, value in results:
+                    jumps_ref[k, :, c] = value
+                return carry
+
+            lax.fori_loop(0, (high - low) // BATCH, step, 0)
         for s in range(SUBLANES):
             copy = pltpu.make_async_copy(
-                jumps_ref.at[pl.ds(part * SUBLANES, SUBLANES), s, :],
-                out_hbm.at[pl.ds(s * depth + part * SUBLANES, SUBLANES), :],
+                jumps_ref.at[pl.ds(low, high - low), s, :], out_hbm.at[pl.ds(s * depth + low, high - low), :],
                 sems.at[part, s],
             )
             copy.start()
@@ -300,14 +337,20 @@
     }
 
     block = vmem(depth, SUBLANES, cols)
-    strip, line, pair = vmem(SUBLANES, cols), vmem(1, rows), vmem(2, cols)
+    strip, line, pair = vmem(SUBLANES, cols), vmem(SUBLANES, LANES), vmem(2, cols)
     spread = vmem(depth, SUBLANES, LANES)
-
-    state, const, minus, totals, weighted, message, limits, marks = call(
-        functools.partial(begin_kernel, chips, beta, count), "begin", [signal, jump_sizes, thresholds.reshape(1, rows)],
-        [block, block, strip, strip, strip, pair, line, vmem(chips + 1, cols)], hbm=(0, 1),
-        scratch=[pltpu.SemaphoreType.DMA((2, depth // SUBLANES, SUBLANES))],
+    begin_cuts = (0, depth // 8 * 5, depth)
+    end_cuts = tuple(depth // 4 * i for i in range(5))
+
+    state, signals, minus, totals, weighted, message, limits, marks = call(
+        functools.partial(begin_kernel, chips, count, begin_cuts), "begin",
+        [signal, jump_sizes, thresholds.reshape(1, rows)],
+        [block, block, strip, strip, strip, pair, line, vmem(chips + 1, cols)], hbm=(0, 1, 2),
+        scratch=[
+            vmem(1, rows), pltpu.SemaphoreType.DMA((len(begin_cuts) - 1, 2, SUBLANES)), pltpu.SemaphoreType.DMA
+        ],
     )
+    (const,) = call(functools.partial(suffix_kernel, beta), "suffix", [signals], [block], kept=(0,), aliases={0: 0})
     factor = None
     for iteration in range(ITERS):
         if iteration:
@@ -331,16 +374,16 @@
         )
         state, own = call(
             functools.partial(outer_kernel, alpha, chips, offsets), "outer", [inner, slope, base, *received],
-            [block, line], kept=(0, 1, 2), aliases={0: 0}, scratch=[vmem(rows, LANES * len(groups(cols, OUTER_WIDTH)))],
+            [block, line], kept=(0, 1, 2), aliases={0: 0}, scratch=[vmem(len(groups(cols, WIDTH)), depth, SUBLANES, LANES)],
         )
         if halves == 2:
             other = lax.ppermute(own, "prof", swap)
         else:
             own, other = lax.psum(own, "prof"), jnp.zeros_like(own)
     return call(
-        end_kernel, "finish", [own, other, limits, state], jax.ShapeDtypeStruct((rows, cols), jnp.float32), kept=(3,),
+        functools.partial(end_kernel, end_cuts), "finish", [own, other, limits, state], jax.ShapeDtypeStruct((rows, cols), jnp.float32), kept=(3,),
         hbm_out=True,
-        scratch=[spread, block, pltpu.SemaphoreType.DMA((depth // SUBLANES, SUBLANES))],
+        scratch=[spread, block, pltpu.SemaphoreType.DMA((len(end_cuts) - 1, SUBLANES))],
     )
 
 

time: 115 us -> 109 us (0.948)
  Pallas kernels: 33.4 us -> 27.9 us
    pallas_call x25 -> x26, Pallas kernels: 33.4 us -> 27.9 us  [call(): pl.pallas_call(kernel, out_shape=outs, in_specs=[in_hbm if i in hbm else...]
  transfers between devices with their start and end apart: 40 -> 40, of which waited for: 28 -> 28; matrix products, arithmetic and copies ran while one was open for 0% -> 0% of each run, Pallas kernels for 7% -> 8%
where the time goes in v2:
time: 109 us
  starting transfers between devices  40.1 us (37%)
  waiting for transfers between devices  39.6 us (36%)
  Pallas kernels  27.9 us (26%)
    pallas_call x26, Pallas kernels, call(): pl.pallas_call(kernel, out_shape=outs, in_specs=[in_hbm if i in hbm else...  27.9 us
    ppermute x24, starting transfers between devices, local(): lax.ppermute(jnp.where(marks[1 + k:2 + k] > 0.0, upward, downward), ('pro...  26.6 us
    ppermute x8, waiting for transfers between devices, local(): other = lax.ppermute(own, 'prof', swap)  16.9 us
    ppermute x24, waiting for transfers between devices, local(): lax.ppermute(jnp.where(marks[1 + k:2 + k] > 0.0, upward, downward), ('pro...  13.6 us
    ppermute x8, starting transfers between devices, local(): other = lax.ppermute(own, 'prof', swap)  12.5 us
    ppermute x8, waiting for transfers between devices, local(): sibling = lax.ppermute(message, 'sub', swap)  9.03 us
  transfers between devices with their start and end apart: 40, of which 28 were waited for; matrix products, arithmetic and copies ran while one was open for 0% of the time, Pallas kernels for 8%

profile of v2, /device:TPU:0, one launch (start us, length us, event | category | flops | bytes accessed | tf_op | source)
XLA Modules:
  0.0 108.5 jit_solution(12156482439597049743)
XLA Ops:
  0.0 4.0 %begin.1 = (f32[64,8,2048]{2,1,0:T(8,128)S(1)}, f32[64,8,2048]{2,1,0:T(8,128)S(1)}, f32[8,2048]{1,0:T(8,128)S(1)}, f32[8,2048]{1,0:T(8,128)S(1)}, f32[8,2048]{1,...) custom-call(f32[512,2048]{1,0:T(8,128)} %signal_hbm.1, f32[512,2048]{1,0:T(8,128)} %jumps_hbm.1, ...), custom_call_target="tpu_custom_call" | custom-call | tf_op jit(solution)/shard_map/begin/pallas_call | solution.py:315
  5.4 3.8 %collective-permute-start.2 = (f32[1,2048]{1,0:T(1,128)S(1)}, f32[1,2048]{1,0:T(1,128)S(1)}, u32[]{:S(2)}, u32[]{:S(2)}) collective-permute-start(f32[1,2048]{1,0:T(1,128)S(1)} %get-tuple-element.187), channel_id=1, source_target_pairs={{0,9},{1,8},{4,13},{5,12},{8,1},{9,0},{12,5},{13,4},{2,11},{3,10},... | collective-permute-start | bytes 24584 | tf_op jit(solution)/shard_map/ppermute | solution.py:366
  12.3 1.8 %collective-permute-done.1.refs_0_ = f32[1,2048]{1,0:T(1,128)S(1)} collective-permute-done((f32[1,2048]{1,0:T(1,128)S(1)}, f32[1,2048]{1,0:T(1,128)S(1)}, u32[]{:S(2)}, u32[]{:S(2)}) %collective-permute-start.1) | collective-permute-done | bytes 8224 | tf_op jit(solution)/shard_map/ppermute | solution.py:366
  15.0 1.6 %collective-permute-start.4 = (f32[8,128]{1,0:T(8,128)S(1)}, f32[8,128]{1,0:T(8,128)S(1)}, u32[]{:S(2)}, u32[]{:S(2)}) collective-permute-start(f32[8,128]{1,0:T(8,128)S(1)} %get-tuple-element.92.own_ref), channel_id=1, source_target_pairs={{0,2},{2,0},{1,3},{3,1},{4,6},{6,4},{5,7},{7,5},{8,10},{10,8},{9,1... | collective-permute-start | bytes 12296 | tf_op jit(solution)/shard_map/ppermute | solution.py:380
  16.5 2.1 %collective-permute-done.4.other_ref = f32[8,128]{1,0:T(8,128)S(1)} collective-permute-done((f32[8,128]{1,0:T(8,128)S(1)}, f32[8,128]{1,0:T(8,128)S(1)}, u32[]{:S(2)}, u32[]{:S(2)}) %collective-permute-start.4) | collective-permute-done | bytes 4128 | tf_op jit(solution)/shard_map/ppermute | solution.py:380
  24.9 1.7 %collective-permute-done.6.refs_0_ = f32[1,2048]{1,0:T(1,128)S(1)} collective-permute-done((f32[1,2048]{1,0:T(1,128)S(1)}, f32[1,2048]{1,0:T(1,128)S(1)}, u32[]{:S(2)}, u32[]{:S(2)}) %collective-permute-start.6) | collective-permute-done | bytes 8224 | tf_op jit(solution)/shard_map/ppermute | solution.py:366
  29.1 2.1 %collective-permute-done.9.other_ref = f32[8,128]{1,0:T(8,128)S(1)} collective-permute-done((f32[8,128]{1,0:T(8,128)S(1)}, f32[8,128]{1,0:T(8,128)S(1)}, u32[]{:S(2)}, u32[]{:S(2)}) %collective-permute-start.9) | collective-permute-done | bytes 4128 | tf_op jit(solution)/shard_map/ppermute | solution.py:380
  34.1 1.8 %collective-permute-start.11 = (f32[1,2048]{1,0:T(1,128)S(1)}, f32[1,2048]{1,0:T(1,128)S(1)}, u32[]{:S(2)}, u32[]{:S(2)}) collective-permute-start(f32[1,2048]{1,0:T(1,128)S(1)} %get-tuple-element.184), channel_id=1, source_target_pairs={{0,13},{1,12},{4,9},{5,8},{8,5},{9,4},{12,1},{13,0},{2,15},{3,14},... | collective-permute-start | bytes 24584 | tf_op jit(solution)/shard_map/ppermute | solution.py:366
  41.5 2.1 %collective-permute-done.14.other_ref = f32[8,128]{1,0:T(8,128)S(1)} collective-permute-done((f32[8,128]{1,0:T(8,128)S(1)}, f32[8,128]{1,0:T(8,128)S(1)}, u32[]{:S(2)}, u32[]{:S(2)}) %collective-permute-start.14) | collective-permute-done | bytes 4128 | tf_op jit(solution)/shard_map/ppermute | solution.py:380
  46.6 1.8 %collective-permute-start.16 = (f32[1,2048]{1,0:T(1,128)S(1)}, f32[1,2048]{1,0:T(1,128)S(1)}, u32[]{:S(2)}, u32[]{:S(2)}) collective-permute-start(f32[1,2048]{1,0:T(1,128)S(1)} %get-tuple-element.182), channel_id=1, source_target_pairs={{0,13},{1,12},{4,9},{5,8},{8,5},{9,4},{12,1},{13,0},{2,15},{3,14},... | collective-permute-start | bytes 24584 | tf_op jit(solution)/shard_map/ppermute | solution.py:366
  49.8 1.7 %collective-permute-done.16.refs_0_ = f32[1,2048]{1,0:T(1,128)S(1)} collective-permute-done((f32[1,2048]{1,0:T(1,128)S(1)}, f32[1,2048]{1,0:T(1,128)S(1)}, u32[]{:S(2)}, u32[]{:S(2)}) %collective-permute-start.16) | collective-permute-done | bytes 8224 | tf_op jit(solution)/shard_map/ppermute | solution.py:366
  54.0 2.1 %collective-permute-done.19.other_ref = f32[8,128]{1,0:T(8,128)S(1)} collective-permute-done((f32[8,128]{1,0:T(8,128)S(1)}, f32[8,128]{1,0:T(8,128)S(1)}, u32[]{:S(2)}, u32[]{:S(2)}) %collective-permute-start.19) | collective-permute-done | bytes 4128 | tf_op jit(solution)/shard_map/ppermute | solution.py:380
  58.9 1.9 %collective-permute-start.21 = (f32[1,2048]{1,0:T(1,128)S(1)}, f32[1,2048]{1,0:T(1,128)S(1)}, u32[]{:S(2)}, u32[]{:S(2)}) collective-permute-start(f32[1,2048]{1,0:T(1,128)S(1)} %get-tuple-element.180), channel_id=1, source_target_pairs={{0,13},{1,12},{4,9},{5,8},{8,5},{9,4},{12,1},{13,0},{2,15},{3,14},... | collective-permute-start | bytes 24584 | tf_op jit(solution)/shard_map/ppermute | solution.py:366
  66.4 2.1 %collective-permute-done.24.other_ref = f32[8,128]{1,0:T(8,128)S(1)} collective-permute-done((f32[8,128]{1,0:T(8,128)S(1)}, f32[8,128]{1,0:T(8,128)S(1)}, u32[]{:S(2)}, u32[]{:S(2)}) %collective-permute-start.24) | collective-permute-done | bytes 4128 | tf_op jit(solution)/shard_map/ppermute | solution.py:380
  71.5 1.9 %collective-permute-start.26 = (f32[1,2048]{1,0:T(1,128)S(1)}, f32[1,2048]{1,0:T(1,128)S(1)}, u32[]{:S(2)}, u32[]{:S(2)}) collective-permute-start(f32[1,2048]{1,0:T(1,128)S(1)} %get-tuple-element.178), channel_id=1, source_target_pairs={{0,13},{1,12},{4,9},{5,8},{8,5},{9,4},{12,1},{13,0},{2,15},{3,14},... | collective-permute-start | bytes 24584 | tf_op jit(solution)/shard_map/ppermute | solution.py:366
  74.7 1.6 %collective-permute-done.26.refs_0_ = f32[1,2048]{1,0:T(1,128)S(1)} collective-permute-done((f32[1,2048]{1,0:T(1,128)S(1)}, f32[1,2048]{1,0:T(1,128)S(1)}, u32[]{:S(2)}, u32[]{:S(2)}) %collective-permute-start.26) | collective-permute-done | bytes 8224 | tf_op jit(solution)/shard_map/ppermute | solution.py:366
  78.9 2.1 %collective-permute-done.29.other_ref = f32[8,128]{1,0:T(8,128)S(1)} collective-permute-done((f32[8,128]{1,0:T(8,128)S(1)}, f32[8,128]{1,0:T(8,128)S(1)}, u32[]{:S(2)}, u32[]{:S(2)}) %collective-permute-start.29) | collective-permute-done | bytes 4128 | tf_op jit(solution)/shard_map/ppermute | solution.py:380
  83.9 1.8 %collective-permute-start.31 = (f32[1,2048]{1,0:T(1,128)S(1)}, f32[1,2048]{1,0:T(1,128)S(1)}, u32[]{:S(2)}, u32[]{:S(2)}) collective-permute-start(f32[1,2048]{1,0:T(1,128)S(1)} %get-tuple-element.176), channel_id=1, source_target_pairs={{0,13},{1,12},{4,9},{5,8},{8,5},{9,4},{12,1},{13,0},{2,15},{3,14},... | collective-permute-start | bytes 24584 | tf_op jit(solution)/shard_map/ppermute | solution.py:366
  87.3 1.6 %collective-permute-done.31.refs_0_ = f32[1,2048]{1,0:T(1,128)S(1)} collective-permute-done((f32[1,2048]{1,0:T(1,128)S(1)}, f32[1,2048]{1,0:T(1,128)S(1)}, u32[]{:S(2)}, u32[]{:S(2)}) %collective-permute-start.31) | collective-permute-done | bytes 8224 | tf_op jit(solution)/shard_map/ppermute | solution.py:366
  91.3 2.1 %collective-permute-done.34.other_ref = f32[8,128]{1,0:T(8,128)S(1)} collective-permute-done((f32[8,128]{1,0:T(8,128)S(1)}, f32[8,128]{1,0:T(8,128)S(1)}, u32[]{:S(2)}, u32[]{:S(2)}) %collective-permute-start.34) | collective-permute-done | bytes 4128 | tf_op jit(solution)/shard_map/ppermute | solution.py:380
  96.5 1.8 %collective-permute-start.36 = (f32[1,2048]{1,0:T(1,128)S(1)}, f32[1,2048]{1,0:T(1,128)S(1)}, u32[]{:S(2)}, u32[]{:S(2)}) collective-permute-start(f32[1,2048]{1,0:T(1,128)S(1)} %get-tuple-element.174), channel_id=1, source_target_pairs={{0,13},{1,12},{4,9},{5,8},{8,5},{9,4},{12,1},{13,0},{2,15},{3,14},... | collective-permute-start | bytes 24584 | tf_op jit(solution)/shard_map/ppermute | solution.py:366
  99.7 1.7 %collective-permute-done.36.refs_0_ = f32[1,2048]{1,0:T(1,128)S(1)} collective-permute-done((f32[1,2048]{1,0:T(1,128)S(1)}, f32[1,2048]{1,0:T(1,128)S(1)}, u32[]{:S(2)}, u32[]{:S(2)}) %collective-permute-start.36) | collective-permute-done | bytes 8224 | tf_op jit(solution)/shard_map/ppermute | solution.py:366
  103.9 2.1 %collective-permute-done.39.other_ref = f32[8,128]{1,0:T(8,128)S(1)} collective-permute-done((f32[8,128]{1,0:T(8,128)S(1)}, f32[8,128]{1,0:T(8,128)S(1)}, u32[]{:S(2)}, u32[]{:S(2)}) %collective-permute-start.39) | collective-permute-done | bytes 4128 | tf_op jit(solution)/shard_map/ppermute | solution.py:380
  106.0 2.6 %finish.1 = f32[512,2048]{1,0:T(8,128)} custom-call(f32[8,128]{1,0:T(8,128)S(1)} %get-tuple-element.155.own_ref, f32[8,128]{1,0:T(8,128)S(1)} %collective-permute-done.39.other_ref, f32[8,128]{1,0:T(8,128)S(1)} %get-tuple-element.93.limits_ref, f32[64,8,2048]{2,1,0:T(8,128)S(1)} %get-tuple-element.156.state_ref), custom_call_target="tpu_custom_call" | custom-call | tf_op jit(solution)/shard_map/finish/pallas_call | solution.py:315
  (106 shorter events, 58.1 us)
Async XLA Ops:
  5.4 6.8 %collective-permute-start.2 = (f32[1,2048]{1,0:T(1,128)S(1)}, f32[1,2048]{1,0:T(1,128)S(1)}, u32[]{:S(2)}, u32[]{:S(2)}) collective-permute-start(f32[1,2048]{1,0:T(1,128)S(1)} %get-tuple-element.187), channel_id=1, source_target_pairs={{0,9},{1,8},{4,13},{5,12},{8,1},{9,0},{12,5},{13,4},{2,11},{3,10},... | collective-permute-start | bytes 24584 | tf_op jit(solution)/shard_map/ppermute | solution.py:366
  9.2 4.9 %collective-permute-start.1 = (f32[1,2048]{1,0:T(1,128)S(1)}, f32[1,2048]{1,0:T(1,128)S(1)}, u32[]{:S(2)}, u32[]{:S(2)}) collective-permute-start(f32[1,2048]{1,0:T(1,128)S(1)} %get-tuple-element.188), channel_id=1, source_target_pairs={{0,13},{1,12},{4,9},{5,8},{8,5},{9,4},{12,1},{13,0},{2,15},{3,14},... | collective-permute-start | bytes 24584 | tf_op jit(solution)/shard_map/ppermute | solution.py:366
  15.0 3.7 %collective-permute-start.4 = (f32[8,128]{1,0:T(8,128)S(1)}, f32[8,128]{1,0:T(8,128)S(1)}, u32[]{:S(2)}, u32[]{:S(2)}) collective-permute-start(f32[8,128]{1,0:T(8,128)S(1)} %get-tuple-element.92.own_ref), channel_id=1, source_target_pairs={{0,2},{2,0},{1,3},{3,1},{4,6},{6,4},{5,7},{7,5},{8,10},{10,8},{9,1... | collective-permute-start | bytes 12296 | tf_op jit(solution)/shard_map/ppermute | solution.py:380
  20.7 4.1 %collective-permute-start.7 = (f32[1,2048]{1,0:T(1,128)S(1)}, f32[1,2048]{1,0:T(1,128)S(1)}, u32[]{:S(2)}, u32[]{:S(2)}) collective-permute-start(f32[1,2048]{1,0:T(1,128)S(1)} %get-tuple-element.185), channel_id=1, source_target_pairs={{0,9},{1,8},{4,13},{5,12},{8,1},{9,0},{12,5},{13,4},{2,11},{3,10},... | collective-permute-start | bytes 24584 | tf_op jit(solution)/shard_map/ppermute | solution.py:366
  21.7 4.9 %collective-permute-start.6 = (f32[1,2048]{1,0:T(1,128)S(1)}, f32[1,2048]{1,0:T(1,128)S(1)}, u32[]{:S(2)}, u32[]{:S(2)}) collective-permute-start(f32[1,2048]{1,0:T(1,128)S(1)} %get-tuple-element.186), channel_id=1, source_target_pairs={{0,13},{1,12},{4,9},{5,8},{8,5},{9,4},{12,1},{13,0},{2,15},{3,14},... | collective-permute-start | bytes 24584 | tf_op jit(solution)/shard_map/ppermute | solution.py:366
  22.7 4.0 %collective-permute-start.8 = (f32[1,2048]{1,0:T(1,128)S(1)}, f32[1,2048]{1,0:T(1,128)S(1)}, u32[]{:S(2)}, u32[]{:S(2)}) collective-permute-start(f32[1,2048]{1,0:T(1,128)S(1)} %get-tuple-element.169), channel_id=1, source_target_pairs={{0,5},{1,4},{4,1},{5,0},{8,13},{9,12},{12,9},{13,8},{2,7},{3,6},{6... | collective-permute-start | bytes 24584 | tf_op jit(solution)/shard_map/ppermute | solution.py:366
  27.5 3.7 %collective-permute-start.9 = (f32[8,128]{1,0:T(8,128)S(1)}, f32[8,128]{1,0:T(8,128)S(1)}, u32[]{:S(2)}, u32[]{:S(2)}) collective-permute-start(f32[8,128]{1,0:T(8,128)S(1)} %get-tuple-element.102.own_ref), channel_id=1, source_target_pairs={{0,2},{2,0},{1,3},{3,1},{4,6},{6,4},{5,7},{7,5},{8,10},{10,8},{9,1... | collective-permute-start | bytes 12296 | tf_op jit(solution)/shard_map/ppermute | solution.py:380
  33.3 4.1 %collective-permute-start.12 = (f32[1,2048]{1,0:T(1,128)S(1)}, f32[1,2048]{1,0:T(1,128)S(1)}, u32[]{:S(2)}, u32[]{:S(2)}) collective-permute-start(f32[1,2048]{1,0:T(1,128)S(1)} %get-tuple-element.183), channel_id=1, source_target_pairs={{0,9},{1,8},{4,13},{5,12},{8,1},{9,0},{12,5},{13,4},{2,11},{3,10},... | collective-permute-start | bytes 24584 | tf_op jit(solution)/shard_map/ppermute | solution.py:366
  34.1 4.9 %collective-permute-start.11 = (f32[1,2048]{1,0:T(1,128)S(1)}, f32[1,2048]{1,0:T(1,128)S(1)}, u32[]{:S(2)}, u32[]{:S(2)}) collective-permute-start(f32[1,2048]{1,0:T(1,128)S(1)} %get-tuple-element.184), channel_id=1, source_target_pairs={{0,13},{1,12},{4,9},{5,8},{8,5},{9,4},{12,1},{13,0},{2,15},{3,14},... | collective-permute-start | bytes 24584 | tf_op jit(solution)/shard_map/ppermute | solution.py:366
  39.9 3.7 %collective-permute-start.14 = (f32[8,128]{1,0:T(8,128)S(1)}, f32[8,128]{1,0:T(8,128)S(1)}, u32[]{:S(2)}, u32[]{:S(2)}) collective-permute-start(f32[8,128]{1,0:T(8,128)S(1)} %get-tuple-element.111.own_ref), channel_id=1, source_target_pairs={{0,2},{2,0},{1,3},{3,1},{4,6},{6,4},{5,7},{7,5},{8,10},{10,8},{9,1... | collective-permute-start | bytes 12296 | tf_op jit(solution)/shard_map/ppermute | solution.py:380
  45.7 4.1 %collective-permute-start.17 = (f32[1,2048]{1,0:T(1,128)S(1)}, f32[1,2048]{1,0:T(1,128)S(1)}, u32[]{:S(2)}, u32[]{:S(2)}) collective-permute-start(f32[1,2048]{1,0:T(1,128)S(1)} %get-tuple-element.181), channel_id=1, source_target_pairs={{0,9},{1,8},{4,13},{5,12},{8,1},{9,0},{12,5},{13,4},{2,11},{3,10},... | collective-permute-start | bytes 24584 | tf_op jit(solution)/shard_map/ppermute | solution.py:366
  46.6 4.9 %collective-permute-start.16 = (f32[1,2048]{1,0:T(1,128)S(1)}, f32[1,2048]{1,0:T(1,128)S(1)}, u32[]{:S(2)}, u32[]{:S(2)}) collective-permute-start(f32[1,2048]{1,0:T(1,128)S(1)} %get-tuple-element.182), channel_id=1, source_target_pairs={{0,13},{1,12},{4,9},{5,8},{8,5},{9,4},{12,1},{13,0},{2,15},{3,14},... | collective-permute-start | bytes 24584 | tf_op jit(solution)/shard_map/ppermute | solution.py:366
  52.4 3.7 %collective-permute-start.19 = (f32[8,128]{1,0:T(8,128)S(1)}, f32[8,128]{1,0:T(8,128)S(1)}, u32[]{:S(2)}, u32[]{:S(2)}) collective-permute-start(f32[8,128]{1,0:T(8,128)S(1)} %get-tuple-element.120.own_ref), channel_id=1, source_target_pairs={{0,2},{2,0},{1,3},{3,1},{4,6},{6,4},{5,7},{7,5},{8,10},{10,8},{9,1... | collective-permute-start | bytes 12296 | tf_op jit(solution)/shard_map/ppermute | solution.py:380
  58.2 4.1 %collective-permute-start.22 = (f32[1,2048]{1,0:T(1,128)S(1)}, f32[1,2048]{1,0:T(1,128)S(1)}, u32[]{:S(2)}, u32[]{:S(2)}) collective-permute-start(f32[1,2048]{1,0:T(1,128)S(1)} %get-tuple-element.179), channel_id=1, source_target_pairs={{0,9},{1,8},{4,13},{5,12},{8,1},{9,0},{12,5},{13,4},{2,11},{3,10},... | collective-permute-start | bytes 24584 | tf_op jit(solution)/shard_map/ppermute | solution.py:366
  58.9 4.9 %collective-permute-start.21 = (f32[1,2048]{1,0:T(1,128)S(1)}, f32[1,2048]{1,0:T(1,128)S(1)}, u32[]{:S(2)}, u32[]{:S(2)}) collective-permute-start(f32[1,2048]{1,0:T(1,128)S(1)} %get-tuple-element.180), channel_id=1, source_target_pairs={{0,13},{1,12},{4,9},{5,8},{8,5},{9,4},{12,1},{13,0},{2,15},{3,14},... | collective-permute-start | bytes 24584 | tf_op jit(solution)/shard_map/ppermute | solution.py:366
  64.8 3.7 %collective-permute-start.24 = (f32[8,128]{1,0:T(8,128)S(1)}, f32[8,128]{1,0:T(8,128)S(1)}, u32[]{:S(2)}, u32[]{:S(2)}) collective-permute-start(f32[8,128]{1,0:T(8,128)S(1)} %get-tuple-element.129.own_ref), channel_id=1, source_target_pairs={{0,2},{2,0},{1,3},{3,1},{4,6},{6,4},{5,7},{7,5},{8,10},{10,8},{9,1... | collective-permute-start | bytes 12296 | tf_op jit(solution)/shard_map/ppermute | solution.py:380
  70.6 4.1 %collective-permute-start.27 = (f32[1,2048]{1,0:T(1,128)S(1)}, f32[1,2048]{1,0:T(1,128)S(1)}, u32[]{:S(2)}, u32[]{:S(2)}) collective-permute-start(f32[1,2048]{1,0:T(1,128)S(1)} %get-tuple-element.177), channel_id=1, source_target_pairs={{0,9},{1,8},{4,13},{5,12},{8,1},{9,0},{12,5},{13,4},{2,11},{3,10},... | collective-permute-start | bytes 24584 | tf_op jit(solution)/shard_map/ppermute | solution.py:366
  71.5 4.9 %collective-permute-start.26 = (f32[1,2048]{1,0:T(1,128)S(1)}, f32[1,2048]{1,0:T(1,128)S(1)}, u32[]{:S(2)}, u32[]{:S(2)}) collective-permute-start(f32[1,2048]{1,0:T(1,128)S(1)} %get-tuple-element.178), channel_id=1, source_target_pairs={{0,13},{1,12},{4,9},{5,8},{8,5},{9,4},{12,1},{13,0},{2,15},{3,14},... | collective-permute-start | bytes 24584 | tf_op jit(solution)/shard_map/ppermute | solution.py:366
  77.3 3.7 %collective-permute-start.29 = (f32[8,128]{1,0:T(8,128)S(1)}, f32[8,128]{1,0:T(8,128)S(1)}, u32[]{:S(2)}, u32[]{:S(2)}) collective-permute-start(f32[8,128]{1,0:T(8,128)S(1)} %get-tuple-element.138.own_ref), channel_id=1, source_target_pairs={{0,2},{2,0},{1,3},{3,1},{4,6},{6,4},{5,7},{7,5},{8,10},{10,8},{9,1... | collective-permute-start | bytes 12296 | tf_op jit(solution)/shard_map/ppermute | solution.py:380
  83.1 4.1 %collective-permute-start.32 = (f32[1,2048]{1,0:T(1,128)S(1)}, f32[1,2048]{1,0:T(1,128)S(1)}, u32[]{:S(2)}, u32[]{:S(2)}) collective-permute-start(f32[1,2048]{1,0:T(1,128)S(1)} %get-tuple-element.175), channel_id=1, source_target_pairs={{0,9},{1,8},{4,13},{5,12},{8,1},{9,0},{12,5},{13,4},{2,11},{3,10},... | collective-permute-start | bytes 24584 | tf_op jit(solution)/shard_map/ppermute | solution.py:366
  83.9 5.0 %collective-permute-start.31 = (f32[1,2048]{1,0:T(1,128)S(1)}, f32[1,2048]{1,0:T(1,128)S(1)}, u32[]{:S(2)}, u32[]{:S(2)}) collective-permute-start(f32[1,2048]{1,0:T(1,128)S(1)} %get-tuple-element.176), channel_id=1, source_target_pairs={{0,13},{1,12},{4,9},{5,8},{8,5},{9,4},{12,1},{13,0},{2,15},{3,14},... | collective-permute-start | bytes 24584 | tf_op jit(solution)/shard_map/ppermute | solution.py:366
  89.8 3.7 %collective-permute-start.34 = (f32[8,128]{1,0:T(8,128)S(1)}, f32[8,128]{1,0:T(8,128)S(1)}, u32[]{:S(2)}, u32[]{:S(2)}) collective-permute-start(f32[8,128]{1,0:T(8,128)S(1)} %get-tuple-element.147.own_ref), channel_id=1, source_target_pairs={{0,2},{2,0},{1,3},{3,1},{4,6},{6,4},{5,7},{7,5},{8,10},{10,8},{9,1... | collective-permute-start | bytes 12296 | tf_op jit(solution)/shard_map/ppermute | solution.py:380
  95.5 4.1 %collective-permute-start.37 = (f32[1,2048]{1,0:T(1,128)S(1)}, f32[1,2048]{1,0:T(1,128)S(1)}, u32[]{:S(2)}, u32[]{:S(2)}) collective-permute-start(f32[1,2048]{1,0:T(1,128)S(1)} %get-tuple-element.173), channel_id=1, source_target_pairs={{0,9},{1,8},{4,13},{5,12},{8,1},{9,0},{12,5},{13,4},{2,11},{3,10},... | collective-permute-start | bytes 24584 | tf_op jit(solution)/shard_map/ppermute | solution.py:366
  96.5 5.0 %collective-permute-start.36 = (f32[1,2048]{1,0:T(1,128)S(1)}, f32[1,2048]{1,0:T(1,128)S(1)}, u32[]{:S(2)}, u32[]{:S(2)}) collective-permute-start(f32[1,2048]{1,0:T(1,128)S(1)} %get-tuple-element.174), channel_id=1, source_target_pairs={{0,13},{1,12},{4,9},{5,8},{8,5},{9,4},{12,1},{13,0},{2,15},{3,14},... | collective-permute-start | bytes 24584 | tf_op jit(solution)/shard_map/ppermute | solution.py:366
  (16 other events, 36.2 us)

commit v3 on v2

--- a/solution.py
+++ b/solution.py
@@ -12,7 +12,7 @@
 LANES = 128
 SUBLANES = 8
 VMEM_LIMIT = 16 * 1024 * 1024
-WIDTH, BATCH, SUM_BATCH = 8, 4, 8
+WIDTH, BATCH = 8, 4
 
 
 def tiles(cols):
@@ -59,7 +59,7 @@
 
     chip, core = lax.axis_index("probe"), lax.axis_index("sub")
     later = (chips - 1 - chip).astype(jnp.float32) * (2.0 * rows)
-    marks = [(core == 0).astype(jnp.float32), later]
+    marks = [(core == 0).astype(jnp.float32), later, jnp.float32(rows)]
     marks += [(jnp.bitwise_xor(chip, k) > chip).astype(jnp.float32) for k in range(1, chips)]
     for i, mark in enumerate(marks):
         marks_ref[i : i + 1, :] = jnp.full((1, cols), mark, jnp.float32)
@@ -139,23 +139,26 @@
     zero = jnp.zeros((SUBLANES, LANES), jnp.float32)
     totals, weights = [], []
     for group in groups(cols, WIDTH):
-
-        def step(i, carry, group=group):
-            total, weighted = (list(x) for x in carry)
-            for q in range(SUM_BATCH):
-                k = i * SUM_BATCH + q
-                factor = factor_ref[k]
-                for j, c in enumerate(group):
-                    total[j] = total[j] + state_ref[k, :, c] * factor
-                    weighted[j] = weighted[j] + total[j]
-            return total, weighted
-
-        total, weighted = lax.fori_loop(
-            0, depth // SUM_BATCH, step, ([zero] * len(group), [minus_ref[:, c] for c in group])
-        )
+        total, weighted = [zero] * len(group), [minus_ref[:, c] for c in group]
+        for k in range(depth):
+            factor = factor_ref[k]
+            for j, c in enumerate(group):
+                total[j] = total[j] + state_ref[k, :, c] * factor
+                weighted[j] = weighted[j] + total[j]
         totals += total
         weights += weighted
     finish_sums(depth, totals, weights, totals_ref, weighted_ref, message_ref, cols)
+
+
+def route_kernel(offsets, message_ref, sibling_ref, marks_ref, *out_refs):
+    for c in tiles(message_ref.shape[1]):
+        own, sibling = message_ref[0:1, c], sibling_ref[0:1, c]
+        lower = jnp.where(marks_ref[0:1, c] > 0.0, own, sibling)
+        upward = own + sibling
+        weighted = message_ref[1:2, c] + sibling_ref[1:2, c]
+        downward = weighted + marks_ref[1:2, c] * upward + marks_ref[2:3, c] * lower
+        for k, ref in zip(offsets, out_refs):
+            ref[:, c] = jnp.where(marks_ref[2 + k : 3 + k, c] > 0.0, upward, downward)
 
 
 def prefix_rows(x, sublane):
@@ -259,7 +262,7 @@
                 wide_ref[g, k] = total
             return value
 
-        lax.fori_loop(0, depth // BATCH, step, value, unroll=2)
+        lax.fori_loop(0, depth // BATCH, step, value, unroll=4)
     lane = lax.broadcasted_iota(jnp.int32, (SUBLANES, LANES), 1)
     parts = []
     for low in range(0, depth, SUBLANES):
@@ -340,12 +343,12 @@
     strip, line, pair = vmem(SUBLANES, cols), vmem(SUBLANES, LANES), vmem(2, cols)
     spread = vmem(depth, SUBLANES, LANES)
     begin_cuts = (0, depth // 8 * 5, depth)
-    end_cuts = tuple(depth // 4 * i for i in range(5))
+    end_cuts = tuple(depth // 8 * i for i in (0, 1, 3, 5, 8))
 
     state, signals, minus, totals, weighted, message, limits, marks = call(
         functools.partial(begin_kernel, chips, count, begin_cuts), "begin",
         [signal, jump_sizes, thresholds.reshape(1, rows)],
-        [block, block, strip, strip, strip, pair, line, vmem(chips + 1, cols)], hbm=(0, 1, 2),
+        [block, block, strip, strip, strip, pair, line, vmem(chips + 2, cols)], hbm=(0, 1, 2),
         scratch=[
             vmem(1, rows), pltpu.SemaphoreType.DMA((len(begin_cuts) - 1, 2, SUBLANES)), pltpu.SemaphoreType.DMA
         ],
@@ -358,14 +361,10 @@
                 sums_kernel, "sums", [own, other, limits, state, minus], [spread, strip, strip, pair], kept=(3, 4)
             )
         sibling = lax.ppermute(message, "sub", swap)
-        both = message + sibling
-        lower = jnp.where(marks[0:1] > 0.0, message[0:1], sibling[0:1])
-        upward = both[0:1]
-        downward = both[1:2] + float(rows) * lower + marks[1:2] * upward
-        received = [
-            lax.ppermute(jnp.where(marks[1 + k : 2 + k] > 0.0, upward, downward), ("probe", "sub"), routes[k])
-            for k in offsets
-        ]
+        routed = call(
+            functools.partial(route_kernel, offsets), "route", [message, sibling, marks], [vmem(1, cols)] * len(offsets)
+        )
+        received = [lax.ppermute(x, ("probe", "sub"), routes[k]) for k, x in zip(offsets, routed)]
         scaled = factor is not None
         inner, slope, base = call(
             functools.partial(inner_kernel, alpha, chips, scaled), "inner",

time: 109 us -> 106 us (0.972)
  waiting for transfers between devices: 39.6 us -> 32.9 us
  starting transfers between devices: 40.1 us -> 46.4 us
  Pallas kernels: 27.9 us -> 26.6 us
    ppermute x24, waiting for transfers between devices: 13.6 us -> 6.94 us  [local(): lax.ppermute(x, ('probe', 'sub'), routes[k])]
    ppermute x24, starting transfers between devices: 26.6 us -> 33 us  [local(): lax.ppermute(x, ('probe', 'sub'), routes[k])]
    pallas_call x26 -> x34, Pallas kernels: 27.9 us -> 26.6 us  [call(): pl.pallas_call(kernel, out_shape=outs, in_specs=[in_hbm if i in hbm else...]
  transfers between devices with their start and end apart: 40 -> 40, of which waited for: 28 -> 30; matrix products, arithmetic and copies ran while one was open for 0% -> 0% of each run, Pallas kernels for 8% -> 9%
where the time goes in v3:
time: 106 us
  starting transfers between devices  46.4 us (44%)
  waiting for transfers between devices  32.9 us (31%)
  Pallas kernels  26.6 us (25%)
    ppermute x24, starting transfers between devices, local(): lax.ppermute(x, ('probe', 'sub'), routes[k])  33 us
    pallas_call x34, Pallas kernels, call(): pl.pallas_call(kernel, out_shape=outs, in_specs=[in_hbm if i in hbm else...  26.6 us
    ppermute x8, waiting for transfers between devices, local(): other = lax.ppermute(own, 'prof', swap)  16.9 us
    ppermute x8, starting transfers between devices, local(): other = lax.ppermute(own, 'prof', swap)  12.5 us
    ppermute x8, waiting for transfers between devices, local(): sibling = lax.ppermute(message, 'sub', swap)  9.03 us
    ppermute x24, waiting for transfers between devices, local(): lax.ppermute(x, ('probe', 'sub'), routes[k])  6.94 us
  transfers between devices with their start and end apart: 40, of which 30 were waited for; matrix products, arithmetic and copies ran while one was open for 0% of the time, Pallas kernels for 9%

profile of v3, /device:TPU:0, one launch (start us, length us, event | category | flops | bytes accessed | tf_op | source)
XLA Modules:
  0.0 106.2 jit_solution(12735217454089992054)
XLA Ops:
  0.0 4.0 %begin.1 = (f32[64,8,2048]{2,1,0:T(8,128)S(1)}, f32[64,8,2048]{2,1,0:T(8,128)S(1)}, f32[8,2048]{1,0:T(8,128)S(1)}, f32[8,2048]{1,0:T(8,128)S(1)}, f32[8,2048]{1,...) custom-call(f32[512,2048]{1,0:T(8,128)} %signal_hbm.1, f32[512,2048]{1,0:T(8,128)} %jumps_hbm.1, ...), custom_call_target="tpu_custom_call" | custom-call | tf_op jit(solution)/shard_map/begin/pallas_call | solution.py:318
  5.4 4.8 %collective-permute-start.1 = (f32[1,2048]{1,0:T(1,128)S(1)}, f32[1,2048]{1,0:T(1,128)S(1)}, u32[]{:S(2)}, u32[]{:S(2)}) collective-permute-start(f32[1,2048]{1,0:T(1,128)S(1)} %get-tuple-element.115), channel_id=1, source_target_pairs={{0,13},{1,12},{4,9},{5,8},{8,5},{9,4},{12,1},{13,0},{2,15},{3,14},... | collective-permute-start | bytes 24584 | tf_op jit(solution)/shard_map/ppermute | solution.py:367
  12.3 1.9 %collective-permute-done.2.refs_1_ = f32[1,2048]{1,0:T(1,128)S(1)} collective-permute-done((f32[1,2048]{1,0:T(1,128)S(1)}, f32[1,2048]{1,0:T(1,128)S(1)}, u32[]{:S(2)}, u32[]{:S(2)}) %collective-permute-start.2) | collective-permute-done | bytes 8224 | tf_op jit(solution)/shard_map/ppermute | solution.py:367
  15.0 1.6 %collective-permute-start.4 = (f32[8,128]{1,0:T(8,128)S(1)}, f32[8,128]{1,0:T(8,128)S(1)}, u32[]{:S(2)}, u32[]{:S(2)}) collective-permute-start(f32[8,128]{1,0:T(8,128)S(1)} %get-tuple-element.119.own_ref), channel_id=1, source_target_pairs={{0,2},{2,0},{1,3},{3,1},{4,6},{6,4},{5,7},{7,5},{8,10},{10,8},{9,1... | collective-permute-start | bytes 12296 | tf_op jit(solution)/shard_map/ppermute | solution.py:379
  16.6 2.1 %collective-permute-done.4.other_ref = f32[8,128]{1,0:T(8,128)S(1)} collective-permute-done((f32[8,128]{1,0:T(8,128)S(1)}, f32[8,128]{1,0:T(8,128)S(1)}, u32[]{:S(2)}, u32[]{:S(2)}) %collective-permute-start.4) | collective-permute-done | bytes 4128 | tf_op jit(solution)/shard_map/ppermute | solution.py:379
  22.4 2.1 %collective-permute-start.8 = (f32[1,2048]{1,0:T(1,128)S(1)}, f32[1,2048]{1,0:T(1,128)S(1)}, u32[]{:S(2)}, u32[]{:S(2)}) collective-permute-start(f32[1,2048]{1,0:T(1,128)S(1)} %get-tuple-element.130), channel_id=1, source_target_pairs={{0,5},{1,4},{4,1},{5,0},{8,13},{9,12},{12,9},{13,8},{2,7},{3,6},{6... | collective-permute-start | bytes 24584 | tf_op jit(solution)/shard_map/ppermute | solution.py:367
  26.9 1.6 %collective-permute-start.9 = (f32[8,128]{1,0:T(8,128)S(1)}, f32[8,128]{1,0:T(8,128)S(1)}, u32[]{:S(2)}, u32[]{:S(2)}) collective-permute-start(f32[8,128]{1,0:T(8,128)S(1)} %get-tuple-element.132.own_ref), channel_id=1, source_target_pairs={{0,2},{2,0},{1,3},{3,1},{4,6},{6,4},{5,7},{7,5},{8,10},{10,8},{9,1... | collective-permute-start | bytes 12296 | tf_op jit(solution)/shard_map/ppermute | solution.py:379
  28.4 2.1 %collective-permute-done.9.other_ref = f32[8,128]{1,0:T(8,128)S(1)} collective-permute-done((f32[8,128]{1,0:T(8,128)S(1)}, f32[8,128]{1,0:T(8,128)S(1)}, u32[]{:S(2)}, u32[]{:S(2)}) %collective-permute-start.9) | collective-permute-done | bytes 4128 | tf_op jit(solution)/shard_map/ppermute | solution.py:379
  32.4 2.1 %collective-permute-start.11 = (f32[1,2048]{1,0:T(1,128)S(1)}, f32[1,2048]{1,0:T(1,128)S(1)}, u32[]{:S(2)}, u32[]{:S(2)}) collective-permute-start(f32[1,2048]{1,0:T(1,128)S(1)} %get-tuple-element.140), channel_id=1, source_target_pairs={{0,13},{1,12},{4,9},{5,8},{8,5},{9,4},{12,1},{13,0},{2,15},{3,14},... | collective-permute-start | bytes 24584 | tf_op jit(solution)/shard_map/ppermute | solution.py:367
  41.0 2.1 %collective-permute-done.14.other_ref = f32[8,128]{1,0:T(8,128)S(1)} collective-permute-done((f32[8,128]{1,0:T(8,128)S(1)}, f32[8,128]{1,0:T(8,128)S(1)}, u32[]{:S(2)}, u32[]{:S(2)}) %collective-permute-start.14) | collective-permute-done | bytes 4128 | tf_op jit(solution)/shard_map/ppermute | solution.py:379
  47.3 1.6 %collective-permute-start.18 = (f32[1,2048]{1,0:T(1,128)S(1)}, f32[1,2048]{1,0:T(1,128)S(1)}, u32[]{:S(2)}, u32[]{:S(2)}) collective-permute-start(f32[1,2048]{1,0:T(1,128)S(1)} %get-tuple-element.154), channel_id=1, source_target_pairs={{0,5},{1,4},{4,1},{5,0},{8,13},{9,12},{12,9},{13,8},{2,7},{3,6},{6... | collective-permute-start | bytes 24584 | tf_op jit(solution)/shard_map/ppermute | solution.py:367
  51.3 1.6 %collective-permute-start.19 = (f32[8,128]{1,0:T(8,128)S(1)}, f32[8,128]{1,0:T(8,128)S(1)}, u32[]{:S(2)}, u32[]{:S(2)}) collective-permute-start(f32[8,128]{1,0:T(8,128)S(1)} %get-tuple-element.156.own_ref), channel_id=1, source_target_pairs={{0,2},{2,0},{1,3},{3,1},{4,6},{6,4},{5,7},{7,5},{8,10},{10,8},{9,1... | collective-permute-start | bytes 12296 | tf_op jit(solution)/shard_map/ppermute | solution.py:379
  52.8 2.1 %collective-permute-done.19.other_ref = f32[8,128]{1,0:T(8,128)S(1)} collective-permute-done((f32[8,128]{1,0:T(8,128)S(1)}, f32[8,128]{1,0:T(8,128)S(1)}, u32[]{:S(2)}, u32[]{:S(2)}) %collective-permute-start.19) | collective-permute-done | bytes 4128 | tf_op jit(solution)/shard_map/ppermute | solution.py:379
  56.8 2.1 %collective-permute-start.21 = (f32[1,2048]{1,0:T(1,128)S(1)}, f32[1,2048]{1,0:T(1,128)S(1)}, u32[]{:S(2)}, u32[]{:S(2)}) collective-permute-start(f32[1,2048]{1,0:T(1,128)S(1)} %get-tuple-element.164), channel_id=1, source_target_pairs={{0,13},{1,12},{4,9},{5,8},{8,5},{9,4},{12,1},{13,0},{2,15},{3,14},... | collective-permute-start | bytes 24584 | tf_op jit(solution)/shard_map/ppermute | solution.py:367
  63.8 1.6 %collective-permute-start.24 = (f32[8,128]{1,0:T(8,128)S(1)}, f32[8,128]{1,0:T(8,128)S(1)}, u32[]{:S(2)}, u32[]{:S(2)}) collective-permute-start(f32[8,128]{1,0:T(8,128)S(1)} %get-tuple-element.168.own_ref), channel_id=1, source_target_pairs={{0,2},{2,0},{1,3},{3,1},{4,6},{6,4},{5,7},{7,5},{8,10},{10,8},{9,1... | collective-permute-start | bytes 12296 | tf_op jit(solution)/shard_map/ppermute | solution.py:379
  65.3 2.1 %collective-permute-done.24.other_ref = f32[8,128]{1,0:T(8,128)S(1)} collective-permute-done((f32[8,128]{1,0:T(8,128)S(1)}, f32[8,128]{1,0:T(8,128)S(1)}, u32[]{:S(2)}, u32[]{:S(2)}) %collective-permute-start.24) | collective-permute-done | bytes 4128 | tf_op jit(solution)/shard_map/ppermute | solution.py:379
  71.7 1.6 %collective-permute-start.28 = (f32[1,2048]{1,0:T(1,128)S(1)}, f32[1,2048]{1,0:T(1,128)S(1)}, u32[]{:S(2)}, u32[]{:S(2)}) collective-permute-start(f32[1,2048]{1,0:T(1,128)S(1)} %get-tuple-element.178), channel_id=1, source_target_pairs={{0,5},{1,4},{4,1},{5,0},{8,13},{9,12},{12,9},{13,8},{2,7},{3,6},{6... | collective-permute-start | bytes 24584 | tf_op jit(solution)/shard_map/ppermute | solution.py:367
  75.7 1.6 %collective-permute-start.29 = (f32[8,128]{1,0:T(8,128)S(1)}, f32[8,128]{1,0:T(8,128)S(1)}, u32[]{:S(2)}, u32[]{:S(2)}) collective-permute-start(f32[8,128]{1,0:T(8,128)S(1)} %get-tuple-element.180.own_ref), channel_id=1, source_target_pairs={{0,2},{2,0},{1,3},{3,1},{4,6},{6,4},{5,7},{7,5},{8,10},{10,8},{9,1... | collective-permute-start | bytes 12296 | tf_op jit(solution)/shard_map/ppermute | solution.py:379
  77.2 2.1 %collective-permute-done.29.other_ref = f32[8,128]{1,0:T(8,128)S(1)} collective-permute-done((f32[8,128]{1,0:T(8,128)S(1)}, f32[8,128]{1,0:T(8,128)S(1)}, u32[]{:S(2)}, u32[]{:S(2)}) %collective-permute-start.29) | collective-permute-done | bytes 4128 | tf_op jit(solution)/shard_map/ppermute | solution.py:379
  81.2 2.1 %collective-permute-start.31 = (f32[1,2048]{1,0:T(1,128)S(1)}, f32[1,2048]{1,0:T(1,128)S(1)}, u32[]{:S(2)}, u32[]{:S(2)}) collective-permute-start(f32[1,2048]{1,0:T(1,128)S(1)} %get-tuple-element.188), channel_id=1, source_target_pairs={{0,13},{1,12},{4,9},{5,8},{8,5},{9,4},{12,1},{13,0},{2,15},{3,14},... | collective-permute-start | bytes 24584 | tf_op jit(solution)/shard_map/ppermute | solution.py:367
  89.7 2.1 %collective-permute-done.34.other_ref = f32[8,128]{1,0:T(8,128)S(1)} collective-permute-done((f32[8,128]{1,0:T(8,128)S(1)}, f32[8,128]{1,0:T(8,128)S(1)}, u32[]{:S(2)}, u32[]{:S(2)}) %collective-permute-start.34) | collective-permute-done | bytes 4128 | tf_op jit(solution)/shard_map/ppermute | solution.py:379
  96.1 1.6 %collective-permute-start.38 = (f32[1,2048]{1,0:T(1,128)S(1)}, f32[1,2048]{1,0:T(1,128)S(1)}, u32[]{:S(2)}, u32[]{:S(2)}) collective-permute-start(f32[1,2048]{1,0:T(1,128)S(1)} %get-tuple-element.202), channel_id=1, source_target_pairs={{0,5},{1,4},{4,1},{5,0},{8,13},{9,12},{12,9},{13,8},{2,7},{3,6},{6... | collective-permute-start | bytes 24584 | tf_op jit(solution)/shard_map/ppermute | solution.py:367
  101.6 2.1 %collective-permute-done.39.other_ref = f32[8,128]{1,0:T(8,128)S(1)} collective-permute-done((f32[8,128]{1,0:T(8,128)S(1)}, f32[8,128]{1,0:T(8,128)S(1)}, u32[]{:S(2)}, u32[]{:S(2)}) %collective-permute-start.39) | collective-permute-done | bytes 4128 | tf_op jit(solution)/shard_map/ppermute | solution.py:379
  103.7 2.5 %finish.1 = f32[512,2048]{1,0:T(8,128)} custom-call(f32[8,128]{1,0:T(8,128)S(1)} %get-tuple-element.203.own_ref, f32[8,128]{1,0:T(8,128)S(1)} %collective-permute-done.39.other_ref, f32[8,128]{1,0:T(8,128)S(1)} %get-tuple-element.120.limits_ref, f32[64,8,2048]{2,1,0:T(8,128)S(1)} %get-tuple-element.204.state_ref), custom_call_target="tpu_custom_call" | custom-call | tf_op jit(solution)/shard_map/finish/pallas_call | solution.py:318
  (90 shorter events, 55.1 us)
Async XLA Ops:
  5.4 6.9 %collective-permute-start.1 = (f32[1,2048]{1,0:T(1,128)S(1)}, f32[1,2048]{1,0:T(1,128)S(1)}, u32[]{:S(2)}, u32[]{:S(2)}) collective-permute-start(f32[1,2048]{1,0:T(1,128)S(1)} %get-tuple-element.115), channel_id=1, source_target_pairs={{0,13},{1,12},{4,9},{5,8},{8,5},{9,4},{12,1},{13,0},{2,15},{3,14},... | collective-permute-start | bytes 24584 | tf_op jit(solution)/shard_map/ppermute | solution.py:367
  10.2 4.0 %collective-permute-start.2 = (f32[1,2048]{1,0:T(1,128)S(1)}, f32[1,2048]{1,0:T(1,128)S(1)}, u32[]{:S(2)}, u32[]{:S(2)}) collective-permute-start(f32[1,2048]{1,0:T(1,128)S(1)} %get-tuple-element.116), channel_id=1, source_target_pairs={{0,9},{1,8},{4,13},{5,12},{8,1},{9,0},{12,5},{13,4},{2,11},{3,10},... | collective-permute-start | bytes 24584 | tf_op jit(solution)/shard_map/ppermute | solution.py:367
  10.2 4.0 %collective-permute-start.3 = (f32[1,2048]{1,0:T(1,128)S(1)}, f32[1,2048]{1,0:T(1,128)S(1)}, u32[]{:S(2)}, u32[]{:S(2)}) collective-permute-start(f32[1,2048]{1,0:T(1,128)S(1)} %get-tuple-element.117), channel_id=1, source_target_pairs={{0,5},{1,4},{4,1},{5,0},{8,13},{9,12},{12,9},{13,8},{2,7},{3,6},{6... | collective-permute-start | bytes 24584 | tf_op jit(solution)/shard_map/ppermute | solution.py:367
  15.0 3.7 %collective-permute-start.4 = (f32[8,128]{1,0:T(8,128)S(1)}, f32[8,128]{1,0:T(8,128)S(1)}, u32[]{:S(2)}, u32[]{:S(2)}) collective-permute-start(f32[8,128]{1,0:T(8,128)S(1)} %get-tuple-element.119.own_ref), channel_id=1, source_target_pairs={{0,2},{2,0},{1,3},{3,1},{4,6},{6,4},{5,7},{7,5},{8,10},{10,8},{9,1... | collective-permute-start | bytes 12296 | tf_op jit(solution)/shard_map/ppermute | solution.py:379
  20.5 5.0 %collective-permute-start.6 = (f32[1,2048]{1,0:T(1,128)S(1)}, f32[1,2048]{1,0:T(1,128)S(1)}, u32[]{:S(2)}, u32[]{:S(2)}) collective-permute-start(f32[1,2048]{1,0:T(1,128)S(1)} %get-tuple-element.128), channel_id=1, source_target_pairs={{0,13},{1,12},{4,9},{5,8},{8,5},{9,4},{12,1},{13,0},{2,15},{3,14},... | collective-permute-start | bytes 24584 | tf_op jit(solution)/shard_map/ppermute | solution.py:367
  22.1 4.0 %collective-permute-start.7 = (f32[1,2048]{1,0:T(1,128)S(1)}, f32[1,2048]{1,0:T(1,128)S(1)}, u32[]{:S(2)}, u32[]{:S(2)}) collective-permute-start(f32[1,2048]{1,0:T(1,128)S(1)} %get-tuple-element.129), channel_id=1, source_target_pairs={{0,9},{1,8},{4,13},{5,12},{8,1},{9,0},{12,5},{13,4},{2,11},{3,10},... | collective-permute-start | bytes 24584 | tf_op jit(solution)/shard_map/ppermute | solution.py:367
  26.9 3.7 %collective-permute-start.9 = (f32[8,128]{1,0:T(8,128)S(1)}, f32[8,128]{1,0:T(8,128)S(1)}, u32[]{:S(2)}, u32[]{:S(2)}) collective-permute-start(f32[8,128]{1,0:T(8,128)S(1)} %get-tuple-element.132.own_ref), channel_id=1, source_target_pairs={{0,2},{2,0},{1,3},{3,1},{4,6},{6,4},{5,7},{7,5},{8,10},{10,8},{9,1... | collective-permute-start | bytes 12296 | tf_op jit(solution)/shard_map/ppermute | solution.py:379
  32.4 5.0 %collective-permute-start.11 = (f32[1,2048]{1,0:T(1,128)S(1)}, f32[1,2048]{1,0:T(1,128)S(1)}, u32[]{:S(2)}, u32[]{:S(2)}) collective-permute-start(f32[1,2048]{1,0:T(1,128)S(1)} %get-tuple-element.140), channel_id=1, source_target_pairs={{0,13},{1,12},{4,9},{5,8},{8,5},{9,4},{12,1},{13,0},{2,15},{3,14},... | collective-permute-start | bytes 24584 | tf_op jit(solution)/shard_map/ppermute | solution.py:367
  34.5 4.0 %collective-permute-start.12 = (f32[1,2048]{1,0:T(1,128)S(1)}, f32[1,2048]{1,0:T(1,128)S(1)}, u32[]{:S(2)}, u32[]{:S(2)}) collective-permute-start(f32[1,2048]{1,0:T(1,128)S(1)} %get-tuple-element.141), channel_id=1, source_target_pairs={{0,9},{1,8},{4,13},{5,12},{8,1},{9,0},{12,5},{13,4},{2,11},{3,10},... | collective-permute-start | bytes 24584 | tf_op jit(solution)/shard_map/ppermute | solution.py:367
  44.9 5.0 %collective-permute-start.16 = (f32[1,2048]{1,0:T(1,128)S(1)}, f32[1,2048]{1,0:T(1,128)S(1)}, u32[]{:S(2)}, u32[]{:S(2)}) collective-permute-start(f32[1,2048]{1,0:T(1,128)S(1)} %get-tuple-element.152), channel_id=1, source_target_pairs={{0,13},{1,12},{4,9},{5,8},{8,5},{9,4},{12,1},{13,0},{2,15},{3,14},... | collective-permute-start | bytes 24584 | tf_op jit(solution)/shard_map/ppermute | solution.py:367
  46.4 4.0 %collective-permute-start.17 = (f32[1,2048]{1,0:T(1,128)S(1)}, f32[1,2048]{1,0:T(1,128)S(1)}, u32[]{:S(2)}, u32[]{:S(2)}) collective-permute-start(f32[1,2048]{1,0:T(1,128)S(1)} %get-tuple-element.153), channel_id=1, source_target_pairs={{0,9},{1,8},{4,13},{5,12},{8,1},{9,0},{12,5},{13,4},{2,11},{3,10},... | collective-permute-start | bytes 24584 | tf_op jit(solution)/shard_map/ppermute | solution.py:367
  51.3 3.7 %collective-permute-start.19 = (f32[8,128]{1,0:T(8,128)S(1)}, f32[8,128]{1,0:T(8,128)S(1)}, u32[]{:S(2)}, u32[]{:S(2)}) collective-permute-start(f32[8,128]{1,0:T(8,128)S(1)} %get-tuple-element.156.own_ref), channel_id=1, source_target_pairs={{0,2},{2,0},{1,3},{3,1},{4,6},{6,4},{5,7},{7,5},{8,10},{10,8},{9,1... | collective-permute-start | bytes 12296 | tf_op jit(solution)/shard_map/ppermute | solution.py:379
  56.8 5.0 %collective-permute-start.21 = (f32[1,2048]{1,0:T(1,128)S(1)}, f32[1,2048]{1,0:T(1,128)S(1)}, u32[]{:S(2)}, u32[]{:S(2)}) collective-permute-start(f32[1,2048]{1,0:T(1,128)S(1)} %get-tuple-element.164), channel_id=1, source_target_pairs={{0,13},{1,12},{4,9},{5,8},{8,5},{9,4},{12,1},{13,0},{2,15},{3,14},... | collective-permute-start | bytes 24584 | tf_op jit(solution)/shard_map/ppermute | solution.py:367
  58.9 4.0 %collective-permute-start.22 = (f32[1,2048]{1,0:T(1,128)S(1)}, f32[1,2048]{1,0:T(1,128)S(1)}, u32[]{:S(2)}, u32[]{:S(2)}) collective-permute-start(f32[1,2048]{1,0:T(1,128)S(1)} %get-tuple-element.165), channel_id=1, source_target_pairs={{0,9},{1,8},{4,13},{5,12},{8,1},{9,0},{12,5},{13,4},{2,11},{3,10},... | collective-permute-start | bytes 24584 | tf_op jit(solution)/shard_map/ppermute | solution.py:367
  63.8 3.7 %collective-permute-start.24 = (f32[8,128]{1,0:T(8,128)S(1)}, f32[8,128]{1,0:T(8,128)S(1)}, u32[]{:S(2)}, u32[]{:S(2)}) collective-permute-start(f32[8,128]{1,0:T(8,128)S(1)} %get-tuple-element.168.own_ref), channel_id=1, source_target_pairs={{0,2},{2,0},{1,3},{3,1},{4,6},{6,4},{5,7},{7,5},{8,10},{10,8},{9,1... | collective-permute-start | bytes 12296 | tf_op jit(solution)/shard_map/ppermute | solution.py:379
  69.3 5.0 %collective-permute-start.26 = (f32[1,2048]{1,0:T(1,128)S(1)}, f32[1,2048]{1,0:T(1,128)S(1)}, u32[]{:S(2)}, u32[]{:S(2)}) collective-permute-start(f32[1,2048]{1,0:T(1,128)S(1)} %get-tuple-element.176), channel_id=1, source_target_pairs={{0,13},{1,12},{4,9},{5,8},{8,5},{9,4},{12,1},{13,0},{2,15},{3,14},... | collective-permute-start | bytes 24584 | tf_op jit(solution)/shard_map/ppermute | solution.py:367
  70.7 4.0 %collective-permute-start.27 = (f32[1,2048]{1,0:T(1,128)S(1)}, f32[1,2048]{1,0:T(1,128)S(1)}, u32[]{:S(2)}, u32[]{:S(2)}) collective-permute-start(f32[1,2048]{1,0:T(1,128)S(1)} %get-tuple-element.177), channel_id=1, source_target_pairs={{0,9},{1,8},{4,13},{5,12},{8,1},{9,0},{12,5},{13,4},{2,11},{3,10},... | collective-permute-start | bytes 24584 | tf_op jit(solution)/shard_map/ppermute | solution.py:367
  75.7 3.7 %collective-permute-start.29 = (f32[8,128]{1,0:T(8,128)S(1)}, f32[8,128]{1,0:T(8,128)S(1)}, u32[]{:S(2)}, u32[]{:S(2)}) collective-permute-start(f32[8,128]{1,0:T(8,128)S(1)} %get-tuple-element.180.own_ref), channel_id=1, source_target_pairs={{0,2},{2,0},{1,3},{3,1},{4,6},{6,4},{5,7},{7,5},{8,10},{10,8},{9,1... | collective-permute-start | bytes 12296 | tf_op jit(solution)/shard_map/ppermute | solution.py:379
  81.2 5.0 %collective-permute-start.31 = (f32[1,2048]{1,0:T(1,128)S(1)}, f32[1,2048]{1,0:T(1,128)S(1)}, u32[]{:S(2)}, u32[]{:S(2)}) collective-permute-start(f32[1,2048]{1,0:T(1,128)S(1)} %get-tuple-element.188), channel_id=1, source_target_pairs={{0,13},{1,12},{4,9},{5,8},{8,5},{9,4},{12,1},{13,0},{2,15},{3,14},... | collective-permute-start | bytes 24584 | tf_op jit(solution)/shard_map/ppermute | solution.py:367
  83.2 4.0 %collective-permute-start.32 = (f32[1,2048]{1,0:T(1,128)S(1)}, f32[1,2048]{1,0:T(1,128)S(1)}, u32[]{:S(2)}, u32[]{:S(2)}) collective-permute-start(f32[1,2048]{1,0:T(1,128)S(1)} %get-tuple-element.189), channel_id=1, source_target_pairs={{0,9},{1,8},{4,13},{5,12},{8,1},{9,0},{12,5},{13,4},{2,11},{3,10},... | collective-permute-start | bytes 24584 | tf_op jit(solution)/shard_map/ppermute | solution.py:367
  88.1 3.7 %collective-permute-start.34 = (f32[8,128]{1,0:T(8,128)S(1)}, f32[8,128]{1,0:T(8,128)S(1)}, u32[]{:S(2)}, u32[]{:S(2)}) collective-permute-start(f32[8,128]{1,0:T(8,128)S(1)} %get-tuple-element.192.own_ref), channel_id=1, source_target_pairs={{0,2},{2,0},{1,3},{3,1},{4,6},{6,4},{5,7},{7,5},{8,10},{10,8},{9,1... | collective-permute-start | bytes 12296 | tf_op jit(solution)/shard_map/ppermute | solution.py:379
  93.7 5.0 %collective-permute-start.36 = (f32[1,2048]{1,0:T(1,128)S(1)}, f32[1,2048]{1,0:T(1,128)S(1)}, u32[]{:S(2)}, u32[]{:S(2)}) collective-permute-start(f32[1,2048]{1,0:T(1,128)S(1)} %get-tuple-element.200), channel_id=1, source_target_pairs={{0,13},{1,12},{4,9},{5,8},{8,5},{9,4},{12,1},{13,0},{2,15},{3,14},... | collective-permute-start | bytes 24584 | tf_op jit(solution)/shard_map/ppermute | solution.py:367
  95.1 4.0 %collective-permute-start.37 = (f32[1,2048]{1,0:T(1,128)S(1)}, f32[1,2048]{1,0:T(1,128)S(1)}, u32[]{:S(2)}, u32[]{:S(2)}) collective-permute-start(f32[1,2048]{1,0:T(1,128)S(1)} %get-tuple-element.201), channel_id=1, source_target_pairs={{0,9},{1,8},{4,13},{5,12},{8,1},{9,0},{12,5},{13,4},{2,11},{3,10},... | collective-permute-start | bytes 24584 | tf_op jit(solution)/shard_map/ppermute | solution.py:367
  100.0 3.7 %collective-permute-start.39 = (f32[8,128]{1,0:T(8,128)S(1)}, f32[8,128]{1,0:T(8,128)S(1)}, u32[]{:S(2)}, u32[]{:S(2)}) collective-permute-start(f32[8,128]{1,0:T(8,128)S(1)} %get-tuple-element.203.own_ref), channel_id=1, source_target_pairs={{0,2},{2,0},{1,3},{3,1},{4,6},{6,4},{5,7},{7,5},{8,10},{10,8},{9,1... | collective-permute-start | bytes 12296 | tf_op jit(solution)/shard_map/ppermute | solution.py:379
  (16 other events, 36.2 us)

commit v4 on v3

--- a/solution.py
+++ b/solution.py
@@ -186,15 +186,13 @@
 
     zero = jnp.zeros((SUBLANES, LANES), jnp.float32)
     for group in groups(cols, WIDTH):
-
-        def step(i, carry, group=group):
-            running, double = (list(x) for x in carry)
-            start = depth - (i + 1) * BATCH
+        running, double = [totals_ref[:, c] * alpha for c in group], [zero] * len(group)
+        for start in reversed(range(0, depth, BATCH)):
             results = []
-            for k in reversed([start + q for q in range(BATCH)]):
+            for k in reversed(range(start, start + BATCH)):
                 factor = factor_ref[k] if scaled else None
                 for j, c in enumerate(group):
-                    jump = state_ref[k, :, c]
+                    jump = inner_ref[k, :, c]
                     if scaled:
                         jump = jump * factor
                     double[j] = double[j] + running[j]
@@ -202,11 +200,6 @@
                     running[j] = running[j] - jump * alpha
             for k, c, value in results:
                 inner_ref[k, :, c] = value
-            return running, double
-
-        lax.fori_loop(
-            0, depth // BATCH, step, ([totals_ref[:, c] * alpha for c in group], [zero] * len(group))
-        )
 
     for c in cs:
         total = totals_ref[:, c]
@@ -224,7 +217,7 @@
 
 
 def outer_kernel(alpha, chips, offsets, inner_ref, slope_ref, base_ref, *refs):
-    received, (state_ref, squares_ref, wide_ref) = refs[: len(offsets)], refs[len(offsets) :]
+    received, (state_ref, squares_ref) = refs[: len(offsets)], refs[len(offsets) :]
     depth, _, cols = inner_ref.shape
     rows = float(depth * SUBLANES)
     chip, core = lax.axis_index("probe"), lax.axis_index("sub")
@@ -232,8 +225,9 @@
     weights = row_weights() * float(depth) + later
     earlier = [(jnp.bitwise_xor(chip, k) < chip).astype(jnp.float32) for k in offsets]
 
-    grouped = groups(cols, WIDTH)
-    for g, group in enumerate(grouped):
+    lane = lax.broadcasted_iota(jnp.int32, (SUBLANES, LANES), 1) % depth
+    sums = [jnp.zeros((SUBLANES, LANES), jnp.float32)] * 4
+    for group in groups(cols, WIDTH):
         slope, value = [], []
         for c in group:
             above = sum(e * ref[:, c] for e, ref in zip(earlier, received))
@@ -242,36 +236,18 @@
             slope.append(slope_ref[:, c] + above)
             value.append(base_ref[:, c] + below + weights * above + slope[-1])
 
-        def step(i, value, g=g, group=group, slope=slope):
-            value = list(value)
-            start = depth - (i + 1) * BATCH
-            results, sums = [], []
-            for k in reversed([start + q for q in range(BATCH)]):
-                squares = []
-                for j, c in enumerate(group):
-                    stepped = inner_ref[k, :, c] - value[j]
-                    value[j] = value[j] + slope[j]
-                    results.append((k, c, stepped))
-                    squares.append(stepped * stepped)
-                while len(squares) > 1:
-                    squares = [a + b for a, b in zip(squares[::2], squares[1::2])]
-                sums.append((k, squares[0]))
-            for k, c, stepped in results:
+        for k in reversed(range(depth)):
+            squares = []
+            for j, c in enumerate(group):
+                stepped = state_ref[k, :, c] - value[j]
+                value[j] = value[j] + slope[j]
                 state_ref[k, :, c] = stepped
-            for k, total in sums:
-                wide_ref[g, k] = total
-            return value
-
-        lax.fori_loop(0, depth // BATCH, step, value, unroll=4)
-    lane = lax.broadcasted_iota(jnp.int32, (SUBLANES, LANES), 1)
-    parts = []
-    for low in range(0, depth, SUBLANES):
-        part = jnp.zeros((SUBLANES, LANES), jnp.float32)
-        for k in range(low, low + SUBLANES):
-            total = jnp.sum(sum(wide_ref[g, k] for g in range(len(grouped))), axis=1, keepdims=True)
-            part = jnp.where(lane % depth == k, jnp.broadcast_to(total, part.shape), part)
-        parts.append(part)
-    squares_ref[...] = sum(parts)
+                squares.append(stepped * stepped)
+            while len(squares) > 1:
+                squares = [a + b for a, b in zip(squares[::2], squares[1::2])]
+            total = jnp.broadcast_to(jnp.sum(squares[0], axis=1, keepdims=True), (SUBLANES, LANES))
+            sums[k % 4] = sums[k % 4] + jnp.where(lane == k, total, 0.0)
+    squares_ref[...] = (sums[0] + sums[1]) + (sums[2] + sums[3])
 
 
 def end_kernel(cuts, own_ref, other_ref, limits_ref, state_ref, out_hbm, factor_ref, jumps_ref, sems):
@@ -373,7 +349,7 @@
         )
         state, own = call(
             functools.partial(outer_kernel, alpha, chips, offsets), "outer", [inner, slope, base, *received],
-            [block, line], kept=(0, 1, 2), aliases={0: 0}, scratch=[vmem(len(groups(cols, WIDTH)), depth, SUBLANES, LANES)],
+            [block, line], kept=(0, 1, 2), aliases={0: 0},
         )
         if halves == 2:
             other = lax.ppermute(own, "prof", swap)

time: 106 us -> 105 us (level)
  Pallas kernels: 26.6 us -> 24.3 us
  waiting for transfers between devices: 32.9 us -> 34.2 us
    pallas_call x34, Pallas kernels: 26.6 us -> 24.3 us  [call(): pl.pallas_call(kernel, out_shape=outs, in_specs=[in_hbm if i in hbm else...]
    ppermute x24, waiting for transfers between devices: 6.94 us -> 8.26 us  [local(): lax.ppermute(x, ('probe', 'sub'), routes[k])]
  transfers between devices with their start and end apart: 40 -> 40, of which waited for: 30 -> 37; matrix products, arithmetic and copies ran while one was open for 0% -> 0% of each run, Pallas kernels for 9% -> 7%
where the time goes in v4:
time: 105 us
  starting transfers between devices  46.4 us (44%)
  waiting for transfers between devices  34.2 us (33%)
  Pallas kernels  24.3 us (23%)
    ppermute x24, starting transfers between devices, local(): lax.ppermute(x, ('probe', 'sub'), routes[k])  33 us
    pallas_call x34, Pallas kernels, call(): pl.pallas_call(kernel, out_shape=outs, in_specs=[in_hbm if i in hbm else...  24.3 us
    ppermute x8, waiting for transfers between devices, local(): other = lax.ppermute(own, 'prof', swap)  16.9 us
    ppermute x8, starting transfers between devices, local(): other = lax.ppermute(own, 'prof', swap)  12.4 us
    ppermute x8, waiting for transfers between devices, local(): sibling = lax.ppermute(message, 'sub', swap)  9.03 us
    ppermute x24, waiting for transfers between devices, local(): lax.ppermute(x, ('probe', 'sub'), routes[k])  8.26 us
  transfers between devices with their start and end apart: 40, of which 37 were waited for; matrix products, arithmetic and copies ran while one was open for 0% of the time, Pallas kernels for 7%

profile of v4, /device:TPU:0, one launch (start us, length us, event | category | flops | bytes accessed | tf_op | source)
XLA Modules:
  0.0 105.3 jit_solution(7853045717463044576)
XLA Ops:
  0.0 4.0 %begin.1 = (f32[64,8,2048]{2,1,0:T(8,128)S(1)}, f32[64,8,2048]{2,1,0:T(8,128)S(1)}, f32[8,2048]{1,0:T(8,128)S(1)}, f32[8,2048]{1,0:T(8,128)S(1)}, f32[8,2048]{1,...) custom-call(f32[512,2048]{1,0:T(8,128)} %signal_hbm.1, f32[512,2048]{1,0:T(8,128)} %jumps_hbm.1, ...), custom_call_target="tpu_custom_call" | custom-call | tf_op jit(solution)/shard_map/begin/pallas_call | solution.py:294
  5.4 4.8 %collective-permute-start.1 = (f32[1,2048]{1,0:T(1,128)S(1)}, f32[1,2048]{1,0:T(1,128)S(1)}, u32[]{:S(2)}, u32[]{:S(2)}) collective-permute-start(f32[1,2048]{1,0:T(1,128)S(1)} %get-tuple-element.115), channel_id=1, source_target_pairs={{0,13},{1,12},{4,9},{5,8},{8,5},{9,4},{12,1},{13,0},{2,15},{3,14},... | collective-permute-start | bytes 24584 | tf_op jit(solution)/shard_map/ppermute | solution.py:343
  12.1 2.0 %collective-permute-done.2.refs_1_ = f32[1,2048]{1,0:T(1,128)S(1)} collective-permute-done((f32[1,2048]{1,0:T(1,128)S(1)}, f32[1,2048]{1,0:T(1,128)S(1)}, u32[]{:S(2)}, u32[]{:S(2)}) %collective-permute-start.2) | collective-permute-done | bytes 8224 | tf_op jit(solution)/shard_map/ppermute | solution.py:343
  14.9 1.5 %collective-permute-start.4 = (f32[8,128]{1,0:T(8,128)S(1)}, f32[8,128]{1,0:T(8,128)S(1)}, u32[]{:S(2)}, u32[]{:S(2)}) collective-permute-start(f32[8,128]{1,0:T(8,128)S(1)} %get-tuple-element.119.own_ref), channel_id=1, source_target_pairs={{0,2},{2,0},{1,3},{3,1},{4,6},{6,4},{5,7},{7,5},{8,10},{10,8},{9,1... | collective-permute-start | bytes 12296 | tf_op jit(solution)/shard_map/ppermute | solution.py:355
  16.4 2.1 %collective-permute-done.4.other_ref = f32[8,128]{1,0:T(8,128)S(1)} collective-permute-done((f32[8,128]{1,0:T(8,128)S(1)}, f32[8,128]{1,0:T(8,128)S(1)}, u32[]{:S(2)}, u32[]{:S(2)}) %collective-permute-start.4) | collective-permute-done | bytes 4128 | tf_op jit(solution)/shard_map/ppermute | solution.py:355
  22.3 2.1 %collective-permute-start.8 = (f32[1,2048]{1,0:T(1,128)S(1)}, f32[1,2048]{1,0:T(1,128)S(1)}, u32[]{:S(2)}, u32[]{:S(2)}) collective-permute-start(f32[1,2048]{1,0:T(1,128)S(1)} %get-tuple-element.130), channel_id=1, source_target_pairs={{0,5},{1,4},{4,1},{5,0},{8,13},{9,12},{12,9},{13,8},{2,7},{3,6},{6... | collective-permute-start | bytes 24584 | tf_op jit(solution)/shard_map/ppermute | solution.py:343
  26.5 1.5 %collective-permute-start.9 = (f32[8,128]{1,0:T(8,128)S(1)}, f32[8,128]{1,0:T(8,128)S(1)}, u32[]{:S(2)}, u32[]{:S(2)}) collective-permute-start(f32[8,128]{1,0:T(8,128)S(1)} %get-tuple-element.132.own_ref), channel_id=1, source_target_pairs={{0,2},{2,0},{1,3},{3,1},{4,6},{6,4},{5,7},{7,5},{8,10},{10,8},{9,1... | collective-permute-start | bytes 12296 | tf_op jit(solution)/shard_map/ppermute | solution.py:355
  28.1 2.1 %collective-permute-done.9.other_ref = f32[8,128]{1,0:T(8,128)S(1)} collective-permute-done((f32[8,128]{1,0:T(8,128)S(1)}, f32[8,128]{1,0:T(8,128)S(1)}, u32[]{:S(2)}, u32[]{:S(2)}) %collective-permute-start.9) | collective-permute-done | bytes 4128 | tf_op jit(solution)/shard_map/ppermute | solution.py:355
  32.1 2.1 %collective-permute-start.11 = (f32[1,2048]{1,0:T(1,128)S(1)}, f32[1,2048]{1,0:T(1,128)S(1)}, u32[]{:S(2)}, u32[]{:S(2)}) collective-permute-start(f32[1,2048]{1,0:T(1,128)S(1)} %get-tuple-element.140), channel_id=1, source_target_pairs={{0,13},{1,12},{4,9},{5,8},{8,5},{9,4},{12,1},{13,0},{2,15},{3,14},... | collective-permute-start | bytes 24584 | tf_op jit(solution)/shard_map/ppermute | solution.py:343
  39.0 1.5 %collective-permute-start.14 = (f32[8,128]{1,0:T(8,128)S(1)}, f32[8,128]{1,0:T(8,128)S(1)}, u32[]{:S(2)}, u32[]{:S(2)}) collective-permute-start(f32[8,128]{1,0:T(8,128)S(1)} %get-tuple-element.144.own_ref), channel_id=1, source_target_pairs={{0,2},{2,0},{1,3},{3,1},{4,6},{6,4},{5,7},{7,5},{8,10},{10,8},{9,1... | collective-permute-start | bytes 12296 | tf_op jit(solution)/shard_map/ppermute | solution.py:355
  40.5 2.1 %collective-permute-done.14.other_ref = f32[8,128]{1,0:T(8,128)S(1)} collective-permute-done((f32[8,128]{1,0:T(8,128)S(1)}, f32[8,128]{1,0:T(8,128)S(1)}, u32[]{:S(2)}, u32[]{:S(2)}) %collective-permute-start.14) | collective-permute-done | bytes 4128 | tf_op jit(solution)/shard_map/ppermute | solution.py:355
  46.8 1.6 %collective-permute-start.18 = (f32[1,2048]{1,0:T(1,128)S(1)}, f32[1,2048]{1,0:T(1,128)S(1)}, u32[]{:S(2)}, u32[]{:S(2)}) collective-permute-start(f32[1,2048]{1,0:T(1,128)S(1)} %get-tuple-element.154), channel_id=1, source_target_pairs={{0,5},{1,4},{4,1},{5,0},{8,13},{9,12},{12,9},{13,8},{2,7},{3,6},{6... | collective-permute-start | bytes 24584 | tf_op jit(solution)/shard_map/ppermute | solution.py:343
  50.6 1.5 %collective-permute-start.19 = (f32[8,128]{1,0:T(8,128)S(1)}, f32[8,128]{1,0:T(8,128)S(1)}, u32[]{:S(2)}, u32[]{:S(2)}) collective-permute-start(f32[8,128]{1,0:T(8,128)S(1)} %get-tuple-element.156.own_ref), channel_id=1, source_target_pairs={{0,2},{2,0},{1,3},{3,1},{4,6},{6,4},{5,7},{7,5},{8,10},{10,8},{9,1... | collective-permute-start | bytes 12296 | tf_op jit(solution)/shard_map/ppermute | solution.py:355
  52.2 2.1 %collective-permute-done.19.other_ref = f32[8,128]{1,0:T(8,128)S(1)} collective-permute-done((f32[8,128]{1,0:T(8,128)S(1)}, f32[8,128]{1,0:T(8,128)S(1)}, u32[]{:S(2)}, u32[]{:S(2)}) %collective-permute-start.19) | collective-permute-done | bytes 4128 | tf_op jit(solution)/shard_map/ppermute | solution.py:355
  56.1 2.1 %collective-permute-start.21 = (f32[1,2048]{1,0:T(1,128)S(1)}, f32[1,2048]{1,0:T(1,128)S(1)}, u32[]{:S(2)}, u32[]{:S(2)}) collective-permute-start(f32[1,2048]{1,0:T(1,128)S(1)} %get-tuple-element.164), channel_id=1, source_target_pairs={{0,13},{1,12},{4,9},{5,8},{8,5},{9,4},{12,1},{13,0},{2,15},{3,14},... | collective-permute-start | bytes 24584 | tf_op jit(solution)/shard_map/ppermute | solution.py:343
  63.2 1.5 %collective-permute-start.24 = (f32[8,128]{1,0:T(8,128)S(1)}, f32[8,128]{1,0:T(8,128)S(1)}, u32[]{:S(2)}, u32[]{:S(2)}) collective-permute-start(f32[8,128]{1,0:T(8,128)S(1)} %get-tuple-element.168.own_ref), channel_id=1, source_target_pairs={{0,2},{2,0},{1,3},{3,1},{4,6},{6,4},{5,7},{7,5},{8,10},{10,8},{9,1... | collective-permute-start | bytes 12296 | tf_op jit(solution)/shard_map/ppermute | solution.py:355
  64.7 2.1 %collective-permute-done.24.other_ref = f32[8,128]{1,0:T(8,128)S(1)} collective-permute-done((f32[8,128]{1,0:T(8,128)S(1)}, f32[8,128]{1,0:T(8,128)S(1)}, u32[]{:S(2)}, u32[]{:S(2)}) %collective-permute-start.24) | collective-permute-done | bytes 4128 | tf_op jit(solution)/shard_map/ppermute | solution.py:355
  71.0 1.6 %collective-permute-start.28 = (f32[1,2048]{1,0:T(1,128)S(1)}, f32[1,2048]{1,0:T(1,128)S(1)}, u32[]{:S(2)}, u32[]{:S(2)}) collective-permute-start(f32[1,2048]{1,0:T(1,128)S(1)} %get-tuple-element.178), channel_id=1, source_target_pairs={{0,5},{1,4},{4,1},{5,0},{8,13},{9,12},{12,9},{13,8},{2,7},{3,6},{6... | collective-permute-start | bytes 24584 | tf_op jit(solution)/shard_map/ppermute | solution.py:343
  76.4 2.1 %collective-permute-done.29.other_ref = f32[8,128]{1,0:T(8,128)S(1)} collective-permute-done((f32[8,128]{1,0:T(8,128)S(1)}, f32[8,128]{1,0:T(8,128)S(1)}, u32[]{:S(2)}, u32[]{:S(2)}) %collective-permute-start.29) | collective-permute-done | bytes 4128 | tf_op jit(solution)/shard_map/ppermute | solution.py:355
  80.4 2.1 %collective-permute-start.31 = (f32[1,2048]{1,0:T(1,128)S(1)}, f32[1,2048]{1,0:T(1,128)S(1)}, u32[]{:S(2)}, u32[]{:S(2)}) collective-permute-start(f32[1,2048]{1,0:T(1,128)S(1)} %get-tuple-element.188), channel_id=1, source_target_pairs={{0,13},{1,12},{4,9},{5,8},{8,5},{9,4},{12,1},{13,0},{2,15},{3,14},... | collective-permute-start | bytes 24584 | tf_op jit(solution)/shard_map/ppermute | solution.py:343
  88.8 2.1 %collective-permute-done.34.other_ref = f32[8,128]{1,0:T(8,128)S(1)} collective-permute-done((f32[8,128]{1,0:T(8,128)S(1)}, f32[8,128]{1,0:T(8,128)S(1)}, u32[]{:S(2)}, u32[]{:S(2)}) %collective-permute-start.34) | collective-permute-done | bytes 4128 | tf_op jit(solution)/shard_map/ppermute | solution.py:355
  95.1 1.6 %collective-permute-start.38 = (f32[1,2048]{1,0:T(1,128)S(1)}, f32[1,2048]{1,0:T(1,128)S(1)}, u32[]{:S(2)}, u32[]{:S(2)}) collective-permute-start(f32[1,2048]{1,0:T(1,128)S(1)} %get-tuple-element.202), channel_id=1, source_target_pairs={{0,5},{1,4},{4,1},{5,0},{8,13},{9,12},{12,9},{13,8},{2,7},{3,6},{6... | collective-permute-start | bytes 24584 | tf_op jit(solution)/shard_map/ppermute | solution.py:343
  100.5 2.1 %collective-permute-done.39.other_ref = f32[8,128]{1,0:T(8,128)S(1)} collective-permute-done((f32[8,128]{1,0:T(8,128)S(1)}, f32[8,128]{1,0:T(8,128)S(1)}, u32[]{:S(2)}, u32[]{:S(2)}) %collective-permute-start.39) | collective-permute-done | bytes 4128 | tf_op jit(solution)/shard_map/ppermute | solution.py:355
  102.6 2.5 %finish.1 = f32[512,2048]{1,0:T(8,128)} custom-call(f32[8,128]{1,0:T(8,128)S(1)} %get-tuple-element.203.own_ref, f32[8,128]{1,0:T(8,128)S(1)} %collective-permute-done.39.other_ref, f32[8,128]{1,0:T(8,128)S(1)} %get-tuple-element.120.limits_ref, f32[64,8,2048]{2,1,0:T(8,128)S(1)} %get-tuple-element.204.state_ref), custom_call_target="tpu_custom_call" | custom-call | tf_op jit(solution)/shard_map/finish/pallas_call | solution.py:294
  (90 shorter events, 53.7 us)
Async XLA Ops:
  5.4 6.7 %collective-permute-start.1 = (f32[1,2048]{1,0:T(1,128)S(1)}, f32[1,2048]{1,0:T(1,128)S(1)}, u32[]{:S(2)}, u32[]{:S(2)}) collective-permute-start(f32[1,2048]{1,0:T(1,128)S(1)} %get-tuple-element.115), channel_id=1, source_target_pairs={{0,13},{1,12},{4,9},{5,8},{8,5},{9,4},{12,1},{13,0},{2,15},{3,14},... | collective-permute-start | bytes 24584 | tf_op jit(solution)/shard_map/ppermute | solution.py:343
  10.2 4.0 %collective-permute-start.2 = (f32[1,2048]{1,0:T(1,128)S(1)}, f32[1,2048]{1,0:T(1,128)S(1)}, u32[]{:S(2)}, u32[]{:S(2)}) collective-permute-start(f32[1,2048]{1,0:T(1,128)S(1)} %get-tuple-element.116), channel_id=1, source_target_pairs={{0,9},{1,8},{4,13},{5,12},{8,1},{9,0},{12,5},{13,4},{2,11},{3,10},... | collective-permute-start | bytes 24584 | tf_op jit(solution)/shard_map/ppermute | solution.py:343
  10.2 4.0 %collective-permute-start.3 = (f32[1,2048]{1,0:T(1,128)S(1)}, f32[1,2048]{1,0:T(1,128)S(1)}, u32[]{:S(2)}, u32[]{:S(2)}) collective-permute-start(f32[1,2048]{1,0:T(1,128)S(1)} %get-tuple-element.117), channel_id=1, source_target_pairs={{0,5},{1,4},{4,1},{5,0},{8,13},{9,12},{12,9},{13,8},{2,7},{3,6},{6... | collective-permute-start | bytes 24584 | tf_op jit(solution)/shard_map/ppermute | solution.py:343
  14.9 3.7 %collective-permute-start.4 = (f32[8,128]{1,0:T(8,128)S(1)}, f32[8,128]{1,0:T(8,128)S(1)}, u32[]{:S(2)}, u32[]{:S(2)}) collective-permute-start(f32[8,128]{1,0:T(8,128)S(1)} %get-tuple-element.119.own_ref), channel_id=1, source_target_pairs={{0,2},{2,0},{1,3},{3,1},{4,6},{6,4},{5,7},{7,5},{8,10},{10,8},{9,1... | collective-permute-start | bytes 12296 | tf_op jit(solution)/shard_map/ppermute | solution.py:355
  20.4 4.9 %collective-permute-start.6 = (f32[1,2048]{1,0:T(1,128)S(1)}, f32[1,2048]{1,0:T(1,128)S(1)}, u32[]{:S(2)}, u32[]{:S(2)}) collective-permute-start(f32[1,2048]{1,0:T(1,128)S(1)} %get-tuple-element.128), channel_id=1, source_target_pairs={{0,13},{1,12},{4,9},{5,8},{8,5},{9,4},{12,1},{13,0},{2,15},{3,14},... | collective-permute-start | bytes 24584 | tf_op jit(solution)/shard_map/ppermute | solution.py:343
  21.7 4.1 %collective-permute-start.7 = (f32[1,2048]{1,0:T(1,128)S(1)}, f32[1,2048]{1,0:T(1,128)S(1)}, u32[]{:S(2)}, u32[]{:S(2)}) collective-permute-start(f32[1,2048]{1,0:T(1,128)S(1)} %get-tuple-element.129), channel_id=1, source_target_pairs={{0,9},{1,8},{4,13},{5,12},{8,1},{9,0},{12,5},{13,4},{2,11},{3,10},... | collective-permute-start | bytes 24584 | tf_op jit(solution)/shard_map/ppermute | solution.py:343
  26.5 3.7 %collective-permute-start.9 = (f32[8,128]{1,0:T(8,128)S(1)}, f32[8,128]{1,0:T(8,128)S(1)}, u32[]{:S(2)}, u32[]{:S(2)}) collective-permute-start(f32[8,128]{1,0:T(8,128)S(1)} %get-tuple-element.132.own_ref), channel_id=1, source_target_pairs={{0,2},{2,0},{1,3},{3,1},{4,6},{6,4},{5,7},{7,5},{8,10},{10,8},{9,1... | collective-permute-start | bytes 12296 | tf_op jit(solution)/shard_map/ppermute | solution.py:355
  32.1 4.9 %collective-permute-start.11 = (f32[1,2048]{1,0:T(1,128)S(1)}, f32[1,2048]{1,0:T(1,128)S(1)}, u32[]{:S(2)}, u32[]{:S(2)}) collective-permute-start(f32[1,2048]{1,0:T(1,128)S(1)} %get-tuple-element.140), channel_id=1, source_target_pairs={{0,13},{1,12},{4,9},{5,8},{8,5},{9,4},{12,1},{13,0},{2,15},{3,14},... | collective-permute-start | bytes 24584 | tf_op jit(solution)/shard_map/ppermute | solution.py:343
  34.2 4.0 %collective-permute-start.12 = (f32[1,2048]{1,0:T(1,128)S(1)}, f32[1,2048]{1,0:T(1,128)S(1)}, u32[]{:S(2)}, u32[]{:S(2)}) collective-permute-start(f32[1,2048]{1,0:T(1,128)S(1)} %get-tuple-element.141), channel_id=1, source_target_pairs={{0,9},{1,8},{4,13},{5,12},{8,1},{9,0},{12,5},{13,4},{2,11},{3,10},... | collective-permute-start | bytes 24584 | tf_op jit(solution)/shard_map/ppermute | solution.py:343
  39.0 3.7 %collective-permute-start.14 = (f32[8,128]{1,0:T(8,128)S(1)}, f32[8,128]{1,0:T(8,128)S(1)}, u32[]{:S(2)}, u32[]{:S(2)}) collective-permute-start(f32[8,128]{1,0:T(8,128)S(1)} %get-tuple-element.144.own_ref), channel_id=1, source_target_pairs={{0,2},{2,0},{1,3},{3,1},{4,6},{6,4},{5,7},{7,5},{8,10},{10,8},{9,1... | collective-permute-start | bytes 12296 | tf_op jit(solution)/shard_map/ppermute | solution.py:355
  44.5 4.9 %collective-permute-start.16 = (f32[1,2048]{1,0:T(1,128)S(1)}, f32[1,2048]{1,0:T(1,128)S(1)}, u32[]{:S(2)}, u32[]{:S(2)}) collective-permute-start(f32[1,2048]{1,0:T(1,128)S(1)} %get-tuple-element.152), channel_id=1, source_target_pairs={{0,13},{1,12},{4,9},{5,8},{8,5},{9,4},{12,1},{13,0},{2,15},{3,14},... | collective-permute-start | bytes 24584 | tf_op jit(solution)/shard_map/ppermute | solution.py:343
  45.9 4.0 %collective-permute-start.17 = (f32[1,2048]{1,0:T(1,128)S(1)}, f32[1,2048]{1,0:T(1,128)S(1)}, u32[]{:S(2)}, u32[]{:S(2)}) collective-permute-start(f32[1,2048]{1,0:T(1,128)S(1)} %get-tuple-element.153), channel_id=1, source_target_pairs={{0,9},{1,8},{4,13},{5,12},{8,1},{9,0},{12,5},{13,4},{2,11},{3,10},... | collective-permute-start | bytes 24584 | tf_op jit(solution)/shard_map/ppermute | solution.py:343
  50.6 3.7 %collective-permute-start.19 = (f32[8,128]{1,0:T(8,128)S(1)}, f32[8,128]{1,0:T(8,128)S(1)}, u32[]{:S(2)}, u32[]{:S(2)}) collective-permute-start(f32[8,128]{1,0:T(8,128)S(1)} %get-tuple-element.156.own_ref), channel_id=1, source_target_pairs={{0,2},{2,0},{1,3},{3,1},{4,6},{6,4},{5,7},{7,5},{8,10},{10,8},{9,1... | collective-permute-start | bytes 12296 | tf_op jit(solution)/shard_map/ppermute | solution.py:355
  56.1 4.9 %collective-permute-start.21 = (f32[1,2048]{1,0:T(1,128)S(1)}, f32[1,2048]{1,0:T(1,128)S(1)}, u32[]{:S(2)}, u32[]{:S(2)}) collective-permute-start(f32[1,2048]{1,0:T(1,128)S(1)} %get-tuple-element.164), channel_id=1, source_target_pairs={{0,13},{1,12},{4,9},{5,8},{8,5},{9,4},{12,1},{13,0},{2,15},{3,14},... | collective-permute-start | bytes 24584 | tf_op jit(solution)/shard_map/ppermute | solution.py:343
  58.2 4.0 %collective-permute-start.22 = (f32[1,2048]{1,0:T(1,128)S(1)}, f32[1,2048]{1,0:T(1,128)S(1)}, u32[]{:S(2)}, u32[]{:S(2)}) collective-permute-start(f32[1,2048]{1,0:T(1,128)S(1)} %get-tuple-element.165), channel_id=1, source_target_pairs={{0,9},{1,8},{4,13},{5,12},{8,1},{9,0},{12,5},{13,4},{2,11},{3,10},... | collective-permute-start | bytes 24584 | tf_op jit(solution)/shard_map/ppermute | solution.py:343
  63.2 3.7 %collective-permute-start.24 = (f32[8,128]{1,0:T(8,128)S(1)}, f32[8,128]{1,0:T(8,128)S(1)}, u32[]{:S(2)}, u32[]{:S(2)}) collective-permute-start(f32[8,128]{1,0:T(8,128)S(1)} %get-tuple-element.168.own_ref), channel_id=1, source_target_pairs={{0,2},{2,0},{1,3},{3,1},{4,6},{6,4},{5,7},{7,5},{8,10},{10,8},{9,1... | collective-permute-start | bytes 12296 | tf_op jit(solution)/shard_map/ppermute | solution.py:355
  68.7 4.9 %collective-permute-start.26 = (f32[1,2048]{1,0:T(1,128)S(1)}, f32[1,2048]{1,0:T(1,128)S(1)}, u32[]{:S(2)}, u32[]{:S(2)}) collective-permute-start(f32[1,2048]{1,0:T(1,128)S(1)} %get-tuple-element.176), channel_id=1, source_target_pairs={{0,13},{1,12},{4,9},{5,8},{8,5},{9,4},{12,1},{13,0},{2,15},{3,14},... | collective-permute-start | bytes 24584 | tf_op jit(solution)/shard_map/ppermute | solution.py:343
  70.1 4.0 %collective-permute-start.27 = (f32[1,2048]{1,0:T(1,128)S(1)}, f32[1,2048]{1,0:T(1,128)S(1)}, u32[]{:S(2)}, u32[]{:S(2)}) collective-permute-start(f32[1,2048]{1,0:T(1,128)S(1)} %get-tuple-element.177), channel_id=1, source_target_pairs={{0,9},{1,8},{4,13},{5,12},{8,1},{9,0},{12,5},{13,4},{2,11},{3,10},... | collective-permute-start | bytes 24584 | tf_op jit(solution)/shard_map/ppermute | solution.py:343
  74.9 3.7 %collective-permute-start.29 = (f32[8,128]{1,0:T(8,128)S(1)}, f32[8,128]{1,0:T(8,128)S(1)}, u32[]{:S(2)}, u32[]{:S(2)}) collective-permute-start(f32[8,128]{1,0:T(8,128)S(1)} %get-tuple-element.180.own_ref), channel_id=1, source_target_pairs={{0,2},{2,0},{1,3},{3,1},{4,6},{6,4},{5,7},{7,5},{8,10},{10,8},{9,1... | collective-permute-start | bytes 12296 | tf_op jit(solution)/shard_map/ppermute | solution.py:355
  80.4 4.9 %collective-permute-start.31 = (f32[1,2048]{1,0:T(1,128)S(1)}, f32[1,2048]{1,0:T(1,128)S(1)}, u32[]{:S(2)}, u32[]{:S(2)}) collective-permute-start(f32[1,2048]{1,0:T(1,128)S(1)} %get-tuple-element.188), channel_id=1, source_target_pairs={{0,13},{1,12},{4,9},{5,8},{8,5},{9,4},{12,1},{13,0},{2,15},{3,14},... | collective-permute-start | bytes 24584 | tf_op jit(solution)/shard_map/ppermute | solution.py:343
  82.5 4.0 %collective-permute-start.32 = (f32[1,2048]{1,0:T(1,128)S(1)}, f32[1,2048]{1,0:T(1,128)S(1)}, u32[]{:S(2)}, u32[]{:S(2)}) collective-permute-start(f32[1,2048]{1,0:T(1,128)S(1)} %get-tuple-element.189), channel_id=1, source_target_pairs={{0,9},{1,8},{4,13},{5,12},{8,1},{9,0},{12,5},{13,4},{2,11},{3,10},... | collective-permute-start | bytes 24584 | tf_op jit(solution)/shard_map/ppermute | solution.py:343
  92.8 4.9 %collective-permute-start.36 = (f32[1,2048]{1,0:T(1,128)S(1)}, f32[1,2048]{1,0:T(1,128)S(1)}, u32[]{:S(2)}, u32[]{:S(2)}) collective-permute-start(f32[1,2048]{1,0:T(1,128)S(1)} %get-tuple-element.200), channel_id=1, source_target_pairs={{0,13},{1,12},{4,9},{5,8},{8,5},{9,4},{12,1},{13,0},{2,15},{3,14},... | collective-permute-start | bytes 24584 | tf_op jit(solution)/shard_map/ppermute | solution.py:343
  94.2 4.0 %collective-permute-start.37 = (f32[1,2048]{1,0:T(1,128)S(1)}, f32[1,2048]{1,0:T(1,128)S(1)}, u32[]{:S(2)}, u32[]{:S(2)}) collective-permute-start(f32[1,2048]{1,0:T(1,128)S(1)} %get-tuple-element.201), channel_id=1, source_target_pairs={{0,9},{1,8},{4,13},{5,12},{8,1},{9,0},{12,5},{13,4},{2,11},{3,10},... | collective-permute-start | bytes 24584 | tf_op jit(solution)/shard_map/ppermute | solution.py:343
  98.9 3.7 %collective-permute-start.39 = (f32[8,128]{1,0:T(8,128)S(1)}, f32[8,128]{1,0:T(8,128)S(1)}, u32[]{:S(2)}, u32[]{:S(2)}) collective-permute-start(f32[8,128]{1,0:T(8,128)S(1)} %get-tuple-element.203.own_ref), channel_id=1, source_target_pairs={{0,2},{2,0},{1,3},{3,1},{4,6},{6,4},{5,7},{7,5},{8,10},{10,8},{9,1... | collective-permute-start | bytes 12296 | tf_op jit(solution)/shard_map/ppermute | solution.py:355
  (16 other events, 36.1 us)

commit v5 on v4

--- a/solution.py
+++ b/solution.py
@@ -126,16 +126,20 @@
         lax.fori_loop(0, depth // BATCH, step, [zero] * len(group))
 
 
-def shrink(own_ref, other_ref, limits_ref, factor_ref):
+def row_factors(own_ref, other_ref, limits_ref):
     squares = own_ref[...] + other_ref[...]
-    factor = jnp.maximum(0.0, 1.0 - limits_ref[...] / jnp.sqrt(squares + 1e-06))
-    for k in range(factor_ref.shape[0]):
-        factor_ref[k] = jnp.broadcast_to(factor[:, k : k + 1], (SUBLANES, LANES))
+    return jnp.maximum(0.0, 1.0 - limits_ref[...] / jnp.sqrt(squares + 1e-06))
+
+
+def spread(factor, k):
+    return jnp.broadcast_to(factor[:, k : k + 1], (SUBLANES, LANES))
 
 
 def sums_kernel(own_ref, other_ref, limits_ref, state_ref, minus_ref, factor_ref, totals_ref, weighted_ref, message_ref):
     depth, _, cols = state_ref.shape
-    shrink(own_ref, other_ref, limits_ref, factor_ref)
+    factor = row_factors(own_ref, other_ref, limits_ref)
+    for k in range(depth):
+        factor_ref[k] = spread(factor, k)
     zero = jnp.zeros((SUBLANES, LANES), jnp.float32)
     totals, weights = [], []
     for group in groups(cols, WIDTH):
@@ -250,25 +254,18 @@
     squares_ref[...] = (sums[0] + sums[1]) + (sums[2] + sums[3])
 
 
-def end_kernel(cuts, own_ref, other_ref, limits_ref, state_ref, out_hbm, factor_ref, jumps_ref, sems):
+def end_kernel(cuts, own_ref, other_ref, limits_ref, state_ref, out_hbm, jumps_ref, sems):
     depth, _, cols = state_ref.shape
-    shrink(own_ref, other_ref, limits_ref, factor_ref)
+    factor = row_factors(own_ref, other_ref, limits_ref)
     copies = []
     for part in range(len(cuts) - 1):
         low, high = cuts[part], cuts[part + 1]
-        for group in groups(cols, WIDTH):
-
-            def step(i, carry, low=low, group=group):
-                results = []
-                for q in range(BATCH):
-                    k = low + i * BATCH + q
-                    factor = factor_ref[k]
-                    results += [(k, c, state_ref[k, :, c] * factor) for c in group]
+        for start in range(low, high, BATCH):
+            rows = [(k, spread(factor, k)) for k in range(start, start + BATCH)]
+            for group in groups(cols, WIDTH):
+                results = [(k, c, state_ref[k, :, c] * row) for k, row in rows for c in group]
                 for k, c, value in results:
                     jumps_ref[k, :, c] = value
-                return carry
-
-            lax.fori_loop(0, (high - low) // BATCH, step, 0)
         for s in range(SUBLANES):
             copy = pltpu.make_async_copy(
                 jumps_ref.at[pl.ds(low, high - low), s, :], out_hbm.at[pl.ds(s * depth + low, high - low), :],
@@ -317,8 +314,8 @@
 
     block = vmem(depth, SUBLANES, cols)
     strip, line, pair = vmem(SUBLANES, cols), vmem(SUBLANES, LANES), vmem(2, cols)
-    spread = vmem(depth, SUBLANES, LANES)
-    begin_cuts = (0, depth // 8 * 5, depth)
+    factors = vmem(depth, SUBLANES, LANES)
+    begin_cuts = (0, depth // 4 * 3, depth)
     end_cuts = tuple(depth // 8 * i for i in (0, 1, 3, 5, 8))
 
     state, signals, minus, totals, weighted, message, limits, marks = call(
@@ -334,7 +331,7 @@
     for iteration in range(ITERS):
         if iteration:
             factor, totals, weighted, message = call(
-                sums_kernel, "sums", [own, other, limits, state, minus], [spread, strip, strip, pair], kept=(3, 4)
+                sums_kernel, "sums", [own, other, limits, state, minus], [factors, strip, strip, pair], kept=(3, 4)
             )
         sibling = lax.ppermute(message, "sub", swap)
         routed = call(
@@ -358,7 +355,7 @@
     return call(
         functools.partial(end_kernel, end_cuts), "finish", [own, other, limits, state], jax.ShapeDtypeStruct((rows, cols), jnp.float32), kept=(3,),
         hbm_out=True,
-        scratch=[spread, block, pltpu.SemaphoreType.DMA((len(end_cuts) - 1, SUBLANES))],
+        scratch=[block, pltpu.SemaphoreType.DMA((len(end_cuts) - 1, SUBLANES))],
     )
 
 

time: 105 us -> 105 us (level)
  no operation moved by 1% of the time
where the time goes in v5:
time: 105 us
  starting transfers between devices  46.4 us (44%)
  waiting for transfers between devices  34.2 us (33%)
  Pallas kernels  24.1 us (23%)
    ppermute x24, starting transfers between devices, local(): lax.ppermute(x, ('probe', 'sub'), routes[k])  33 us
    pallas_call x34, Pallas kernels, call(): pl.pallas_call(kernel, out_shape=outs, in_specs=[in_hbm if i in hbm else...  24.1 us
    ppermute x8, waiting for transfers between devices, local(): other = lax.ppermute(own, 'prof', swap)  16.9 us
    ppermute x8, starting transfers between devices, local(): other = lax.ppermute(own, 'prof', swap)  12.4 us
    ppermute x8, waiting for transfers between devices, local(): sibling = lax.ppermute(message, 'sub', swap)  9.03 us
    ppermute x24, waiting for transfers between devices, local(): lax.ppermute(x, ('probe', 'sub'), routes[k])  8.26 us
  transfers between devices with their start and end apart: 40, of which 37 were waited for; matrix products, arithmetic and copies ran while one was open for 0% of the time, Pallas kernels for 7%

profile of v5, /device:TPU:0, one launch (start us, length us, event | category | flops | bytes accessed | tf_op | source)
XLA Modules:
  0.0 105.0 jit_solution(15838344318166639586)
XLA Ops:
  0.0 3.9 %begin.1 = (f32[64,8,2048]{2,1,0:T(8,128)S(1)}, f32[64,8,2048]{2,1,0:T(8,128)S(1)}, f32[8,2048]{1,0:T(8,128)S(1)}, f32[8,2048]{1,0:T(8,128)S(1)}, f32[8,2048]{1,...) custom-call(f32[512,2048]{1,0:T(8,128)} %signal_hbm.1, f32[512,2048]{1,0:T(8,128)} %jumps_hbm.1, ...), custom_call_target="tpu_custom_call" | custom-call | tf_op jit(solution)/shard_map/begin/pallas_call | solution.py:291
  5.3 4.8 %collective-permute-start.1 = (f32[1,2048]{1,0:T(1,128)S(1)}, f32[1,2048]{1,0:T(1,128)S(1)}, u32[]{:S(2)}, u32[]{:S(2)}) collective-permute-start(f32[1,2048]{1,0:T(1,128)S(1)} %get-tuple-element.115), channel_id=1, source_target_pairs={{0,13},{1,12},{4,9},{5,8},{8,5},{9,4},{12,1},{13,0},{2,15},{3,14},... | collective-permute-start | bytes 24584 | tf_op jit(solution)/shard_map/ppermute | solution.py:340
  12.0 2.0 %collective-permute-done.2.refs_1_ = f32[1,2048]{1,0:T(1,128)S(1)} collective-permute-done((f32[1,2048]{1,0:T(1,128)S(1)}, f32[1,2048]{1,0:T(1,128)S(1)}, u32[]{:S(2)}, u32[]{:S(2)}) %collective-permute-start.2) | collective-permute-done | bytes 8224 | tf_op jit(solution)/shard_map/ppermute | solution.py:340
  14.8 1.5 %collective-permute-start.4 = (f32[8,128]{1,0:T(8,128)S(1)}, f32[8,128]{1,0:T(8,128)S(1)}, u32[]{:S(2)}, u32[]{:S(2)}) collective-permute-start(f32[8,128]{1,0:T(8,128)S(1)} %get-tuple-element.119.own_ref), channel_id=1, source_target_pairs={{0,2},{2,0},{1,3},{3,1},{4,6},{6,4},{5,7},{7,5},{8,10},{10,8},{9,1... | collective-permute-start | bytes 12296 | tf_op jit(solution)/shard_map/ppermute | solution.py:352
  16.3 2.1 %collective-permute-done.4.other_ref = f32[8,128]{1,0:T(8,128)S(1)} collective-permute-done((f32[8,128]{1,0:T(8,128)S(1)}, f32[8,128]{1,0:T(8,128)S(1)}, u32[]{:S(2)}, u32[]{:S(2)}) %collective-permute-start.4) | collective-permute-done | bytes 4128 | tf_op jit(solution)/shard_map/ppermute | solution.py:352
  22.2 2.1 %collective-permute-start.8 = (f32[1,2048]{1,0:T(1,128)S(1)}, f32[1,2048]{1,0:T(1,128)S(1)}, u32[]{:S(2)}, u32[]{:S(2)}) collective-permute-start(f32[1,2048]{1,0:T(1,128)S(1)} %get-tuple-element.130), channel_id=1, source_target_pairs={{0,5},{1,4},{4,1},{5,0},{8,13},{9,12},{12,9},{13,8},{2,7},{3,6},{6... | collective-permute-start | bytes 24584 | tf_op jit(solution)/shard_map/ppermute | solution.py:340
  26.4 1.5 %collective-permute-start.9 = (f32[8,128]{1,0:T(8,128)S(1)}, f32[8,128]{1,0:T(8,128)S(1)}, u32[]{:S(2)}, u32[]{:S(2)}) collective-permute-start(f32[8,128]{1,0:T(8,128)S(1)} %get-tuple-element.132.own_ref), channel_id=1, source_target_pairs={{0,2},{2,0},{1,3},{3,1},{4,6},{6,4},{5,7},{7,5},{8,10},{10,8},{9,1... | collective-permute-start | bytes 12296 | tf_op jit(solution)/shard_map/ppermute | solution.py:352
  28.0 2.1 %collective-permute-done.9.other_ref = f32[8,128]{1,0:T(8,128)S(1)} collective-permute-done((f32[8,128]{1,0:T(8,128)S(1)}, f32[8,128]{1,0:T(8,128)S(1)}, u32[]{:S(2)}, u32[]{:S(2)}) %collective-permute-start.9) | collective-permute-done | bytes 4128 | tf_op jit(solution)/shard_map/ppermute | solution.py:352
  32.0 2.1 %collective-permute-start.11 = (f32[1,2048]{1,0:T(1,128)S(1)}, f32[1,2048]{1,0:T(1,128)S(1)}, u32[]{:S(2)}, u32[]{:S(2)}) collective-permute-start(f32[1,2048]{1,0:T(1,128)S(1)} %get-tuple-element.140), channel_id=1, source_target_pairs={{0,13},{1,12},{4,9},{5,8},{8,5},{9,4},{12,1},{13,0},{2,15},{3,14},... | collective-permute-start | bytes 24584 | tf_op jit(solution)/shard_map/ppermute | solution.py:340
  40.4 2.1 %collective-permute-done.14.other_ref = f32[8,128]{1,0:T(8,128)S(1)} collective-permute-done((f32[8,128]{1,0:T(8,128)S(1)}, f32[8,128]{1,0:T(8,128)S(1)}, u32[]{:S(2)}, u32[]{:S(2)}) %collective-permute-start.14) | collective-permute-done | bytes 4128 | tf_op jit(solution)/shard_map/ppermute | solution.py:352
  46.7 1.6 %collective-permute-start.18 = (f32[1,2048]{1,0:T(1,128)S(1)}, f32[1,2048]{1,0:T(1,128)S(1)}, u32[]{:S(2)}, u32[]{:S(2)}) collective-permute-start(f32[1,2048]{1,0:T(1,128)S(1)} %get-tuple-element.154), channel_id=1, source_target_pairs={{0,5},{1,4},{4,1},{5,0},{8,13},{9,12},{12,9},{13,8},{2,7},{3,6},{6... | collective-permute-start | bytes 24584 | tf_op jit(solution)/shard_map/ppermute | solution.py:340
  50.5 1.5 %collective-permute-start.19 = (f32[8,128]{1,0:T(8,128)S(1)}, f32[8,128]{1,0:T(8,128)S(1)}, u32[]{:S(2)}, u32[]{:S(2)}) collective-permute-start(f32[8,128]{1,0:T(8,128)S(1)} %get-tuple-element.156.own_ref), channel_id=1, source_target_pairs={{0,2},{2,0},{1,3},{3,1},{4,6},{6,4},{5,7},{7,5},{8,10},{10,8},{9,1... | collective-permute-start | bytes 12296 | tf_op jit(solution)/shard_map/ppermute | solution.py:352
  52.1 2.1 %collective-permute-done.19.other_ref = f32[8,128]{1,0:T(8,128)S(1)} collective-permute-done((f32[8,128]{1,0:T(8,128)S(1)}, f32[8,128]{1,0:T(8,128)S(1)}, u32[]{:S(2)}, u32[]{:S(2)}) %collective-permute-start.19) | collective-permute-done | bytes 4128 | tf_op jit(solution)/shard_map/ppermute | solution.py:352
  56.0 2.1 %collective-permute-start.21 = (f32[1,2048]{1,0:T(1,128)S(1)}, f32[1,2048]{1,0:T(1,128)S(1)}, u32[]{:S(2)}, u32[]{:S(2)}) collective-permute-start(f32[1,2048]{1,0:T(1,128)S(1)} %get-tuple-element.164), channel_id=1, source_target_pairs={{0,13},{1,12},{4,9},{5,8},{8,5},{9,4},{12,1},{13,0},{2,15},{3,14},... | collective-permute-start | bytes 24584 | tf_op jit(solution)/shard_map/ppermute | solution.py:340
  63.1 1.5 %collective-permute-start.24 = (f32[8,128]{1,0:T(8,128)S(1)}, f32[8,128]{1,0:T(8,128)S(1)}, u32[]{:S(2)}, u32[]{:S(2)}) collective-permute-start(f32[8,128]{1,0:T(8,128)S(1)} %get-tuple-element.168.own_ref), channel_id=1, source_target_pairs={{0,2},{2,0},{1,3},{3,1},{4,6},{6,4},{5,7},{7,5},{8,10},{10,8},{9,1... | collective-permute-start | bytes 12296 | tf_op jit(solution)/shard_map/ppermute | solution.py:352
  64.6 2.1 %collective-permute-done.24.other_ref = f32[8,128]{1,0:T(8,128)S(1)} collective-permute-done((f32[8,128]{1,0:T(8,128)S(1)}, f32[8,128]{1,0:T(8,128)S(1)}, u32[]{:S(2)}, u32[]{:S(2)}) %collective-permute-start.24) | collective-permute-done | bytes 4128 | tf_op jit(solution)/shard_map/ppermute | solution.py:352
  70.9 1.6 %collective-permute-start.28 = (f32[1,2048]{1,0:T(1,128)S(1)}, f32[1,2048]{1,0:T(1,128)S(1)}, u32[]{:S(2)}, u32[]{:S(2)}) collective-permute-start(f32[1,2048]{1,0:T(1,128)S(1)} %get-tuple-element.178), channel_id=1, source_target_pairs={{0,5},{1,4},{4,1},{5,0},{8,13},{9,12},{12,9},{13,8},{2,7},{3,6},{6... | collective-permute-start | bytes 24584 | tf_op jit(solution)/shard_map/ppermute | solution.py:340
  74.8 1.5 %collective-permute-start.29 = (f32[8,128]{1,0:T(8,128)S(1)}, f32[8,128]{1,0:T(8,128)S(1)}, u32[]{:S(2)}, u32[]{:S(2)}) collective-permute-start(f32[8,128]{1,0:T(8,128)S(1)} %get-tuple-element.180.own_ref), channel_id=1, source_target_pairs={{0,2},{2,0},{1,3},{3,1},{4,6},{6,4},{5,7},{7,5},{8,10},{10,8},{9,1... | collective-permute-start | bytes 12296 | tf_op jit(solution)/shard_map/ppermute | solution.py:352
  76.3 2.1 %collective-permute-done.29.other_ref = f32[8,128]{1,0:T(8,128)S(1)} collective-permute-done((f32[8,128]{1,0:T(8,128)S(1)}, f32[8,128]{1,0:T(8,128)S(1)}, u32[]{:S(2)}, u32[]{:S(2)}) %collective-permute-start.29) | collective-permute-done | bytes 4128 | tf_op jit(solution)/shard_map/ppermute | solution.py:352
  80.3 2.1 %collective-permute-start.31 = (f32[1,2048]{1,0:T(1,128)S(1)}, f32[1,2048]{1,0:T(1,128)S(1)}, u32[]{:S(2)}, u32[]{:S(2)}) collective-permute-start(f32[1,2048]{1,0:T(1,128)S(1)} %get-tuple-element.188), channel_id=1, source_target_pairs={{0,13},{1,12},{4,9},{5,8},{8,5},{9,4},{12,1},{13,0},{2,15},{3,14},... | collective-permute-start | bytes 24584 | tf_op jit(solution)/shard_map/ppermute | solution.py:340
  88.7 2.1 %collective-permute-done.34.other_ref = f32[8,128]{1,0:T(8,128)S(1)} collective-permute-done((f32[8,128]{1,0:T(8,128)S(1)}, f32[8,128]{1,0:T(8,128)S(1)}, u32[]{:S(2)}, u32[]{:S(2)}) %collective-permute-start.34) | collective-permute-done | bytes 4128 | tf_op jit(solution)/shard_map/ppermute | solution.py:352
  95.0 1.6 %collective-permute-start.38 = (f32[1,2048]{1,0:T(1,128)S(1)}, f32[1,2048]{1,0:T(1,128)S(1)}, u32[]{:S(2)}, u32[]{:S(2)}) collective-permute-start(f32[1,2048]{1,0:T(1,128)S(1)} %get-tuple-element.202), channel_id=1, source_target_pairs={{0,5},{1,4},{4,1},{5,0},{8,13},{9,12},{12,9},{13,8},{2,7},{3,6},{6... | collective-permute-start | bytes 24584 | tf_op jit(solution)/shard_map/ppermute | solution.py:340
  100.4 2.1 %collective-permute-done.39.other_ref = f32[8,128]{1,0:T(8,128)S(1)} collective-permute-done((f32[8,128]{1,0:T(8,128)S(1)}, f32[8,128]{1,0:T(8,128)S(1)}, u32[]{:S(2)}, u32[]{:S(2)}) %collective-permute-start.39) | collective-permute-done | bytes 4128 | tf_op jit(solution)/shard_map/ppermute | solution.py:352
  102.5 2.4 %finish.1 = f32[512,2048]{1,0:T(8,128)} custom-call(f32[8,128]{1,0:T(8,128)S(1)} %get-tuple-element.203.own_ref, f32[8,128]{1,0:T(8,128)S(1)} %collective-permute-done.39.other_ref, f32[8,128]{1,0:T(8,128)S(1)} %get-tuple-element.120.limits_ref, f32[64,8,2048]{2,1,0:T(8,128)S(1)} %get-tuple-element.204.state_ref), custom_call_target="tpu_custom_call" | custom-call | tf_op jit(solution)/shard_map/finish/pallas_call | solution.py:291
  (90 shorter events, 53.7 us)
Async XLA Ops:
  5.3 6.7 %collective-permute-start.1 = (f32[1,2048]{1,0:T(1,128)S(1)}, f32[1,2048]{1,0:T(1,128)S(1)}, u32[]{:S(2)}, u32[]{:S(2)}) collective-permute-start(f32[1,2048]{1,0:T(1,128)S(1)} %get-tuple-element.115), channel_id=1, source_target_pairs={{0,13},{1,12},{4,9},{5,8},{8,5},{9,4},{12,1},{13,0},{2,15},{3,14},... | collective-permute-start | bytes 24584 | tf_op jit(solution)/shard_map/ppermute | solution.py:340
  10.1 4.0 %collective-permute-start.2 = (f32[1,2048]{1,0:T(1,128)S(1)}, f32[1,2048]{1,0:T(1,128)S(1)}, u32[]{:S(2)}, u32[]{:S(2)}) collective-permute-start(f32[1,2048]{1,0:T(1,128)S(1)} %get-tuple-element.116), channel_id=1, source_target_pairs={{0,9},{1,8},{4,13},{5,12},{8,1},{9,0},{12,5},{13,4},{2,11},{3,10},... | collective-permute-start | bytes 24584 | tf_op jit(solution)/shard_map/ppermute | solution.py:340
  10.1 4.0 %collective-permute-start.3 = (f32[1,2048]{1,0:T(1,128)S(1)}, f32[1,2048]{1,0:T(1,128)S(1)}, u32[]{:S(2)}, u32[]{:S(2)}) collective-permute-start(f32[1,2048]{1,0:T(1,128)S(1)} %get-tuple-element.117), channel_id=1, source_target_pairs={{0,5},{1,4},{4,1},{5,0},{8,13},{9,12},{12,9},{13,8},{2,7},{3,6},{6... | collective-permute-start | bytes 24584 | tf_op jit(solution)/shard_map/ppermute | solution.py:340
  14.8 3.7 %collective-permute-start.4 = (f32[8,128]{1,0:T(8,128)S(1)}, f32[8,128]{1,0:T(8,128)S(1)}, u32[]{:S(2)}, u32[]{:S(2)}) collective-permute-start(f32[8,128]{1,0:T(8,128)S(1)} %get-tuple-element.119.own_ref), channel_id=1, source_target_pairs={{0,2},{2,0},{1,3},{3,1},{4,6},{6,4},{5,7},{7,5},{8,10},{10,8},{9,1... | collective-permute-start | bytes 12296 | tf_op jit(solution)/shard_map/ppermute | solution.py:352
  20.3 4.9 %collective-permute-start.6 = (f32[1,2048]{1,0:T(1,128)S(1)}, f32[1,2048]{1,0:T(1,128)S(1)}, u32[]{:S(2)}, u32[]{:S(2)}) collective-permute-start(f32[1,2048]{1,0:T(1,128)S(1)} %get-tuple-element.128), channel_id=1, source_target_pairs={{0,13},{1,12},{4,9},{5,8},{8,5},{9,4},{12,1},{13,0},{2,15},{3,14},... | collective-permute-start | bytes 24584 | tf_op jit(solution)/shard_map/ppermute | solution.py:340
  21.6 4.1 %collective-permute-start.7 = (f32[1,2048]{1,0:T(1,128)S(1)}, f32[1,2048]{1,0:T(1,128)S(1)}, u32[]{:S(2)}, u32[]{:S(2)}) collective-permute-start(f32[1,2048]{1,0:T(1,128)S(1)} %get-tuple-element.129), channel_id=1, source_target_pairs={{0,9},{1,8},{4,13},{5,12},{8,1},{9,0},{12,5},{13,4},{2,11},{3,10},... | collective-permute-start | bytes 24584 | tf_op jit(solution)/shard_map/ppermute | solution.py:340
  26.4 3.7 %collective-permute-start.9 = (f32[8,128]{1,0:T(8,128)S(1)}, f32[8,128]{1,0:T(8,128)S(1)}, u32[]{:S(2)}, u32[]{:S(2)}) collective-permute-start(f32[8,128]{1,0:T(8,128)S(1)} %get-tuple-element.132.own_ref), channel_id=1, source_target_pairs={{0,2},{2,0},{1,3},{3,1},{4,6},{6,4},{5,7},{7,5},{8,10},{10,8},{9,1... | collective-permute-start | bytes 12296 | tf_op jit(solution)/shard_map/ppermute | solution.py:352
  32.0 4.9 %collective-permute-start.11 = (f32[1,2048]{1,0:T(1,128)S(1)}, f32[1,2048]{1,0:T(1,128)S(1)}, u32[]{:S(2)}, u32[]{:S(2)}) collective-permute-start(f32[1,2048]{1,0:T(1,128)S(1)} %get-tuple-element.140), channel_id=1, source_target_pairs={{0,13},{1,12},{4,9},{5,8},{8,5},{9,4},{12,1},{13,0},{2,15},{3,14},... | collective-permute-start | bytes 24584 | tf_op jit(solution)/shard_map/ppermute | solution.py:340
  34.1 4.0 %collective-permute-start.12 = (f32[1,2048]{1,0:T(1,128)S(1)}, f32[1,2048]{1,0:T(1,128)S(1)}, u32[]{:S(2)}, u32[]{:S(2)}) collective-permute-start(f32[1,2048]{1,0:T(1,128)S(1)} %get-tuple-element.141), channel_id=1, source_target_pairs={{0,9},{1,8},{4,13},{5,12},{8,1},{9,0},{12,5},{13,4},{2,11},{3,10},... | collective-permute-start | bytes 24584 | tf_op jit(solution)/shard_map/ppermute | solution.py:340
  38.9 3.7 %collective-permute-start.14 = (f32[8,128]{1,0:T(8,128)S(1)}, f32[8,128]{1,0:T(8,128)S(1)}, u32[]{:S(2)}, u32[]{:S(2)}) collective-permute-start(f32[8,128]{1,0:T(8,128)S(1)} %get-tuple-element.144.own_ref), channel_id=1, source_target_pairs={{0,2},{2,0},{1,3},{3,1},{4,6},{6,4},{5,7},{7,5},{8,10},{10,8},{9,1... | collective-permute-start | bytes 12296 | tf_op jit(solution)/shard_map/ppermute | solution.py:352
  44.4 4.9 %collective-permute-start.16 = (f32[1,2048]{1,0:T(1,128)S(1)}, f32[1,2048]{1,0:T(1,128)S(1)}, u32[]{:S(2)}, u32[]{:S(2)}) collective-permute-start(f32[1,2048]{1,0:T(1,128)S(1)} %get-tuple-element.152), channel_id=1, source_target_pairs={{0,13},{1,12},{4,9},{5,8},{8,5},{9,4},{12,1},{13,0},{2,15},{3,14},... | collective-permute-start | bytes 24584 | tf_op jit(solution)/shard_map/ppermute | solution.py:340
  45.8 4.0 %collective-permute-start.17 = (f32[1,2048]{1,0:T(1,128)S(1)}, f32[1,2048]{1,0:T(1,128)S(1)}, u32[]{:S(2)}, u32[]{:S(2)}) collective-permute-start(f32[1,2048]{1,0:T(1,128)S(1)} %get-tuple-element.153), channel_id=1, source_target_pairs={{0,9},{1,8},{4,13},{5,12},{8,1},{9,0},{12,5},{13,4},{2,11},{3,10},... | collective-permute-start | bytes 24584 | tf_op jit(solution)/shard_map/ppermute | solution.py:340
  50.5 3.7 %collective-permute-start.19 = (f32[8,128]{1,0:T(8,128)S(1)}, f32[8,128]{1,0:T(8,128)S(1)}, u32[]{:S(2)}, u32[]{:S(2)}) collective-permute-start(f32[8,128]{1,0:T(8,128)S(1)} %get-tuple-element.156.own_ref), channel_id=1, source_target_pairs={{0,2},{2,0},{1,3},{3,1},{4,6},{6,4},{5,7},{7,5},{8,10},{10,8},{9,1... | collective-permute-start | bytes 12296 | tf_op jit(solution)/shard_map/ppermute | solution.py:352
  56.0 4.9 %collective-permute-start.21 = (f32[1,2048]{1,0:T(1,128)S(1)}, f32[1,2048]{1,0:T(1,128)S(1)}, u32[]{:S(2)}, u32[]{:S(2)}) collective-permute-start(f32[1,2048]{1,0:T(1,128)S(1)} %get-tuple-element.164), channel_id=1, source_target_pairs={{0,13},{1,12},{4,9},{5,8},{8,5},{9,4},{12,1},{13,0},{2,15},{3,14},... | collective-permute-start | bytes 24584 | tf_op jit(solution)/shard_map/ppermute | solution.py:340
  58.1 4.0 %collective-permute-start.22 = (f32[1,2048]{1,0:T(1,128)S(1)}, f32[1,2048]{1,0:T(1,128)S(1)}, u32[]{:S(2)}, u32[]{:S(2)}) collective-permute-start(f32[1,2048]{1,0:T(1,128)S(1)} %get-tuple-element.165), channel_id=1, source_target_pairs={{0,9},{1,8},{4,13},{5,12},{8,1},{9,0},{12,5},{13,4},{2,11},{3,10},... | collective-permute-start | bytes 24584 | tf_op jit(solution)/shard_map/ppermute | solution.py:340
  63.1 3.7 %collective-permute-start.24 = (f32[8,128]{1,0:T(8,128)S(1)}, f32[8,128]{1,0:T(8,128)S(1)}, u32[]{:S(2)}, u32[]{:S(2)}) collective-permute-start(f32[8,128]{1,0:T(8,128)S(1)} %get-tuple-element.168.own_ref), channel_id=1, source_target_pairs={{0,2},{2,0},{1,3},{3,1},{4,6},{6,4},{5,7},{7,5},{8,10},{10,8},{9,1... | collective-permute-start | bytes 12296 | tf_op jit(solution)/shard_map/ppermute | solution.py:352
  68.6 4.9 %collective-permute-start.26 = (f32[1,2048]{1,0:T(1,128)S(1)}, f32[1,2048]{1,0:T(1,128)S(1)}, u32[]{:S(2)}, u32[]{:S(2)}) collective-permute-start(f32[1,2048]{1,0:T(1,128)S(1)} %get-tuple-element.176), channel_id=1, source_target_pairs={{0,13},{1,12},{4,9},{5,8},{8,5},{9,4},{12,1},{13,0},{2,15},{3,14},... | collective-permute-start | bytes 24584 | tf_op jit(solution)/shard_map/ppermute | solution.py:340
  70.0 4.0 %collective-permute-start.27 = (f32[1,2048]{1,0:T(1,128)S(1)}, f32[1,2048]{1,0:T(1,128)S(1)}, u32[]{:S(2)}, u32[]{:S(2)}) collective-permute-start(f32[1,2048]{1,0:T(1,128)S(1)} %get-tuple-element.177), channel_id=1, source_target_pairs={{0,9},{1,8},{4,13},{5,12},{8,1},{9,0},{12,5},{13,4},{2,11},{3,10},... | collective-permute-start | bytes 24584 | tf_op jit(solution)/shard_map/ppermute | solution.py:340
  74.8 3.7 %collective-permute-start.29 = (f32[8,128]{1,0:T(8,128)S(1)}, f32[8,128]{1,0:T(8,128)S(1)}, u32[]{:S(2)}, u32[]{:S(2)}) collective-permute-start(f32[8,128]{1,0:T(8,128)S(1)} %get-tuple-element.180.own_ref), channel_id=1, source_target_pairs={{0,2},{2,0},{1,3},{3,1},{4,6},{6,4},{5,7},{7,5},{8,10},{10,8},{9,1... | collective-permute-start | bytes 12296 | tf_op jit(solution)/shard_map/ppermute | solution.py:352
  80.3 4.9 %collective-permute-start.31 = (f32[1,2048]{1,0:T(1,128)S(1)}, f32[1,2048]{1,0:T(1,128)S(1)}, u32[]{:S(2)}, u32[]{:S(2)}) collective-permute-start(f32[1,2048]{1,0:T(1,128)S(1)} %get-tuple-element.188), channel_id=1, source_target_pairs={{0,13},{1,12},{4,9},{5,8},{8,5},{9,4},{12,1},{13,0},{2,15},{3,14},... | collective-permute-start | bytes 24584 | tf_op jit(solution)/shard_map/ppermute | solution.py:340
  82.4 4.0 %collective-permute-start.32 = (f32[1,2048]{1,0:T(1,128)S(1)}, f32[1,2048]{1,0:T(1,128)S(1)}, u32[]{:S(2)}, u32[]{:S(2)}) collective-permute-start(f32[1,2048]{1,0:T(1,128)S(1)} %get-tuple-element.189), channel_id=1, source_target_pairs={{0,9},{1,8},{4,13},{5,12},{8,1},{9,0},{12,5},{13,4},{2,11},{3,10},... | collective-permute-start | bytes 24584 | tf_op jit(solution)/shard_map/ppermute | solution.py:340
  92.7 4.9 %collective-permute-start.36 = (f32[1,2048]{1,0:T(1,128)S(1)}, f32[1,2048]{1,0:T(1,128)S(1)}, u32[]{:S(2)}, u32[]{:S(2)}) collective-permute-start(f32[1,2048]{1,0:T(1,128)S(1)} %get-tuple-element.200), channel_id=1, source_target_pairs={{0,13},{1,12},{4,9},{5,8},{8,5},{9,4},{12,1},{13,0},{2,15},{3,14},... | collective-permute-start | bytes 24584 | tf_op jit(solution)/shard_map/ppermute | solution.py:340
  94.1 4.0 %collective-permute-start.37 = (f32[1,2048]{1,0:T(1,128)S(1)}, f32[1,2048]{1,0:T(1,128)S(1)}, u32[]{:S(2)}, u32[]{:S(2)}) collective-permute-start(f32[1,2048]{1,0:T(1,128)S(1)} %get-tuple-element.201), channel_id=1, source_target_pairs={{0,9},{1,8},{4,13},{5,12},{8,1},{9,0},{12,5},{13,4},{2,11},{3,10},... | collective-permute-start | bytes 24584 | tf_op jit(solution)/shard_map/ppermute | solution.py:340
  98.8 3.7 %collective-permute-start.39 = (f32[8,128]{1,0:T(8,128)S(1)}, f32[8,128]{1,0:T(8,128)S(1)}, u32[]{:S(2)}, u32[]{:S(2)}) collective-permute-start(f32[8,128]{1,0:T(8,128)S(1)} %get-tuple-element.203.own_ref), channel_id=1, source_target_pairs={{0,2},{2,0},{1,3},{3,1},{4,6},{6,4},{5,7},{7,5},{8,10},{10,8},{9,1... | collective-permute-start | bytes 12296 | tf_op jit(solution)/shard_map/ppermute | solution.py:352
  (16 other events, 36.1 us)
